TPU v7x, 128 devices: a whole 4x4x4 slice. The times are simulated.
128 devices in a mesh: graph: 32 (over z, y, core), feat: 4 (over x).
Axes of the slice: x: 4, y: 4, z: 4, core: 2. Of those that a mesh axis runs over, the one named last changes fastest.
Arguments:
- grid_feat: bfloat16 [131072, 512], P('graph'), may hold values from -6 to 6
- mesh_feat: bfloat16 [65536, 512], P('graph'), may hold values from -6 to 6
- send_rows: int32 [32, 32, 256], P('graph'), may hold values from 0 to 4095
- tile_src: int32 [128, 8], P('graph'), may hold values from 0 to 95
- edge_mask: int32 [65536, 1024], P('graph'), may hold values from 0 to 1, as said below
- gain_src: float32 [512], replicated, may hold values from 0.1 to 1.9
- gain_dst: float32 [512], replicated, may hold values from 0.1 to 1.9
- w_query: bfloat16 [512, 512], P(None, 'feat')
- w_key: bfloat16 [512, 512], P(None, 'feat'), may hold values from -0.25 to 0.25
- w_value: bfloat16 [512, 512], P(None, 'feat'), may hold values from -0.25 to 0.25
- w_out: bfloat16 [512, 512], P('feat'), may hold values from -0.25 to 0.25
- d_out: bfloat16 [65536, 512], P('graph', 'feat'), may hold values from -6 to 6
Outputs:
- mesh_out: bfloat16 [65536, 512], P('graph', 'feat')
- grad_grid: bfloat16 [131072, 512], P('graph', 'feat')
- grad_mesh: bfloat16 [65536, 512], P('graph', 'feat')
- grad_wq: float32 [512, 512], P(None, 'feat')
- grad_wk: float32 [512, 512], P(None, 'feat')
- grad_wv: float32 [512, 512], P(None, 'feat')
- grad_wo: float32 [512, 512], P('feat')
Inputs may be any that keep to these rules, and one draw needn't show every extreme that they name: `edge_mask`: slot 0 of every mesh row is valid.
All inputs are finite; a program needn't handle non-finite values.
Results may differ from a plain program's by a relative error of at most 0.03.
The roundings to bfloat16 on the way count: a program that leaves them out, or rounds other values in their place, can miss the bound.
Values may be sent and summed in bfloat16 or wider, within the bound.
No kernel may reach another device: no remote copies, remote signals or barrier semaphores. Data moves between devices by JAX's collectives and lax.ppermute only.
A program may use at most 192 MiB of HBM per device.

v0:
```python
import jax
import jax.numpy as jnp
from jax import lax
from jax.sharding import PartitionSpec as P

D = 512
HEADS = 8
TS = 128
TM = 512


def normalize(values_in):
    centre = values_in - jnp.mean(values_in, axis=-1, keepdims=True)
    variance = jnp.mean(centre * centre, axis=-1, keepdims=True)
    inverse = lax.rsqrt(variance + 1e-05)
    return (centre * inverse, inverse)


def block_terms(queries, key_block, value_block, validity, grad_block, head_size):
    row_count = queries.shape[0]
    slot_count = key_block.shape[0]
    head_count = queries.shape[1] // head_size
    q_heads = queries.reshape(row_count, head_count, head_size)
    k_heads = key_block.reshape(slot_count, head_count, head_size)
    v_heads = value_block.reshape(slot_count, head_count, head_size)
    g_heads = grad_block.reshape(row_count, head_count, head_size)
    scores = jnp.einsum("thd,ehd->hte", q_heads, k_heads, preferred_element_type=jnp.float32)
    allowed = (validity > 0)[None, :, :]
    scores = jnp.where(allowed, scores, -1e30)
    highest = jnp.max(scores, axis=-1, keepdims=True)
    raised = jnp.where(allowed, jnp.exp(scores - highest), 0.0)
    attention = raised / jnp.sum(raised, axis=-1, keepdims=True)
    weights = attention.astype(jnp.bfloat16)
    attended = (
        jnp.einsum("hte,ehd->thd", weights, v_heads, preferred_element_type=jnp.float32)
        .reshape(row_count, -1)
        .astype(jnp.bfloat16)
    )
    d_weights = jnp.einsum("thd,ehd->hte", g_heads, v_heads, preferred_element_type=jnp.float32)
    d_values = jnp.einsum(
        "hte,thd->ehd", weights, g_heads, preferred_element_type=jnp.float32
    ).reshape(slot_count, -1)
    d_scores = attention * (d_weights - jnp.sum(attention * d_weights, axis=-1, keepdims=True))
    scores_b = d_scores.astype(jnp.bfloat16)
    d_query = jnp.einsum(
        "hte,ehd->thd", scores_b, k_heads, preferred_element_type=jnp.float32
    ).reshape(row_count, -1)
    d_keys = jnp.einsum(
        "hte,thd->ehd", scores_b, q_heads, preferred_element_type=jnp.float32
    ).reshape(slot_count, -1)
    return (attended, d_query, d_keys, d_values)


def body(
    grid_feat,
    mesh_feat,
    send_rows,
    tile_src,
    edge_mask,
    gain_src,
    gain_dst,
    w_query,
    w_key,
    w_value,
    w_out,
    d_out,
):
    full_width = grid_feat.shape[1]
    columns = w_query.shape[1]
    head_size = D // HEADS
    offset = lax.axis_index("feat") * columns
    grid_rows = grid_feat.shape[0]
    mesh_rows = mesh_feat.shape[0]
    src_hat, src_inverse = normalize(grid_feat.astype(jnp.float32))
    src_normed = (src_hat * gain_src).astype(jnp.bfloat16)
    dst_hat, dst_inverse = normalize(mesh_feat.astype(jnp.float32))
    dst_normed = (dst_hat * gain_dst).astype(jnp.bfloat16)
    queries = (jnp.dot(dst_normed, w_query, preferred_element_type=jnp.float32) * 0.125).astype(
        jnp.bfloat16
    )
    own_keys = jnp.dot(src_normed, w_key, preferred_element_type=jnp.float32).astype(jnp.bfloat16)
    own_values = jnp.dot(src_normed, w_value, preferred_element_type=jnp.float32).astype(
        jnp.bfloat16
    )
    outgoing = send_rows[0]
    peer_count = outgoing.shape[0]
    boundary = outgoing.shape[1]
    flat_rows = outgoing.reshape(-1)
    received = lax.all_to_all(
        src_normed[flat_rows].reshape(peer_count, boundary, full_width),
        "graph",
        split_axis=0,
        concat_axis=0,
        tiled=True,
    )
    halo_normed = received.reshape(-1, full_width)
    halo_keys = jnp.dot(halo_normed, w_key, preferred_element_type=jnp.float32).astype(jnp.bfloat16)
    halo_values = jnp.dot(halo_normed, w_value, preferred_element_type=jnp.float32).astype(
        jnp.bfloat16
    )
    key_table = jnp.concatenate([own_keys, halo_keys], axis=0).reshape(-1, TS, columns)
    value_table = jnp.concatenate([own_values, halo_values], axis=0).reshape(-1, TS, columns)
    full_grad = lax.all_gather(d_out, "feat", axis=1, tiled=True)
    d_attn = jnp.dot(full_grad, w_out.T, preferred_element_type=jnp.float32).astype(jnp.bfloat16)
    blocks = mesh_rows // TM

    def one_block(tables, inputs):
        key_grad, value_grad = tables
        query_block, grad_block, validity, tile_ids = inputs
        key_block = key_table[tile_ids].reshape(-1, columns)
        value_block = value_table[tile_ids].reshape(-1, columns)
        attended, d_query, d_keys, d_values = block_terms(
            query_block, key_block, value_block, validity, grad_block, head_size
        )
        key_grad = key_grad.at[tile_ids].add(d_keys.reshape(-1, TS, columns))
        value_grad = value_grad.at[tile_ids].add(d_values.reshape(-1, TS, columns))
        return ((key_grad, value_grad), (attended, d_query.astype(jnp.bfloat16)))

    zero_table = jnp.zeros(key_table.shape, jnp.float32)
    scan_inputs = (
        queries.reshape(blocks, TM, columns),
        d_attn.reshape(blocks, TM, columns),
        edge_mask.reshape(blocks, TM, -1),
        tile_src,
    )
    (key_grad, value_grad), (attended, d_query) = lax.scan(
        one_block, (zero_table, zero_table), scan_inputs
    )
    attended = attended.reshape(mesh_rows, columns)
    d_query = d_query.reshape(mesh_rows, columns)
    key_grad = key_grad.reshape(-1, columns).astype(jnp.bfloat16)
    value_grad = value_grad.reshape(-1, columns).astype(jnp.bfloat16)
    mixed_part = lax.psum_scatter(
        jnp.dot(attended, w_out, preferred_element_type=jnp.float32),
        "feat",
        scatter_dimension=1,
        tiled=True,
    )
    d_dst = 0.125 * jnp.dot(d_query, w_query.T, preferred_element_type=jnp.float32)
    dst_share = lax.psum_scatter(d_dst, "feat", scatter_dimension=1, tiled=True)
    mesh_out = (
        lax.dynamic_slice_in_dim(mesh_feat, offset, columns, 1).astype(jnp.float32) + mixed_part
    ).astype(jnp.bfloat16)
    halo_part = jnp.concatenate([key_grad[grid_rows:], value_grad[grid_rows:]], axis=1).reshape(
        peer_count, boundary, 2 * columns
    )
    returned = lax.all_to_all(halo_part, "graph", split_axis=0, concat_axis=0, tiled=True)
    own_part = jnp.concatenate([key_grad[:grid_rows], value_grad[:grid_rows]], axis=1).astype(
        jnp.float32
    )
    own_part = own_part.at[flat_rows].add(returned.reshape(-1, 2 * columns).astype(jnp.float32))
    own_part = own_part.astype(jnp.bfloat16)
    key_sum = own_part[:, :columns]
    value_sum = own_part[:, columns:]
    d_src = jnp.dot(key_sum, w_key.T, preferred_element_type=jnp.float32) + jnp.dot(
        value_sum, w_value.T, preferred_element_type=jnp.float32
    )
    grad_wk = jnp.dot(src_normed.T, key_sum, preferred_element_type=jnp.float32)
    grad_wv = jnp.dot(src_normed.T, value_sum, preferred_element_type=jnp.float32)
    grad_wo = jnp.dot(attended.T, full_grad, preferred_element_type=jnp.float32)
    grad_wq = 0.125 * jnp.dot(dst_normed.T, d_query, preferred_element_type=jnp.float32)
    src_share = lax.psum_scatter(d_src, "feat", scatter_dimension=1, tiled=True)
    src_piece = lax.dynamic_slice_in_dim(src_hat, offset, columns, 1)
    dst_piece = lax.dynamic_slice_in_dim(dst_hat, offset, columns, 1)
    src_scaled = src_share * lax.dynamic_slice_in_dim(gain_src, offset, columns, 0)
    dst_scaled = dst_share * lax.dynamic_slice_in_dim(gain_dst, offset, columns, 0)
    dst_stats = jnp.stack(
        [jnp.sum(dst_scaled, axis=1), jnp.sum(dst_scaled * dst_piece, axis=1)], axis=0
    )
    src_stats = jnp.stack(
        [jnp.sum(src_scaled, axis=1), jnp.sum(src_scaled * src_piece, axis=1)], axis=0
    )
    dst_sums, src_sums = lax.psum((dst_stats, src_stats), "feat")
    grid_part = (
        src_scaled
        - src_sums[0][:, None] / full_width
        - src_piece * (src_sums[1][:, None] / full_width)
    ) * src_inverse
    mesh_part = (
        dst_scaled
        - dst_sums[0][:, None] / full_width
        - dst_piece * (dst_sums[1][:, None] / full_width)
    ) * dst_inverse
    grad_grid = grid_part.astype(jnp.bfloat16)
    grad_mesh = (d_out.astype(jnp.float32) + mesh_part).astype(jnp.bfloat16)
    grad_wq, grad_wk, grad_wv, grad_wo = lax.psum((grad_wq, grad_wk, grad_wv, grad_wo), "graph")
    return (mesh_out, grad_grid, grad_mesh, grad_wq, grad_wk, grad_wv, grad_wo)


def solution(mesh):
    in_specs = (
        P("graph", None),
        P("graph", None),
        P("graph", None, None),
        P("graph", None),
        P("graph", None),
        P(),
        P(),
        P(None, "feat"),
        P(None, "feat"),
        P(None, "feat"),
        P("feat", None),
        P("graph", "feat"),
    )
    out_specs = (
        P("graph", "feat"),
        P("graph", "feat"),
        P("graph", "feat"),
        P(None, "feat"),
        P(None, "feat"),
        P(None, "feat"),
        P("feat", None),
    )
    return jax.shard_map(body, mesh=mesh, in_specs=in_specs, out_specs=out_specs, check_vma=False)
```

profile of v0, /device:TPU:1, one launch (start us, length us, event | category | flops | bytes accessed | tf_op | source)
XLA Modules:
  0.0 670.2 jit_solution(11028950628244160557)
XLA Ops:
  13.2 5.3 fusion.15
  18.5 36.5 %gather_fusion.2 = bf16[8192,512]{1,0:T(8,128)(2,1)} fusion(bf16[4096,512]{1,0:T(8,128)(2,1)} %get-tuple-element.132, s32[8192]{0:T(1024)S(1)} %broadcast_clamp_fusion), kind=kCustom, calls=%fused_computation.2 | custom fusion | bytes 16809984 | tf_op jit(solution)/shard_map/gather | solution.py:90
  55.0 9.8 %all-to-all-start = ((bf16[32,256,512]{2,1,0:T(8,128)(2,1)}), bf16[32,256,512]{2,1,0:T(8,128)(2,1)}, u32[]{:S(2)}, u32[]{:S(2)}) async-start(bf16[32,256,512]{2,1,0:T(8,128)(2,1)} %bitcast.143), calls=%async_computation | async-start | bytes 16777216 | tf_op jit(solution)/shard_map/all_to_all | solution.py:89
  71.9 30.0 %all-gather.2.cloned.1.call-done = bf16[2048,512]{1,0:T(8,128)(2,1)} async-done(((bf16[2048,128]{1,0:T(8,128)(2,1)}), bf16[2048,512]{1,0:T(8,128)(2,1)}) %all-gather.2.cloned.1.call-update) | async-done | bytes 2097168 | tf_op jit(solution)/shard_map/all_gather | solution.py:103
  105.0 59.5 %all-to-all-done = bf16[32,256,512]{2,1,0:T(8,128)(2,1)} async-done(((bf16[32,256,512]{2,1,0:T(8,128)(2,1)}), bf16[32,256,512]{2,1,0:T(8,128)(2,1)}, u32[]{:S(2)}, u32[]{:S(2)}) %all-to-all-start) | async-done | bytes 8388640 | tf_op jit(solution)/shard_map/all_to_all | solution.py:89
  164.5 5.7 convolution_convert_fusion.3
  170.3 5.7 convolution_convert_fusion.2
  176.0 8.5 %pad_maximum_fusion.1 = bf16[12288,128]{1,0:T(8,128)(2,1)} fusion(bf16[8192,128]{1,0:T(8,128)(2,1)S(1)} %convolution_convert_fusion.3, bf16[4096,128]{1,0:T(8,128)(2,1)S(1)} %convolution_convert_fusion.5), kind=kLoop, calls=%fused_computation.54 | loop fusion | flops 6291456 | bytes 6291456 | tf_op jit(solution)/shard_map/concatenate | solution.py:101
  184.5 8.7 %pad_maximum_fusion.2 = bf16[12288,128]{1,0:T(8,128)(2,1)} fusion(bf16[8192,128]{1,0:T(8,128)(2,1)S(1)} %convolution_convert_fusion.2, bf16[4096,128]{1,0:T(8,128)(2,1)S(1)} %convolution_convert_fusion.4), kind=kLoop, calls=%fused_computation.55 | loop fusion | flops 6291456 | bytes 6291456 | tf_op jit(solution)/shard_map/concatenate | solution.py:102
  193.1 3.5 broadcast_in_dim.24
  196.6 3.4 broadcast_in_dim.24.clone
  199.9 132.1 %while.16 = (s32[]{:T(128)}, f32[96,128,128]{2,1,0:T(8,128)}, f32[96,128,128]{2,1,0:T(8,128)}, bf16[4,512,128]{2,1,0:T(8,128)(2,1)}, bf16[4,512,128]{2,1,0:T(8,1...) while((s32[]{:T(128)}, f32[96,128,128]{2,1,0:T(8,128)}, ...), condition=%wide.region_10.11_spmd, body=%wide.region_4.10_spmd.sunk | while | flops 821953536 | bytes 71075192 | solution.py:126
  206.4 4.0 fusion.102
  223.8 3.2 multiply_reduce_fusion.6
  239.4 4.0 fusion.102
  256.8 3.2 multiply_reduce_fusion.6
  272.4 4.0 fusion.102
  289.8 3.2 multiply_reduce_fusion.6
  305.4 4.0 fusion.102
  322.8 3.2 multiply_reduce_fusion.6
  332.0 3.8 convolution_multiply_fusion
  335.9 3.7 fusion.35
  339.6 3.6 convert_element_type.115
  348.1 11.4 %all-to-all-start.1 = ((bf16[32,256,256]{2,1,0:T(8,128)(2,1)}), bf16[32,256,256]{2,1,0:T(8,128)(2,1)}, u32[]{:S(2)}, u32[]{:S(2)}) async-start(bf16[32,256,256]{2,1,0:T(8,128)(2,1)} %bitcast.144), calls=%async_computation.2 | async-start | bytes 8388608 | tf_op jit(solution)/shard_map/all_to_all | solution.py:147
  363.3 46.7 %all-to-all-done.1 = bf16[32,256,256]{2,1,0:T(8,128)(2,1)} async-done(((bf16[32,256,256]{2,1,0:T(8,128)(2,1)}), bf16[32,256,256]{2,1,0:T(8,128)(2,1)}, u32[]{:S(2)}, u32[]{:S(2)}) %all-to-all-start.1) | async-done | bytes 4194336 | tf_op jit(solution)/shard_map/all_to_all | solution.py:147
  409.9 49.1 %scatter_custom_fusion.2 = f32[4096,256]{1,0:T(8,128)} fusion(f32[4096,256]{1,0:T(8,128)} %maximum_convert_fusion, s32[8192]{0:T(1024)} %bitcast.162, bf16[8192,256]{1,0:T(8,128)(2,1)} %bitcast.37), kind=kCustom, calls=%fused_computation.40 | custom fusion | flops 4194304 | bytes 8388608 | tf_op jit(solution)/shard_map/scatter-add | solution.py:151
  462.8 4.5 convolution_add_fusion
  485.1 62.7 %reduce-scatter.6.cloned.1.call-done = f32[4096,128]{1,0:T(8,128)} async-done(((f32[4096,512]{1,0:T(8,128)}), f32[4096,128]{1,0:T(8,128)}) %reduce-scatter.6.cloned.1.call-update) | async-done | bytes 2097168 | tf_op jit(solution)/shard_map/reduce_scatter | solution.py:162
  547.8 3.5 multiply_reduce_fusion.2
  551.4 12.2 %all-reduce.1 = (f32[2,4096]{1,0:T(2,128)S(1)}, f32[2,2048]{1,0:T(2,128)S(1)}) all-reduce(f32[2,4096]{1,0:T(2,128)S(1)} %pad_maximum_fusion.3, f32[2,2048]{1,0:T(2,128)S(1)} %pad_maximum_fusion.4), channel_id=1, replica_groups=mesh['graph'=32,'feat'=4] {'feat'}, use_global_device_ids=true, to_apply=%region_16.17 | all-reduce | flops 12288 | bytes 98304 | tf_op jit(solution)/shard_map/psum | solution.py:173
  563.7 4.5 multiply_convert_fusion.3
  571.0 85.8 %all-reduce.4.cloned.1.call-done = (f32[512,128]{1,0:T(8,128)}, f32[512,128]{1,0:T(8,128)}, f32[512,128]{1,0:T(8,128)}, f32[128,512]{1,0:T(8,128)}) async-done(((f32[512,128]{1,0:T(8,128)}, f32[512,128]{1,0:T(8,128)}, f32[512,128]{1,0:T(8,128)}, f32[128,512]{1,0:T(8,128)}), (f32[512,128]{1,0:T(8,128)}, f32[512,128]{1,0:T(8,128)}, f32[512,128]{1,0:T(8,128)}, ...) | async-done | bytes 1048592 | tf_op jit(solution)/shard_map/psum | solution.py:186
  (238 shorter events, 158.4 us)
Async XLA Ops:
  7.2 62.2 %copy-start = (bf16[512,128]{1,0:T(8,128)(2,1)S(1)}, bf16[512,128]{1,0:T(8,128)(2,1)}, u32[]{:S(2)}) copy-start(bf16[512,128]{1,0:T(8,128)(2,1)} %param.22) | copy-start | bytes 393220
  7.2 3.5 copy-start.4
  7.2 5.3 copy-start.27
  7.2 6.0 copy-start.28
  12.5 6.0 copy-start.19
  55.0 10.6 %copy-start.5 = (bf16[2048,512]{1,0:T(8,128)(2,1)S(1)}, bf16[2048,512]{1,0:T(8,128)(2,1)}, u32[]{:S(2)}) copy-start(bf16[2048,512]{1,0:T(8,128)(2,1)} %param.15) | copy-start | bytes 6291460
  55.0 109.5 %all-to-all-start = ((bf16[32,256,512]{2,1,0:T(8,128)(2,1)}), bf16[32,256,512]{2,1,0:T(8,128)(2,1)}, u32[]{:S(2)}, u32[]{:S(2)}) async-start(bf16[32,256,512]{2,1,0:T(8,128)(2,1)} %bitcast.143), calls=%async_computation | async-start | bytes 16777216 | tf_op jit(solution)/shard_map/all_to_all | solution.py:89
  64.8 37.1 %all-gather.2.cloned.1.call-start = ((), (), s32[]{:S(2)}) async-start(), calls=%async_computation.5 | async-start | bytes 2621440 | tf_op jit(solution)/shard_map/all_gather | solution.py:103
  65.6 415.2 %reduce-scatter.8.cloned.1.call-start = ((), (), s32[]{:S(2)}) async-start(), calls=%async_computation.8 | async-start | bytes 5242880 | tf_op jit(solution)/shard_map/reduce_scatter | solution.py:140
  66.0 3.4 copy-start.1
  66.0 4.6 copy-start.25
  67.1 3.6 copy-start.23
  70.7 31.2 %copy-start.17 = (bf16[128,512]{1,0:T(8,128)(2,1)S(1)}, bf16[128,512]{1,0:T(8,128)(2,1)}, u32[]{:S(2)}) copy-start(bf16[128,512]{1,0:T(8,128)(2,1)} %param.24) | copy-start | bytes 393220
  223.8 3.4 copy-start.3
  256.8 3.4 copy-start.3
  289.8 3.4 copy-start.3
  322.8 3.4 copy-start.3
  332.0 3.8 copy-start.18
  335.8 147.1 %reduce-scatter.4.cloned.1.call-start = ((), (), s32[]{:S(2)}) async-start(), calls=%async_computation.6 | async-start | bytes 5242880 | tf_op jit(solution)/shard_map/reduce_scatter | solution.py:133
  339.5 4.0 slice-start
  339.6 4.7 slice-start.1
  344.9 3.2 copy-start.7
  348.1 61.8 %all-to-all-start.1 = ((bf16[32,256,256]{2,1,0:T(8,128)(2,1)}), bf16[32,256,256]{2,1,0:T(8,128)(2,1)}, u32[]{:S(2)}, u32[]{:S(2)}) async-start(bf16[32,256,256]{2,1,0:T(8,128)(2,1)} %bitcast.144), calls=%async_computation.2 | async-start | bytes 8388608 | tf_op jit(solution)/shard_map/all_to_all | solution.py:147
  359.6 188.2 %reduce-scatter.6.cloned.1.call-start = ((), (), s32[]{:S(2)}) async-start(), calls=%async_computation.7 | async-start | bytes 10485760 | tf_op jit(solution)/shard_map/reduce_scatter | solution.py:162
  467.3 189.5 %all-reduce.4.cloned.1.call-start = ((), (), s32[]{:S(2)}) async-start(), calls=%async_computation.9 | async-start | bytes 2097152 | tf_op jit(solution)/shard_map/psum | solution.py:186
  468.0 3.3 copy-start.11
  468.9 4.6 copy-start.16
  473.5 3.2 copy-start.9
  480.7 83.0 %copy-start.20 = (f32[4096]{0:T(1024)S(1)}, f32[4096]{0:T(1024)}, u32[]{:S(2)}) copy-start(f32[4096]{0:T(1024)} %copy-done.19) | copy-start | bytes 49156
  547.8 15.9 %copy-start.10 = (f32[4096,128]{1,0:T(8,128)S(1)}, f32[4096,128]{1,0:T(8,128)}, u32[]{:S(2)}) copy-start(f32[4096,128]{1,0:T(8,128)} %reduce-scatter.6.cloned.1.call-done) | copy-start | bytes 6291460
  547.8 20.4 %copy-start.12 = (f32[2048,128]{1,0:T(8,128)S(1)}, f32[2048,128]{1,0:T(8,128)}, u32[]{:S(2)}) copy-start(f32[2048,128]{1,0:T(8,128)} %reduce-scatter.8.cloned.1.call-done) | copy-start | bytes 3145732
  563.6 4.6 copy-start.13
  (12 other events, 18.1 us)
Sparse Core Ops, SparseCore 0:
  67.3 34.5 all-gather.1
  335.9 49.3 reduce-scatter.7
  387.9 46.5 reduce-scatter.3
  467.4 80.3 reduce-scatter.5
  551.8 105.0 all-reduce.3
where the time goes:
time: 677 us; the launch traced here: 670 us
  waiting for transfers between devices  285 us (42%)
  other arithmetic  141 us (21%)
  matrix products  97.5 us (14%)
  local copies, waits for them, and re-layouts  96.8 us (14%)
  starting transfers between devices  21.6 us (3%)
  between operations  14.5 us (2%)
  blocking collectives  12.2 us (2%)
    psum x1, waiting for transfers between devices, body(): lax.psum((grad_wq, grad_wk, grad_wv, grad_wo), 'graph')  85.8 us
    reduce_scatter x1, waiting for transfers between devices, body(): src_share = lax.psum_scatter(d_src, 'feat', scatter_dimension=1, tiled=True)  62.7 us
    all_to_all x1, waiting for transfers between devices, body(): lax.all_to_all(src_normed[flat_rows].reshape(peer_count, boundary, full_w...  59.5 us
    scatter-add x1, other arithmetic, body(): own_part.at[flat_rows]  49.1 us
    all_to_all x1, waiting for transfers between devices, body(): lax.all_to_all(halo_part, 'graph', split_axis=0, concat_axis=0, tiled=True)  46.7 us
    gather x1, local copies, waits for them, and re-layouts, body(): src_normed[flat_rows].reshape(peer_count, boundary, full_width)  36.5 us
    all_gather x1, waiting for transfers between devices, body(): full_grad = lax.all_gather(d_out, 'feat', axis=1, tiled=True)  30 us
    sub x4, matrix products, block_terms(): raised = jnp.where(allowed, jnp.exp(scores - highest), 0.0)  15.8 us
  transfers between devices with their start and end apart: 7, of which 5 were waited for; matrix products, arithmetic and copies ran while one was open for 16% of the time, Pallas kernels for 0%

commit v1 on v0

v1 whole, which is shorter than its diff:
```python
import jax
import jax.numpy as jnp
from jax import lax
from jax.experimental import pallas as pl
from jax.experimental.pallas import tpu as pltpu
from jax.sharding import PartitionSpec as P

HEAD = 64
PAIR = 2 * HEAD
TS = 128
TM = 512
QUAD = 4
BIG = 1e30

NT = (((1,), (1,)), ((), ()))
NN = (((1,), (0,)), ((), ()))
TN = (((0,), (0,)), ((), ()))


def mm(a, b, dims=NN):
    return lax.dot_general(a, b, dims, preferred_element_type=jnp.float32)


def params(mib, *semantics):
    return pltpu.CompilerParams(vmem_limit_bytes=mib * 2**20)


def vmem():
    return pl.BlockSpec(memory_space=pltpu.VMEM)


def smem():
    return pl.BlockSpec(memory_space=pltpu.SMEM)


def hat_of(values):
    centre = values - jnp.mean(values, axis=-1, keepdims=True)
    inverse = lax.rsqrt(jnp.mean(centre * centre, axis=-1, keepdims=True) + 1e-05)
    return centre * inverse, inverse


def norm_back(grad, hat, inverse):
    first = jnp.mean(grad, axis=-1, keepdims=True)
    second = jnp.mean(grad * hat, axis=-1, keepdims=True)
    return (grad - first - hat * second) * inverse


def source_kernel(feat_ref, gain_ref, weight_ref, normed_ref, pairs_ref):
    hat, _ = hat_of(feat_ref[...].astype(jnp.float32))
    normed = (hat * gain_ref[...]).astype(jnp.bfloat16)
    normed_ref[...] = normed
    pairs = mm(normed, weight_ref[...]).astype(jnp.bfloat16)
    for h in range(pairs_ref.shape[0]):
        pairs_ref[h] = pairs[:, h * PAIR : (h + 1) * PAIR]


def source_terms(feat, gain, weight):
    rows, width = feat.shape
    heads = weight.shape[1] // PAIR
    step = 512
    return pl.pallas_call(
        source_kernel,
        grid=(rows // step,),
        in_specs=[
            pl.BlockSpec((step, width), lambda i: (i, 0)),
            pl.BlockSpec((1, width), lambda i: (0, 0)),
            pl.BlockSpec(weight.shape, lambda i: (0, 0)),
        ],
        out_specs=[
            pl.BlockSpec((step, width), lambda i: (i, 0)),
            pl.BlockSpec((heads, step, PAIR), lambda i: (0, i, 0)),
        ],
        out_shape=[
            jax.ShapeDtypeStruct((rows, width), jnp.bfloat16),
            jax.ShapeDtypeStruct((heads, rows, PAIR), jnp.bfloat16),
        ],
        compiler_params=params(32),
        cost_estimate=pl.CostEstimate(
            flops=2 * rows * width * heads * PAIR, bytes_accessed=10 * 2**20, transcendentals=rows
        ),
        name="source_terms",
    )(feat, gain, weight)


def list_tiles(need_ref, list_ref):
    def add(t, count):
        used = need_ref[t] > 0

        @pl.when(used)
        def _():
            list_ref[count] = t

        return count + used.astype(jnp.int32)

    return lax.fori_loop(0, need_ref.shape[0], add, jnp.int32(0))


def gather_kernel(need_ref, pairs_ref, rows_ref, out_ref, table, list_ref):
    heads = pairs_ref.shape[0]
    table_rows = pairs_ref.shape[1]
    for h in range(heads):
        table[:, h * PAIR : (h + 1) * PAIR] = pairs_ref[h]
    count = list_tiles(need_ref, list_ref)
    depth = 256

    def quad(step, carry):
        tiles = [list_ref[jnp.minimum(step * QUAD + k, count - 1)] for k in range(QUAD)]
        wanted = jnp.concatenate(
            [jnp.transpose(jnp.broadcast_to(rows_ref[t], (TS, TS))) for t in tiles], axis=0
        )
        lane = lax.broadcasted_iota(jnp.int32, (QUAD * TS, TS), 1)
        away = wanted - lane
        total = jnp.zeros((QUAD * TS, heads * PAIR), jnp.float32)
        for c in range(table_rows // depth):
            hot = jnp.concatenate(
                [
                    jnp.where(away == c * depth + part * TS, 1.0, 0.0).astype(jnp.bfloat16)
                    for part in range(depth // TS)
                ],
                axis=1,
            )
            total = total + mm(hot, table[c * depth : (c + 1) * depth, :])
        total = total.astype(jnp.bfloat16)
        for k, t in enumerate(tiles):
            for h in range(heads):
                out_ref[t // 2, h, pl.ds((t % 2) * TS, TS), :] = total[
                    k * TS : (k + 1) * TS, h * PAIR : (h + 1) * PAIR
                ]
        return carry

    lax.fori_loop(0, (count + QUAD - 1) // QUAD, quad, 0)


def gather_rows(need, pairs, rows):
    heads, table_rows, _ = pairs.shape
    peers = need.shape[0] // 2
    return pl.pallas_call(
        gather_kernel,
        in_specs=[smem(), vmem(), vmem()],
        out_specs=vmem(),
        out_shape=jax.ShapeDtypeStruct((peers, heads, 2 * TS, PAIR), jnp.bfloat16),
        scratch_shapes=[
            pltpu.VMEM((table_rows, heads * PAIR), jnp.bfloat16),
            pltpu.SMEM((need.shape[0],), jnp.int32),
        ],
        compiler_params=params(40),
        cost_estimate=pl.CostEstimate(
            flops=6 * 10**9, bytes_accessed=6 * 2**20, transcendentals=0
        ),
        name="gather_rows",
    )(need, pairs, rows)


def target_kernel(feat_ref, gain_ref, wq_ref, wo_ref, cot_ref, normed_ref, pairs_ref):
    hat, _ = hat_of(feat_ref[...].astype(jnp.float32))
    normed = (hat * gain_ref[...]).astype(jnp.bfloat16)
    normed_ref[...] = normed
    cot = jnp.concatenate([cot_ref[f] for f in range(cot_ref.shape[0])], axis=1)
    pairs = mm(normed, wq_ref[...]) * 0.125 + mm(cot, wo_ref[...])
    pairs = pairs.astype(jnp.bfloat16)
    for h in range(pairs_ref.shape[0]):
        pairs_ref[h] = pairs[:, h * PAIR : (h + 1) * PAIR]


def target_terms(feat, gain, wq, wo, cot):
    rows, width = feat.shape
    heads = wq.shape[1] // PAIR
    groups, _, columns = cot.shape
    step = 512
    return pl.pallas_call(
        target_kernel,
        grid=(rows // step,),
        in_specs=[
            pl.BlockSpec((step, width), lambda i: (i, 0)),
            pl.BlockSpec((1, width), lambda i: (0, 0)),
            pl.BlockSpec(wq.shape, lambda i: (0, 0)),
            pl.BlockSpec(wo.shape, lambda i: (0, 0)),
            pl.BlockSpec((groups, step, columns), lambda i: (0, i, 0)),
        ],
        out_specs=[
            pl.BlockSpec((step, width), lambda i: (i, 0)),
            pl.BlockSpec((heads, step, PAIR), lambda i: (0, i, 0)),
        ],
        out_shape=[
            jax.ShapeDtypeStruct((rows, width), jnp.bfloat16),
            jax.ShapeDtypeStruct((heads, rows, PAIR), jnp.bfloat16),
        ],
        compiler_params=params(32),
        cost_estimate=pl.CostEstimate(
            flops=4 * rows * width * heads * PAIR, bytes_accessed=8 * 2**20, transcendentals=rows
        ),
        name="target_terms",
    )(feat, gain, wq, wo, cot)


def attention_kernel(
    tiles_ref,
    own_ref,
    halo_ref,
    pairs_ref,
    valid_ref,
    mixed_ref,
    own_grad_ref,
    halo_grad_ref,
    table,
    bias,
    scores,
    slopes,
    both,
    total,
    sems,
):
    j = pl.program_id(0)
    blocks, heads, tiles = table.shape[0], table.shape[1], table.shape[2]
    own_tiles = own_ref.shape[1] // TS

    def fetch(b, h, k, start):
        t = tiles_ref[b, k]
        if not start:
            pltpu.make_async_copy(
                own_ref.at[h, pl.ds(0, TS), :], table.at[b, h, k], sems.at[b, h, k]
            ).wait()
            return

        @pl.when(t < own_tiles)
        def _():
            pltpu.make_async_copy(
                own_ref.at[h, pl.ds(pl.multiple_of(t * TS, TS), TS), :],
                table.at[b, h, k],
                sems.at[b, h, k],
            ).start()

        @pl.when(t >= own_tiles)
        def _():
            o = t - own_tiles
            pltpu.make_async_copy(
                halo_ref.at[o // 2, h, pl.ds(pl.multiple_of((o % 2) * TS, TS), TS), :],
                table.at[b, h, k],
                sems.at[b, h, k],
            ).start()

    @pl.when(j == 0)
    def _():
        for b in range(blocks):
            for h in range(heads):
                for k in range(tiles):
                    fetch(b, h, k, True)

        def clear(t, carry):
            total[t] = jnp.zeros(total.shape[1:], jnp.float32)
            return carry

        lax.fori_loop(0, total.shape[0], clear, 0)

    for k in range(tiles):
        away = (valid_ref[:, k * TS : (k + 1) * TS] - 1).astype(jnp.float32) * BIG
        bias[k] = jnp.transpose(away)

    for h in range(heads):
        for k in range(tiles):
            fetch(j, h, k, False)

    first = lax.broadcasted_iota(jnp.int32, (1, PAIR), 1) < HEAD
    keep_first = jnp.where(first, 1.0, 0.0).astype(jnp.bfloat16)
    keep_second = jnp.where(first, 0.0, 1.0).astype(jnp.bfloat16)

    def fold(values, how):
        return how(values.reshape(TS // 8, 8, values.shape[-1]), axis=0)

    for h in range(heads):
        pairs = pairs_ref[h]
        queries = pairs * keep_first
        cots = pairs * keep_second
        highest = None
        for k in range(tiles):
            s = mm(table[j, h, k], queries, NT) + bias[k]
            scores[k] = s
            top = fold(s, jnp.max)
            highest = top if highest is None else jnp.maximum(highest, top)
        highest = jnp.max(highest, axis=0, keepdims=True)
        norm = None
        for k in range(tiles):
            e = jnp.exp(scores[k] - highest)
            scores[k] = e
            part = fold(e, jnp.sum)
            norm = part if norm is None else norm + part
        scale = 1.0 / jnp.sum(norm, axis=0, keepdims=True)
        delta = None
        for k in range(tiles):
            a = scores[k] * scale
            scores[k] = a
            both[k, :, TM:] = a.astype(jnp.bfloat16)
            d = mm(table[j, h, k], cots, NT)
            slopes[k] = d
            part = fold(a * d, jnp.sum)
            delta = part if delta is None else delta + part
        delta = jnp.sum(delta, axis=0, keepdims=True)
        for k in range(tiles):
            both[k, :, :TM] = (scores[k] * (slopes[k] - delta)).astype(jnp.bfloat16)
        stacked = jnp.concatenate([queries, cots], axis=0)
        for k in range(tiles):
            t = tiles_ref[j, k]
            total[t, h] = total[t, h] + mm(both[k], stacked)
        crossed = mm(
            table[j, h].reshape(tiles * TS, PAIR), both[...].reshape(tiles * TS, 2 * TM), TN
        )
        mixed = jnp.concatenate([crossed[:HEAD, :TM], crossed[HEAD:, TM:]], axis=0)
        mixed_ref[h] = jnp.transpose(mixed).astype(jnp.bfloat16)

    @pl.when(j == blocks - 1)
    def _():
        def own(t, carry):
            for h in range(heads):
                own_grad_ref[h, pl.ds(pl.multiple_of(t * TS, TS), TS), :] = total[t, h].astype(
                    jnp.bfloat16
                )
            return carry

        lax.fori_loop(0, own_tiles, own, 0)

        def halo(q, carry):
            for h in range(heads):
                for half in range(2):
                    halo_grad_ref[q, h, half * TS : (half + 1) * TS, :] = total[
                        own_tiles + 2 * q + half, h
                    ].astype(jnp.bfloat16)
            return carry

        lax.fori_loop(0, halo_grad_ref.shape[0], halo, 0)


def attention(tile_src, own, halo, pairs, valid):
    heads, rows, _ = pairs.shape
    blocks, tiles = tile_src.shape
    table_tiles = own.shape[1] // TS + 2 * halo.shape[0]
    slots = tiles * TS
    anywhere = pl.BlockSpec(memory_space=pl.ANY)
    return pl.pallas_call(
        attention_kernel,
        grid=(blocks,),
        in_specs=[
            smem(),
            anywhere,
            anywhere,
            pl.BlockSpec((heads, TM, PAIR), lambda j: (0, j, 0)),
            pl.BlockSpec((TM, slots), lambda j: (j, 0)),
        ],
        out_specs=[
            pl.BlockSpec((heads, TM, PAIR), lambda j: (0, j, 0)),
            pl.BlockSpec(own.shape, lambda j: (0, 0, 0)),
            pl.BlockSpec(halo.shape, lambda j: (0, 0, 0, 0)),
        ],
        out_shape=[
            jax.ShapeDtypeStruct((heads, rows, PAIR), jnp.bfloat16),
            jax.ShapeDtypeStruct(own.shape, jnp.bfloat16),
            jax.ShapeDtypeStruct(halo.shape, jnp.bfloat16),
        ],
        scratch_shapes=[
            pltpu.VMEM((blocks, heads, tiles, TS, PAIR), jnp.bfloat16),
            pltpu.VMEM((tiles, TS, TM), jnp.float32),
            pltpu.VMEM((tiles, TS, TM), jnp.float32),
            pltpu.VMEM((tiles, TS, TM), jnp.float32),
            pltpu.VMEM((tiles, TS, 2 * TM), jnp.bfloat16),
            pltpu.VMEM((table_tiles, heads, TS, PAIR), jnp.float32),
            pltpu.SemaphoreType.DMA((blocks, heads, tiles)),
        ],
        compiler_params=params(56),
        cost_estimate=pl.CostEstimate(
            flops=12 * heads * rows * slots * PAIR,
            bytes_accessed=24 * 2**20,
            transcendentals=heads * rows * slots,
        ),
        name="attention",
    )(tile_src, own, halo, pairs, valid)


def scatter_kernel(need_ref, own_ref, halo_ref, rows_ref, out_ref, total, list_ref):
    heads, table_rows, _ = own_ref.shape
    groups, _, group_rows, _ = out_ref.shape
    for h in range(heads):
        total[:, h * PAIR : (h + 1) * PAIR] = own_ref[h].astype(jnp.float32)
    count = list_tiles(need_ref, list_ref)

    def quad(step, carry):
        spots, parts = [], []
        for k in range(QUAD):
            place = step * QUAD + k
            t = list_ref[jnp.minimum(place, count - 1)]
            spots.append(jnp.where(place < count, rows_ref[t], -1))
            parts.append(
                jnp.concatenate(
                    [halo_ref[t // 2, h, pl.ds((t % 2) * TS, TS), :] for h in range(heads)], axis=1
                )
            )
        spots = jnp.concatenate(spots, axis=1)
        parts = jnp.concatenate(parts, axis=0)
        away = spots - lax.broadcasted_iota(jnp.int32, (512, QUAD * TS), 0)
        for c in range(table_rows // 512):
            hot = jnp.where(away == c * 512, 1.0, 0.0).astype(jnp.bfloat16)
            here = slice(c * 512, (c + 1) * 512)
            total[here, :] = total[here, :] + mm(hot, parts)
        return carry

    lax.fori_loop(0, (count + QUAD - 1) // QUAD, quad, 0)
    for f in range(groups):
        for h in range(heads):
            out_ref[f, h] = total[
                f * group_rows : (f + 1) * group_rows, h * PAIR : (h + 1) * PAIR
            ].astype(jnp.bfloat16)


def scatter_rows(need, own, halo, rows, groups):
    heads, table_rows, _ = own.shape
    return pl.pallas_call(
        scatter_kernel,
        in_specs=[smem(), vmem(), vmem(), vmem()],
        out_specs=vmem(),
        out_shape=jax.ShapeDtypeStruct(
            (groups, heads, table_rows // groups, PAIR), jnp.bfloat16
        ),
        scratch_shapes=[
            pltpu.VMEM((table_rows, heads * PAIR), jnp.float32),
            pltpu.SMEM((need.shape[0],), jnp.int32),
        ],
        compiler_params=params(40),
        cost_estimate=pl.CostEstimate(
            flops=6 * 10**9, bytes_accessed=8 * 2**20, transcendentals=0
        ),
        name="scatter_rows",
    )(need, own, halo, rows)


def wide_of(ref, keep=None):
    parts = []
    for f in range(ref.shape[0]):
        for h in range(ref.shape[1]):
            part = ref[f, h]
            parts.append(part if keep is None else part * keep)
    return jnp.concatenate(parts, axis=1)


def grid_kernel(where_ref, sums_ref, weight_ref, feat_ref, gain_ref, out_ref):
    groups, heads = sums_ref.shape[0], sums_ref.shape[1]
    weight = weight_ref[...].reshape(groups * heads * PAIR, -1)
    d_src = mm(wide_of(sums_ref), weight)
    hat, inverse = hat_of(feat_ref[...].astype(jnp.float32))
    result = norm_back(d_src * gain_ref[...], hat, inverse).astype(jnp.bfloat16)
    columns = out_ref.shape[2]
    for f in range(groups):
        out_ref[f] = result[:, f * columns : (f + 1) * columns]


def grid_rows(where, sums, weight, feat, gain):
    groups, heads, rows, _ = sums.shape
    width = feat.shape[1]
    step = 512
    steps = rows // step
    return pl.pallas_call(
        grid_kernel,
        grid_spec=pltpu.PrefetchScalarGridSpec(
            num_scalar_prefetch=1,
            grid=(steps,),
            in_specs=[
                pl.BlockSpec((groups, heads, step, PAIR), lambda i, w: (0, 0, i, 0)),
                pl.BlockSpec(weight.shape, lambda i, w: (0, 0, 0, 0)),
                pl.BlockSpec((step, width), lambda i, w: (w[0] * steps + i, 0)),
                pl.BlockSpec((1, width), lambda i, w: (0, 0)),
            ],
            out_specs=pl.BlockSpec((groups, step, width // groups), lambda i, w: (0, i, 0)),
        ),
        out_shape=jax.ShapeDtypeStruct((groups, rows, width // groups), jnp.bfloat16),
        compiler_params=params(32),
        cost_estimate=pl.CostEstimate(
            flops=2 * rows * width * groups * heads * PAIR,
            bytes_accessed=6 * 2**20,
            transcendentals=rows,
        ),
        name="grid_rows",
    )(where, sums, weight, feat, gain)


def mesh_kernel(where_ref, mixed_ref, weight_ref, feat_ref, cot_ref, gain_ref, out_ref):
    groups, heads = mixed_ref.shape[0], mixed_ref.shape[1]
    first = lax.broadcasted_iota(jnp.int32, (1, PAIR), 1) < HEAD
    keep_first = jnp.where(first, 1.0, 0.0).astype(jnp.bfloat16)
    keep_second = jnp.where(first, 0.0, 1.0).astype(jnp.bfloat16)
    weight = weight_ref[...].reshape(groups * heads * PAIR, -1)
    d_dst = mm(wide_of(mixed_ref, keep_first), weight) * 0.125
    added = mm(wide_of(mixed_ref, keep_second), weight)
    feat = feat_ref[...].astype(jnp.float32)
    hat, inverse = hat_of(feat)
    back = norm_back(d_dst * gain_ref[...], hat, inverse)
    cot = jnp.concatenate([cot_ref[f] for f in range(groups)], axis=1).astype(jnp.float32)
    mesh_out = (feat + added).astype(jnp.bfloat16)
    grad_mesh = (cot + back).astype(jnp.bfloat16)
    columns = out_ref.shape[3]
    for f in range(groups):
        out_ref[f, 0] = mesh_out[:, f * columns : (f + 1) * columns]
        out_ref[f, 1] = grad_mesh[:, f * columns : (f + 1) * columns]


def mesh_rows(where, mixed, weight, feat, cot, gain):
    groups, heads, rows, _ = mixed.shape
    width = feat.shape[1]
    columns = width // groups
    return pl.pallas_call(
        mesh_kernel,
        grid_spec=pltpu.PrefetchScalarGridSpec(
            num_scalar_prefetch=1,
            grid=(1,),
            in_specs=[
                pl.BlockSpec(mixed.shape, lambda i, w: (0, 0, 0, 0)),
                pl.BlockSpec(weight.shape, lambda i, w: (0, 0, 0, 0)),
                pl.BlockSpec((rows, width), lambda i, w: (w[0], 0)),
                pl.BlockSpec((groups, rows, columns), lambda i, w: (0, w[0], 0)),
                pl.BlockSpec((1, width), lambda i, w: (0, 0)),
            ],
            out_specs=pl.BlockSpec((groups, 2, rows, columns), lambda i, w: (0, 0, 0, 0)),
        ),
        out_shape=jax.ShapeDtypeStruct((groups, 2, rows, columns), jnp.bfloat16),
        compiler_params=params(32),
        cost_estimate=pl.CostEstimate(
            flops=4 * rows * width * groups * heads * PAIR,
            bytes_accessed=6 * 2**20,
            transcendentals=rows,
        ),
        name="mesh_rows",
    )(where, mixed, weight, feat, cot, gain)


def exchange(values, axis):
    return lax.all_to_all(values, axis, split_axis=0, concat_axis=0, tiled=True)


def sum_over_graph(values, peers):
    rows, columns = values.shape
    shares = exchange(values.reshape(peers, rows // peers, columns), "graph")
    share = jnp.sum(shares, axis=0)
    return exchange(jnp.broadcast_to(share[None], shares.shape), "graph").reshape(rows, columns)


def by_head(first, second, axis):
    parts = []
    for h in range(first.shape[axis] // HEAD):
        parts.append(lax.slice_in_dim(first, h * HEAD, (h + 1) * HEAD, axis=axis))
        parts.append(lax.slice_in_dim(second, h * HEAD, (h + 1) * HEAD, axis=axis))
    return jnp.concatenate(parts, axis=axis)


def body(
    grid_feat,
    mesh_feat,
    send_rows,
    tile_src,
    edge_mask,
    gain_src,
    gain_dst,
    w_query,
    w_key,
    w_value,
    w_out,
    d_out,
):
    grid_count, width = grid_feat.shape
    mesh_count = mesh_feat.shape[0]
    columns = w_query.shape[1]
    heads = columns // HEAD
    groups = width // columns
    peers = send_rows.shape[1]
    own_tiles = grid_count // TS
    where = lax.axis_index("feat").astype(jnp.int32).reshape(1)
    gain_src = gain_src.reshape(1, width)
    gain_dst = gain_dst.reshape(1, width)
    rows = send_rows.reshape(2 * peers, 1, TS)

    wanted = own_tiles + jnp.arange(2 * peers, dtype=jnp.int32)
    need = jnp.any(tile_src.reshape(-1, 1) == wanted[None, :], axis=0).astype(jnp.int32)
    need = exchange(
        jnp.broadcast_to(need.reshape(peers, 2, 1), (peers, 2, TS)), "graph"
    )[:, :, 0].reshape(-1)

    normed_src, pairs = source_terms(grid_feat, gain_src, by_head(w_key, w_value, 1))
    halo = exchange(gather_rows(need, pairs, rows), "graph")

    cot = lax.all_gather(d_out, "feat", axis=0)
    back_weights = jnp.stack(
        [
            by_head(w_key.T, w_value.T, 0).reshape(heads, PAIR, width),
            by_head(w_query.T, w_out, 0).reshape(heads, PAIR, width),
        ]
    )
    back_weights = lax.all_gather(back_weights, "feat", axis=0)

    zeros = jnp.zeros_like(w_query)
    normed_dst, targets = target_terms(
        mesh_feat, gain_dst, by_head(w_query, zeros, 1), by_head(zeros, w_out.T, 1), cot
    )
    mixed, own_grad, halo_grad = attention(tile_src, pairs, halo, targets, edge_mask)

    returned = exchange(halo_grad, "graph")

    mixed_rows = exchange(
        jnp.swapaxes(mixed.reshape(heads, groups, mesh_count // groups, PAIR), 0, 1), "feat"
    )
    mesh_result = exchange(
        mesh_rows(where, mixed_rows, back_weights[:, 1], mesh_feat, cot, gain_dst), "feat"
    )
    mesh_out = mesh_result[:, 0].reshape(mesh_count, columns)
    grad_mesh = mesh_result[:, 1].reshape(mesh_count, columns)
    d_query = jnp.concatenate([mixed[h, :, :HEAD] for h in range(heads)], axis=1)
    attended = jnp.concatenate([mixed[h, :, HEAD:] for h in range(heads)], axis=1)
    full_cot = jnp.swapaxes(cot, 0, 1).reshape(mesh_count, width)
    grad_wq = 0.125 * mm(normed_dst, d_query, TN)
    grad_wo = mm(attended, full_cot, TN)

    sums = scatter_rows(need, own_grad, returned, rows, groups)
    columns_of = jnp.swapaxes(sums, 0, 1).reshape(heads, grid_count, PAIR)
    grad_pairs = [mm(normed_src, columns_of[h], TN) for h in range(heads)]
    grad_wk = jnp.concatenate([g[:, :HEAD] for g in grad_pairs], axis=1)
    grad_wv = jnp.concatenate([g[:, HEAD:] for g in grad_pairs], axis=1)
    sum_rows = exchange(sums, "feat")
    grad_grid = exchange(
        grid_rows(where, sum_rows, back_weights[:, 0], grid_feat, gain_src), "feat"
    ).reshape(grid_count, columns)

    early = sum_over_graph(
        jnp.concatenate([grad_wq, grad_wo.reshape(width, columns)], axis=0), peers
    )
    late = sum_over_graph(jnp.concatenate([grad_wk, grad_wv], axis=0), peers)
    return (
        mesh_out,
        grad_grid,
        grad_mesh,
        early[:width],
        late[:width],
        late[width:],
        early[width:].reshape(columns, width),
    )


def solution(mesh):
    in_specs = (
        P("graph", None),
        P("graph", None),
        P("graph", None, None),
        P("graph", None),
        P("graph", None),
        P(),
        P(),
        P(None, "feat"),
        P(None, "feat"),
        P(None, "feat"),
        P("feat", None),
        P("graph", "feat"),
    )
    out_specs = (
        P("graph", "feat"),
        P("graph", "feat"),
        P("graph", "feat"),
        P(None, "feat"),
        P(None, "feat"),
        P(None, "feat"),
        P("feat", None),
    )
    return jax.shard_map(body, mesh=mesh, in_specs=in_specs, out_specs=out_specs, check_vma=False)
```

time: 677 us -> 368 us (0.54)
  other arithmetic: 141 us -> 5.83 us
  waiting for transfers between devices: 285 us -> 153 us
  matrix products: 97.5 us -> 7.83 us
  Pallas kernels: 0 us -> 59.5 us
  local copies, waits for them, and re-layouts: 96.8 us -> 46.5 us
  starting transfers between devices: 21.6 us -> 59.4 us
  blocking collectives: 12.2 us -> 19.9 us
    psum x1 -> x0, waiting for transfers between devices: 85.8 us -> none  [body(): lax.psum((grad_wq, grad_wk, grad_wv, grad_wo), 'graph')]
    dot_general x34 -> x4, matrix products: 81.7 us -> 7.83 us  [mm(): return lax.dot_general(a, b, dims, preferred_element_type=jnp.float32)]
    scatter-add x9 -> x0, other arithmetic: 70.7 us -> none  [the longest x1 49.1 us: body(): own_part.at[flat_rows]]
    reduce_scatter x3 -> x0, waiting for transfers between devices: 62.7 us -> none  [the longest x1 62.7 us: body(): src_share = lax.psum_scatter(d_src, 'feat', scatter_dimension=1, tiled=True)]
    pallas_call x0 -> x7, Pallas kernels: none -> 59.5 us  [the longest x1 28.4 us: attention(): pl.pallas_call(attention_kernel, grid=(blocks,), in_specs=[smem(), anywhe...]
    gather x17 -> x0, local copies, waits for them, and re-layouts: 57.9 us -> none  [the longest x1 36.5 us: body(): src_normed[flat_rows].reshape(peer_count, boundary, full_width)]
    all_to_all x2 -> x10, starting transfers between devices: 21.2 us -> 58.9 us  [exchange(): return lax.all_to_all(values, axis, split_axis=0, concat_axis=0, tiled=True)]
    all_gather x1 -> x2, waiting for transfers between devices: 30 us -> 63.3 us  [the longest x1 32.9 us: body(): cot = lax.all_gather(d_out, 'feat', axis=0)]
  transfers between devices with their start and end apart: 7 -> 12, of which waited for: 5 -> 10; matrix products, arithmetic and copies ran while one was open for 16% -> 7% of each run, Pallas kernels for 0% -> 6%
where the time goes in v1:
time: 368 us; the launch traced here: 366 us
  waiting for transfers between devices  153 us (42%)
  Pallas kernels  59.5 us (16%)
  starting transfers between devices  59.4 us (16%)
  local copies, waits for them, and re-layouts  46.5 us (13%)
  blocking collectives  19.9 us (5%)
  between operations  14.5 us (4%)
  matrix products  7.83 us (2%)
  other arithmetic  5.83 us (2%)
    all_to_all x10, waiting for transfers between devices, exchange(): return lax.all_to_all(values, axis, split_axis=0, concat_axis=0, tiled=True)  89 us
    all_to_all x10, starting transfers between devices, exchange(): return lax.all_to_all(values, axis, split_axis=0, concat_axis=0, tiled=True)  58.9 us
    all_gather x1, waiting for transfers between devices, body(): cot = lax.all_gather(d_out, 'feat', axis=0)  32.9 us
    all_gather x1, waiting for transfers between devices, body(): back_weights = lax.all_gather(back_weights, 'feat', axis=0)  30.4 us
    pallas_call x1, Pallas kernels, attention(): pl.pallas_call(attention_kernel, grid=(blocks,), in_specs=[smem(), anywhe...  28.4 us
    unnamed x67, local copies, waits for them, and re-layouts  24.4 us
    all_to_all x1, blocking collectives, exchange(): return lax.all_to_all(values, axis, split_axis=0, concat_axis=0, tiled=True)  19.9 us
    pallas_call x1, Pallas kernels, scatter_rows(): pl.pallas_call(scatter_kernel, in_specs=[smem(), vmem(), vmem(), vmem()],...  9.78 us
  transfers between devices with their start and end apart: 12, of which 10 were waited for; matrix products, arithmetic and copies ran while one was open for 7% of the time, Pallas kernels for 6%

profile of v1, /device:TPU:1, one launch (start us, length us, event | category | flops | bytes accessed | tf_op | source)
XLA Modules:
  0.0 366.3 jit_solution(10643196420876110110)
XLA Ops:
  8.9 9.6 %all-to-all-start = ((s32[32,2,128]{2,1,0:T(2,128)}), s32[32,2,128]{2,1,0:T(2,128)S(1)}, u32[]{:S(2)}, u32[]{:S(2)}) async-start(s32[32,2,128]{2,1,0:T(2,128)} %broadcast_in_dim.6), calls=%async_computation | async-start | bytes 65536 | tf_op jit(solution)/shard_map/all_to_all | solution.py:532
  22.8 4.5 %source_terms.1 = (bf16[4096,512]{1,0:T(8,128)(2,1)S(1)}, bf16[2,4096,128]{2,1,0:T(8,128)(2,1)S(1)}) custom-call(bf16[4096,512]{1,0:T(8,128)(2,1)S(1)} %copy-done.1, f32[1,512]{1,0:T(1,128)S(1)} %bitcast.57, bf16[512,256]{1,0:T(8,128)(2,1)S(1)} %pad_maximum_fusion.2.weight_ref), custom_call_target="tpu_custom_call" | custom-call | flops 1073741824 | bytes 10485760 | tf_op jit(solution)/shard_map/source_terms/pallas_call | solution.py:61
  30.1 8.0 %gather_rows.1 = bf16[32,2,256,128]{3,2,1,0:T(8,128)(2,1)S(1)} custom-call(s32[64]{0:T(128)S(1)} %reshape_squeeze.9.need_ref, bf16[2,4096,128]{2,1,0:T(8,128)(2,1)S(1)} %get-tuple-element.14.pairs_ref.own_ref, s32[64,1,128]{2,1,0:T(1,128)S(1)} %reshape.77.rows_ref), custom_call_target="tpu_custom_call" | custom-call | flops 6000000000 | bytes 6291456 | tf_op jit(solution)/shard_map/gather_rows/pallas_call | solution.py:137
  40.2 8.3 %all-to-all-start.1 = ((bf16[32,2,256,128]{3,2,1,0:T(8,128)(2,1)}), bf16[32,2,256,128]{3,2,1,0:T(8,128)(2,1)}, u32[]{:S(2)}, u32[]{:S(2)}) async-start(bf16[32,2,256,128]{3,2,1,0:T(8,128)(2,1)} %copy-done.6), calls=%async_computation.1 | async-start | bytes 8388608 | tf_op jit(solution)/shard_map/all_to_all | solution.py:532
  50.0 32.9 %all-gather.5.cloned.1.call-done = bf16[8192,128]{1,0:T(8,128)(2,1)} async-done(((bf16[2048,128]{1,0:T(8,128)(2,1)}), bf16[8192,128]{1,0:T(8,128)(2,1)}) %all-gather.5.cloned.1.call-update) | async-done | bytes 2097168 | tf_op jit(solution)/shard_map/all_gather | solution.py:585
  82.9 4.1 %copy.44 = bf16[2048,4,128]{0,2,1:T(8,128)(2,1)} copy(bf16[2048,4,128]{2,0,1:T(8,128)(2,1)} %bitcast.51) | data formatting | bytes 4194304 | tf_op jit(solution)/shard_map/transpose | solution.py:612
  88.6 3.1 target_terms.1
  94.0 4.8 %all-to-all-done.1.halo_ref = bf16[32,2,256,128]{3,2,1,0:T(8,128)(2,1)} async-done(((bf16[32,2,256,128]{3,2,1,0:T(8,128)(2,1)}), bf16[32,2,256,128]{3,2,1,0:T(8,128)(2,1)}, u32[]{:S(2)}, u32[]{:S(2)}) %all-to-all-start.1) | async-done | bytes 4194336 | tf_op jit(solution)/shard_map/all_to_all | solution.py:532
  98.8 28.4 %attention.1 = (bf16[2,2048,128]{2,1,0:T(8,128)(2,1)}, bf16[2,4096,128]{2,1,0:T(8,128)(2,1)}, bf16[32,2,256,128]{3,2,1,0:T(8,128)(2,1)}) custom-call(s32[4,8]{1,0:T(4,128)} %tiles_ref.1, bf16[2,4096,128]{2,1,0:T(8,128)(2,1)} %copy-done.16, bf16[32,2,256,128]{3,2,1,0:T(8,128)(2,1)} %all-to-all-done.1.halo_ref, bf16[2,2048,128]{2,1,0:T(8,128)(2,1)} %copy-done.17, ...), custom_call_target="tpu_custom_call" | custom-call | flops 6442450944 | bytes 25165824 | tf_op jit(solution)/shard_map/attention/pallas_call | solution.py:338
  127.3 3.0 slice_bitcast_fusion.5
  131.5 2.9 convolution_multiply_fusion
  135.2 7.7 %all-to-all-start.7 = ((f32[32,32,128]{2,1,0:T(8,128)}), f32[32,32,128]{2,1,0:T(8,128)}, u32[]{:S(2)}, u32[]{:S(2)}) async-start(f32[32,32,128]{2,1,0:T(8,128)} %bitcast.64), calls=%async_computation.7 | async-start | bytes 1048576 | tf_op jit(solution)/shard_map/all_to_all | solution.py:532
  144.0 10.6 %all-to-all-done.7 = f32[32,32,128]{2,1,0:T(8,128)} async-done(((f32[32,32,128]{2,1,0:T(8,128)}), f32[32,32,128]{2,1,0:T(8,128)}, u32[]{:S(2)}, u32[]{:S(2)}) %all-to-all-start.7) | async-done | bytes 524320 | tf_op jit(solution)/shard_map/all_to_all | solution.py:532
  154.6 4.0 %all-to-all-start.2 = ((bf16[4,2,512,128]{3,2,1,0:T(8,128)(2,1)}), bf16[4,2,512,128]{3,2,1,0:T(8,128)(2,1)S(1)}, u32[]{:S(2)}, u32[]{:S(2)}) async-start(bf16[4,2,512,128]{3,2,1,0:T(8,128)(2,1)} %bitcast.62), calls=%async_computation.2 | async-start | bytes 2097152 | tf_op jit(solution)/shard_map/all_to_all | solution.py:532
  159.5 13.6 %all-to-all-done.2.mixed_ref = bf16[4,2,512,128]{3,2,1,0:T(8,128)(2,1)S(1)} async-done(((bf16[4,2,512,128]{3,2,1,0:T(8,128)(2,1)}), bf16[4,2,512,128]{3,2,1,0:T(8,128)(2,1)S(1)}, u32[]{:S(2)}, u32[]{:S(2)}) %all-to-all-start.2) | async-done | bytes 1048608 | tf_op jit(solution)/shard_map/all_to_all | solution.py:532
  174.0 6.1 %all-to-all-start.4 = ((bf16[32,2,256,128]{3,2,1,0:T(8,128)(2,1)}), bf16[32,2,256,128]{3,2,1,0:T(8,128)(2,1)}, u32[]{:S(2)}, u32[]{:S(2)}) async-start(bf16[32,2,256,128]{3,2,1,0:T(8,128)(2,1)} %get-tuple-element.18), calls=%async_computation.4 | async-start | bytes 8388608 | tf_op jit(solution)/shard_map/all_to_all | solution.py:532
  182.9 30.4 %all-gather.7.cloned.1.call-done = bf16[8,2,128,512]{3,2,1,0:T(8,128)(2,1)} async-done(((bf16[2,2,128,512]{3,2,1,0:T(8,128)(2,1)}), bf16[8,2,128,512]{3,2,1,0:T(8,128)(2,1)}) %all-gather.7.cloned.1.call-update) | async-done | bytes 2097168 | tf_op jit(solution)/shard_map/all_gather | solution.py:592
  213.3 2.7 slice_bitcast_fusion
  223.7 6.7 %all-to-all-done.4.halo_ref = bf16[32,2,256,128]{3,2,1,0:T(8,128)(2,1)} async-done(((bf16[32,2,256,128]{3,2,1,0:T(8,128)(2,1)}), bf16[32,2,256,128]{3,2,1,0:T(8,128)(2,1)}, u32[]{:S(2)}, u32[]{:S(2)}) %all-to-all-start.4) | async-done | bytes 4194336 | tf_op jit(solution)/shard_map/all_to_all | solution.py:532
  231.3 7.1 %all-to-all-start.8 = ((f32[32,32,128]{2,1,0:T(8,128)}), f32[32,32,128]{2,1,0:T(8,128)S(1)}, u32[]{:S(2)}, u32[]{:S(2)}) async-start(f32[32,32,128]{2,1,0:T(8,128)} %broadcast_in_dim.7), calls=%async_computation.8 | async-start | bytes 1048576 | tf_op jit(solution)/shard_map/all_to_all | solution.py:532
  240.0 9.8 %scatter_rows.1 = bf16[4,2,1024,128]{3,2,1,0:T(8,128)(2,1)S(1)} custom-call(s32[64]{0:T(128)S(1)} %reshape_squeeze.9.need_ref, bf16[2,4096,128]{2,1,0:T(8,128)(2,1)S(1)} %copy-done.18, bf16[32,2,256,128]{3,2,1,0:T(8,128)(2,1)} %all-to-all-done.4.halo_ref, s32[64,1,128]{2,1,0:T(1,128)S(1)} %reshape.77.rows_ref), custom_call_target="tpu_custom_call" | custom-call | flops 6000000000 | bytes 8388608 | tf_op jit(solution)/shard_map/scatter_rows/pallas_call | solution.py:414
  254.3 3.5 all-to-all-start.3
  257.9 3.0 fusion.24
  261.2 11.5 %all-to-all-done.3 = bf16[4,2,512,128]{3,2,1,0:T(8,128)(2,1)S(1)} async-done(((bf16[4,2,512,128]{3,2,1,0:T(8,128)(2,1)}), bf16[4,2,512,128]{3,2,1,0:T(8,128)(2,1)S(1)}, u32[]{:S(2)}, u32[]{:S(2)}) %all-to-all-start.3) | async-done | bytes 1048608 | tf_op jit(solution)/shard_map/all_to_all | solution.py:532
  272.7 19.9 %all_to_all.55 = f32[32,32,128]{2,1,0:T(8,128)} all-to-all(f32[32,32,128]{2,1,0:T(8,128)S(1)} %bitcast.65), channel_id=1, replica_groups=mesh['graph'=32,'feat'=4] {'graph'}, dimensions={0} | all-to-all | bytes 1048576 | tf_op jit(solution)/shard_map/all_to_all | solution.py:532
  292.6 3.6 all-to-all-start.5
  297.3 24.9 %all-to-all-done.5.sums_ref = bf16[4,2,1024,128]{3,2,1,0:T(8,128)(2,1)S(1)} async-done(((bf16[4,2,1024,128]{3,2,1,0:T(8,128)(2,1)}), bf16[4,2,1024,128]{3,2,1,0:T(8,128)(2,1)S(1)}, u32[]{:S(2)}, u32[]{:S(2)}) %all-to-all-start.5) | async-done | bytes 2097184 | tf_op jit(solution)/shard_map/all_to_all | solution.py:532
  323.1 5.5 %all-to-all-start.10 = ((f32[32,32,128]{2,1,0:T(8,128)}), f32[32,32,128]{2,1,0:T(8,128)}, u32[]{:S(2)}, u32[]{:S(2)}) async-start(f32[32,32,128]{2,1,0:T(8,128)} %broadcast_in_dim.8), calls=%async_computation.10 | async-start | bytes 1048576 | tf_op jit(solution)/shard_map/all_to_all | solution.py:532
  330.8 3.0 grid_rows.1
  333.7 6.5 %all-to-all-done.10 = f32[32,32,128]{2,1,0:T(8,128)} async-done(((f32[32,32,128]{2,1,0:T(8,128)}), f32[32,32,128]{2,1,0:T(8,128)}, u32[]{:S(2)}, u32[]{:S(2)}) %all-to-all-start.10) | async-done | bytes 524320 | tf_op jit(solution)/shard_map/all_to_all | solution.py:532
  340.3 3.5 all-to-all-start.6
  348.2 10.3 %all-to-all-done.6 = bf16[4,1024,128]{2,1,0:T(8,128)(2,1)S(1)} async-done(((bf16[4,1024,128]{2,1,0:T(8,128)(2,1)}), bf16[4,1024,128]{2,1,0:T(8,128)(2,1)S(1)}, u32[]{:S(2)}, u32[]{:S(2)}) %all-to-all-start.6) | async-done | bytes 1048608 | tf_op jit(solution)/shard_map/all_to_all | solution.py:532
  (112 shorter events, 48.1 us)
Async XLA Ops:
  8.9 20.5 %all-to-all-start = ((s32[32,2,128]{2,1,0:T(2,128)}), s32[32,2,128]{2,1,0:T(2,128)S(1)}, u32[]{:S(2)}, u32[]{:S(2)}) async-start(s32[32,2,128]{2,1,0:T(2,128)} %broadcast_in_dim.6), calls=%async_computation | async-start | bytes 65536 | tf_op jit(solution)/shard_map/all_to_all | solution.py:532
  19.9 2.2 copy-start.1
  22.8 6.6 %copy-start.31 = (s32[1,32,256]{2,1,0:T(8,128)S(1)}, s32[1,32,256]{2,1,0:T(8,128)}, u32[]{:S(2)}) copy-start(s32[1,32,256]{2,1,0:T(8,128)} %param.14) | copy-start | bytes 98308
  29.4 8.8 %copy-start.16 = (bf16[2,4096,128]{2,1,0:T(8,128)(2,1)}, bf16[2,4096,128]{2,1,0:T(8,128)(2,1)S(1)}, u32[]{:S(2)}) copy-start(bf16[2,4096,128]{2,1,0:T(8,128)(2,1)S(1)} %get-tuple-element.14.pairs_ref.own_ref) | copy-start | bytes 6291460
  38.2 2.0 copy-start.6
  40.2 9.1 %copy-start.29 = (bf16[128,512]{1,0:T(8,128)(2,1)S(1)}, bf16[128,512]{1,0:T(8,128)(2,1)}, u32[]{:S(2)}) copy-start(bf16[128,512]{1,0:T(8,128)(2,1)} %param.22) | copy-start | bytes 393220
  40.2 9.2 %copy-start.27 = (bf16[512,128]{1,0:T(8,128)(2,1)S(1)}, bf16[512,128]{1,0:T(8,128)(2,1)}, u32[]{:S(2)}) copy-start(bf16[512,128]{1,0:T(8,128)(2,1)} %param.19) | copy-start | bytes 393220
  40.2 58.6 %all-to-all-start.1 = ((bf16[32,2,256,128]{3,2,1,0:T(8,128)(2,1)}), bf16[32,2,256,128]{3,2,1,0:T(8,128)(2,1)}, u32[]{:S(2)}, u32[]{:S(2)}) async-start(bf16[32,2,256,128]{3,2,1,0:T(8,128)(2,1)} %copy-done.6), calls=%async_computation.1 | async-start | bytes 8388608 | tf_op jit(solution)/shard_map/all_to_all | solution.py:532
  48.6 34.3 %all-gather.5.cloned.1.call-start = ((), (), s32[]{:S(2)}) async-start(), calls=%async_computation.11 | async-start | bytes 2621440 | tf_op jit(solution)/shard_map/all_gather | solution.py:585
  82.9 4.1 %copy-start = (bf16[8192,128]{1,0:T(8,128)(2,1)S(1)}, bf16[8192,128]{1,0:T(8,128)(2,1)}, u32[]{:S(2)}) copy-start(bf16[8192,128]{1,0:T(8,128)(2,1)} %all-gather.5.cloned.1.call-done) | copy-start | bytes 6291460
  82.9 4.1 %copy-start.11 = (f32[512]{0:T(512)S(1)}, f32[512]{0:T(512)}, u32[]{:S(2)}) copy-start(f32[512]{0:T(512)} %param.18) | copy-start | bytes 6148
  127.3 3.0 copy-start.20
  131.5 11.4 %copy-start.19 = (bf16[2,2048,128]{2,1,0:T(8,128)(2,1)S(1)}, bf16[2,2048,128]{2,1,0:T(8,128)(2,1)}, u32[]{:S(2)}) copy-start(bf16[2,2048,128]{2,1,0:T(8,128)(2,1)} %get-tuple-element.16) | copy-start | bytes 3145732
  135.2 19.4 %all-to-all-start.7 = ((f32[32,32,128]{2,1,0:T(8,128)}), f32[32,32,128]{2,1,0:T(8,128)}, u32[]{:S(2)}, u32[]{:S(2)}) async-start(f32[32,32,128]{2,1,0:T(8,128)} %bitcast.64), calls=%async_computation.7 | async-start | bytes 1048576 | tf_op jit(solution)/shard_map/all_to_all | solution.py:532
  142.9 15.7 %copy-start.25 = (bf16[512,128]{1,0:T(8,128)(2,1)S(1)}, bf16[512,128]{1,0:T(8,128)(2,1)}, u32[]{:S(2)}) copy-start(bf16[512,128]{1,0:T(8,128)(2,1)} %param.20) | copy-start | bytes 393220
  142.9 15.7 %copy-start.26 = (bf16[512,128]{1,0:T(8,128)(2,1)S(1)}, bf16[512,128]{1,0:T(8,128)(2,1)}, u32[]{:S(2)}) copy-start(bf16[512,128]{1,0:T(8,128)(2,1)} %param.21) | copy-start | bytes 393220
  154.6 18.5 %all-to-all-start.2 = ((bf16[4,2,512,128]{3,2,1,0:T(8,128)(2,1)}), bf16[4,2,512,128]{3,2,1,0:T(8,128)(2,1)S(1)}, u32[]{:S(2)}, u32[]{:S(2)}) async-start(bf16[4,2,512,128]{3,2,1,0:T(8,128)(2,1)} %bitcast.62), calls=%async_computation.2 | async-start | bytes 2097152 | tf_op jit(solution)/shard_map/all_to_all | solution.py:532
  173.1 8.6 %copy-start.28 = (bf16[512,128]{1,0:T(8,128)(2,1)S(1)}, bf16[512,128]{1,0:T(8,128)(2,1)}, u32[]{:S(2)}) copy-start(bf16[512,128]{1,0:T(8,128)(2,1)} %param.19) | copy-start | bytes 393220
  173.1 8.9 %copy-start.30 = (bf16[128,512]{1,0:T(8,128)(2,1)S(1)}, bf16[128,512]{1,0:T(8,128)(2,1)}, u32[]{:S(2)}) copy-start(bf16[128,512]{1,0:T(8,128)(2,1)} %param.22) | copy-start | bytes 393220
  174.0 56.4 %all-to-all-start.4 = ((bf16[32,2,256,128]{3,2,1,0:T(8,128)(2,1)}), bf16[32,2,256,128]{3,2,1,0:T(8,128)(2,1)}, u32[]{:S(2)}, u32[]{:S(2)}) async-start(bf16[32,2,256,128]{3,2,1,0:T(8,128)(2,1)} %get-tuple-element.18), calls=%async_computation.4 | async-start | bytes 8388608 | tf_op jit(solution)/shard_map/all_to_all | solution.py:532
  180.1 33.2 %all-gather.7.cloned.1.call-start = ((), (), s32[]{:S(2)}) async-start(), calls=%async_computation.12 | async-start | bytes 2621440 | tf_op jit(solution)/shard_map/all_gather | solution.py:592
  231.3 22.2 %all-to-all-start.8 = ((f32[32,32,128]{2,1,0:T(8,128)}), f32[32,32,128]{2,1,0:T(8,128)S(1)}, u32[]{:S(2)}, u32[]{:S(2)}) async-start(f32[32,32,128]{2,1,0:T(8,128)} %broadcast_in_dim.7), calls=%async_computation.8 | async-start | bytes 1048576 | tf_op jit(solution)/shard_map/all_to_all | solution.py:532
  249.8 2.9 copy-start.15
  254.3 18.4 %all-to-all-start.3 = ((bf16[4,2,512,128]{3,2,1,0:T(8,128)(2,1)}), bf16[4,2,512,128]{3,2,1,0:T(8,128)(2,1)S(1)}, u32[]{:S(2)}, u32[]{:S(2)}) async-start(bf16[4,2,512,128]{3,2,1,0:T(8,128)(2,1)} %mesh_rows.1), calls=%async_computation.3 | async-start | bytes 2097152 | tf_op jit(solution)/shard_map/all_to_all | solution.py:532
  272.7 19.9 %copy-start.21 = (bf16[4,2,512,128]{3,2,1,0:T(8,128)(2,1)}, bf16[4,2,512,128]{3,2,1,0:T(8,128)(2,1)S(1)}, u32[]{:S(2)}) copy-start(bf16[4,2,512,128]{3,2,1,0:T(8,128)(2,1)S(1)} %all-to-all-done.3) | copy-start | bytes 3145732
  292.6 29.6 %all-to-all-start.5 = ((bf16[4,2,1024,128]{3,2,1,0:T(8,128)(2,1)}), bf16[4,2,1024,128]{3,2,1,0:T(8,128)(2,1)S(1)}, u32[]{:S(2)}, u32[]{:S(2)}) async-start(bf16[4,2,1024,128]{3,2,1,0:T(8,128)(2,1)} %copy-done.3), calls=%async_computation.5 | async-start | bytes 4194304 | tf_op jit(solution)/shard_map/all_to_all | solution.py:532
  296.2 32.3 %copy-start.13 = (f32[512]{0:T(512)S(1)}, f32[512]{0:T(512)}, u32[]{:S(2)}) copy-start(f32[512]{0:T(512)} %param.17) | copy-start | bytes 6148
  323.1 17.2 %all-to-all-start.10 = ((f32[32,32,128]{2,1,0:T(8,128)}), f32[32,32,128]{2,1,0:T(8,128)}, u32[]{:S(2)}, u32[]{:S(2)}) async-start(f32[32,32,128]{2,1,0:T(8,128)} %broadcast_in_dim.8), calls=%async_computation.10 | async-start | bytes 1048576 | tf_op jit(solution)/shard_map/all_to_all | solution.py:532
  328.6 2.2 copy-start.2
  333.7 10.1 %copy-start.24 = (f32[32,32,128]{2,1,0:T(8,128)S(1)}, f32[32,32,128]{2,1,0:T(8,128)}, u32[]{:S(2)}) copy-start(f32[32,32,128]{2,1,0:T(8,128)} %copy-done.23) | copy-start | bytes 1572868
  333.7 11.6 %copy-start.22 = (bf16[4,2,512,128]{3,2,1,0:T(8,128)(2,1)S(1)}, bf16[4,2,512,128]{3,2,1,0:T(8,128)(2,1)}, u32[]{:S(2)}) copy-start(bf16[4,2,512,128]{3,2,1,0:T(8,128)(2,1)} %copy-done.21) | copy-start | bytes 3145732
  340.3 18.2 %all-to-all-start.6 = ((bf16[4,1024,128]{2,1,0:T(8,128)(2,1)}), bf16[4,1024,128]{2,1,0:T(8,128)(2,1)S(1)}, u32[]{:S(2)}, u32[]{:S(2)}) async-start(bf16[4,1024,128]{2,1,0:T(8,128)(2,1)} %grid_rows.1), calls=%async_computation.6 | async-start | bytes 2097152 | tf_op jit(solution)/shard_map/all_to_all | solution.py:532
  (12 other events, 15.4 us)
Sparse Core Ops, SparseCore 0:
  51.1 31.7 all-gather.4
  183.2 30.0 all-gather.6

commit v2 on v0

v2 whole, which is shorter than its diff:
```python
import jax
import jax.numpy as jnp
from jax import lax
from jax.experimental import pallas as pl
from jax.experimental.pallas import tpu as pltpu
from jax.sharding import PartitionSpec as P

HEAD = 64
PAIR = 2 * HEAD
TS = 128
TM = 512
QUAD = 4
BIG = 1e30

NT = (((1,), (1,)), ((), ()))
NN = (((1,), (0,)), ((), ()))
TN = (((0,), (0,)), ((), ()))


def mm(a, b, dims=NN):
    return lax.dot_general(a, b, dims, preferred_element_type=jnp.float32)


def room(mib):
    return pltpu.CompilerParams(vmem_limit_bytes=mib * 2**20)


VMEM = pl.BlockSpec(memory_space=pltpu.VMEM)
SMEM = pl.BlockSpec(memory_space=pltpu.SMEM)
ANY = pl.BlockSpec(memory_space=pl.ANY)


def cost(microseconds):
    return pl.CostEstimate(
        flops=int(microseconds * 1.15e9), bytes_accessed=2**20, transcendentals=0
    )


def hat_of(values):
    centre = values - jnp.mean(values, axis=-1, keepdims=True)
    inverse = lax.rsqrt(jnp.mean(centre * centre, axis=-1, keepdims=True) + 1e-05)
    return centre * inverse, inverse


def norm_back(grad, hat, inverse):
    first = jnp.mean(grad, axis=-1, keepdims=True)
    second = jnp.mean(grad * hat, axis=-1, keepdims=True)
    return (grad - first - hat * second) * inverse


def halves():
    first = lax.broadcasted_iota(jnp.int32, (1, PAIR), 1) < HEAD
    return (
        jnp.where(first, 1.0, 0.0).astype(jnp.bfloat16),
        jnp.where(first, 0.0, 1.0).astype(jnp.bfloat16),
    )


def source_kernel(feat_hbm, gain_ref, key_ref, value_ref, pairs_ref, weight, feat, sems):
    i = pl.program_id(0)
    ahead = 3

    def fetch(n):
        step = feat.shape[1]
        here = pl.ds(pl.multiple_of(n * step, step), step)
        return pltpu.make_async_copy(feat_hbm.at[here, :], feat.at[n], sems.at[n])

    @pl.when(i == 0)
    def _():
        for n in range(ahead):
            fetch(n).start()
        for h in range(key_ref.shape[1] // HEAD):
            here = slice(h * HEAD, (h + 1) * HEAD)
            weight[:, h * PAIR : (h + 1) * PAIR] = jnp.concatenate(
                [key_ref[:, here], value_ref[:, here]], axis=1
            )

    @pl.when(i + ahead < feat.shape[0])
    def _():
        fetch(i + ahead).start()

    fetch(i).wait()
    hat, _ = hat_of(feat[i].astype(jnp.float32))
    normed = (hat * gain_ref[...]).astype(jnp.bfloat16)
    pairs_ref[...] = mm(normed, weight[...]).astype(jnp.bfloat16)


def source_terms(feat, gain, w_key, w_value):
    rows, width = feat.shape
    wide = 2 * w_key.shape[1]
    step = 512
    steps = rows // step
    whole = pl.BlockSpec(w_key.shape, lambda i: (0, 0))
    return pl.pallas_call(
        source_kernel,
        grid=(steps,),
        in_specs=[ANY, pl.BlockSpec((1, width), lambda i: (0, 0)), whole, whole],
        out_specs=pl.BlockSpec((step, wide), lambda i: (i, 0)),
        out_shape=jax.ShapeDtypeStruct((rows, wide), jnp.bfloat16),
        scratch_shapes=[
            pltpu.VMEM((width, wide), jnp.bfloat16),
            pltpu.VMEM((steps, step, width), jnp.bfloat16),
            pltpu.SemaphoreType.DMA((steps,)),
        ],
        compiler_params=room(60),
        cost_estimate=cost(8),
        name="source_terms",
    )(feat, gain, w_key, w_value)


def list_tiles(need_ref, list_ref):
    def add(t, count):
        used = need_ref[t] > 0

        @pl.when(used)
        def _():
            list_ref[count] = t

        return count + used.astype(jnp.int32)

    return lax.fori_loop(0, need_ref.shape[0], add, jnp.int32(0))


def gather_kernel(need_ref, rows_ref, table_ref, *rest):
    out_refs = rest[:-4]
    hot, sent, list_ref, sems = rest[-4:]
    half = table_ref.shape[1]
    count = list_tiles(need_ref, list_ref)

    def copy(slot, k, h, t):
        return pltpu.make_async_copy(
            sent.at[slot, h, pl.ds(k * TS, TS), :],
            out_refs[h].at[t // 2, pl.ds(pl.multiple_of((t % 2) * TS, TS), TS), :],
            sems.at[slot, k, h],
        )

    def each(step, act):
        for k in range(QUAD):
            place = step * QUAD + k

            @pl.when(jnp.logical_and(place >= 0, place < count))
            def _():
                t = list_ref[jnp.maximum(place, 0)]
                for h in range(len(out_refs)):
                    act(copy(lax.rem(step + 2, 2), k, h, t))

    def quad(step, carry):
        tiles = [list_ref[jnp.minimum(step * QUAD + k, count - 1)] for k in range(QUAD)]
        wanted = jnp.concatenate(
            [jnp.transpose(jnp.broadcast_to(rows_ref[t], (TS, TS))) for t in tiles], axis=0
        )
        upper = wanted >= half
        away = jnp.where(upper, wanted - half, wanted)
        away = away - lax.broadcasted_iota(jnp.int32, (QUAD * TS, TS), 1)
        for c in range(half // TS):
            hot[:, c * TS : (c + 1) * TS] = jnp.where(away == c * TS, 1.0, 0.0).astype(
                jnp.bfloat16
            )
        low = mm(hot[...], table_ref[0])
        high = mm(hot[...], table_ref[1])
        each(step - 2, lambda c: c.wait())
        slot = lax.rem(step, 2)
        for h in range(len(out_refs)):
            here = slice(h * PAIR, (h + 1) * PAIR)
            sent[slot, h] = jnp.where(upper, high[:, here], low[:, here]).astype(jnp.bfloat16)
        each(step, lambda c: c.start())
        return carry

    steps = (count + QUAD - 1) // QUAD
    lax.fori_loop(0, steps, quad, 0)
    each(steps - 2, lambda c: c.wait())
    each(steps - 1, lambda c: c.wait())


def gather_rows(need, rows, pairs):
    count, wide = pairs.shape
    heads = wide // PAIR
    peers = need.shape[0] // 2
    return pl.pallas_call(
        gather_kernel,
        in_specs=[SMEM, VMEM, VMEM],
        out_specs=[ANY] * heads,
        out_shape=[jax.ShapeDtypeStruct((peers, 2 * TS, PAIR), jnp.bfloat16)] * heads,
        scratch_shapes=[
            pltpu.VMEM((QUAD * TS, count // 2), jnp.bfloat16),
            pltpu.VMEM((2, heads, QUAD * TS, PAIR), jnp.bfloat16),
            pltpu.SMEM((need.shape[0],), jnp.int32),
            pltpu.SemaphoreType.DMA((2, QUAD, heads)),
        ],
        compiler_params=room(60),
        cost_estimate=cost(10),
        name="gather_rows",
    )(need, rows, pairs.reshape(2, count // 2, wide))


def normed_kernel(feat_ref, gain_ref, normed_ref):
    hat, _ = hat_of(feat_ref[...].astype(jnp.float32))
    normed_ref[...] = (hat * gain_ref[...]).astype(jnp.bfloat16)


def normed_rows(feat, gain):
    rows, width = feat.shape
    step = 512
    return pl.pallas_call(
        normed_kernel,
        grid=(rows // step,),
        in_specs=[
            pl.BlockSpec((step, width), lambda i: (i, 0)),
            pl.BlockSpec((1, width), lambda i: (0, 0)),
        ],
        out_specs=pl.BlockSpec((step, width), lambda i: (i, 0)),
        out_shape=jax.ShapeDtypeStruct((rows, width), jnp.bfloat16),
        compiler_params=room(60),
        cost_estimate=cost(8),
        name="normed_rows",
    )(feat, gain)


def target_kernel(feat_ref, gain_ref, wq_ref, wo_ref, cot_ref, normed_ref, *pairs_refs):
    hat, _ = hat_of(feat_ref[...].astype(jnp.float32))
    normed = (hat * gain_ref[...]).astype(jnp.bfloat16)
    normed_ref[...] = normed
    cot = jnp.concatenate([cot_ref[f] for f in range(cot_ref.shape[0])], axis=1)
    queries = (mm(normed, wq_ref[...]) * 0.125).astype(jnp.bfloat16)
    cots = mm(cot, wo_ref[...], NT).astype(jnp.bfloat16)
    for h, ref in enumerate(pairs_refs):
        here = slice(h * HEAD, (h + 1) * HEAD)
        ref[...] = jnp.concatenate([queries[:, here], cots[:, here]], axis=1)


def target_terms(feat, gain, w_query, w_out, cot):
    rows, width = feat.shape
    groups, _, columns = cot.shape
    heads = columns // HEAD
    step = 512
    return pl.pallas_call(
        target_kernel,
        grid=(rows // step,),
        in_specs=[
            pl.BlockSpec((step, width), lambda i: (i, 0)),
            pl.BlockSpec((1, width), lambda i: (0, 0)),
            pl.BlockSpec(w_query.shape, lambda i: (0, 0)),
            pl.BlockSpec(w_out.shape, lambda i: (0, 0)),
            pl.BlockSpec((groups, step, columns), lambda i: (0, i, 0)),
        ],
        out_specs=[pl.BlockSpec((step, width), lambda i: (i, 0))]
        + [pl.BlockSpec((step, PAIR), lambda i: (i, 0))] * heads,
        out_shape=[jax.ShapeDtypeStruct((rows, width), jnp.bfloat16)]
        + [jax.ShapeDtypeStruct((rows, PAIR), jnp.bfloat16)] * heads,
        compiler_params=room(60),
        cost_estimate=cost(6),
        name="target_terms",
    )(feat, gain, w_query, w_out, cot)


def attention_kernel(
    head,
    tiles_ref,
    own_ref,
    halo_ref,
    pairs_ref,
    valid_ref,
    normed_ref,
    cot_ref,
    own_grad_ref,
    halo_grad_ref,
    weight_grad_ref,
    mixed_ref,
    table,
    bias,
    scores,
    slopes,
    both,
    total,
    sems,
):
    j = pl.program_id(0)
    blocks, tiles = table.shape[0], table.shape[1]
    own_tiles = own_ref.shape[0] // TS

    def fetch(b, k):
        t = tiles_ref[b, k]

        @pl.when(t < own_tiles)
        def _():
            here = pl.ds(pl.multiple_of(t * TS, TS), TS)
            pltpu.make_async_copy(
                own_ref.at[here, pl.ds(head * PAIR, PAIR)], table.at[b, k], sems.at[b, k]
            ).start()

        @pl.when(t >= own_tiles)
        def _():
            o = t - own_tiles
            here = pl.ds(pl.multiple_of((o % 2) * TS, TS), TS)
            pltpu.make_async_copy(
                halo_ref.at[o // 2, here, :], table.at[b, k], sems.at[b, k]
            ).start()

    @pl.when(j == 0)
    def _():
        for b in range(blocks):
            for k in range(tiles):
                fetch(b, k)

        def clear(t, carry):
            total[t] = jnp.zeros(total.shape[1:], jnp.float32)
            return carry

        lax.fori_loop(0, total.shape[0], clear, 0)
        weight_grad_ref[...] = jnp.zeros(weight_grad_ref.shape, jnp.float32)

    for k in range(tiles):
        away = (valid_ref[:, k * TS : (k + 1) * TS] - 1).astype(jnp.float32) * BIG
        bias[k] = jnp.transpose(away)

    for k in range(tiles):
        pltpu.make_async_copy(
            own_ref.at[pl.ds(0, TS), pl.ds(head * PAIR, PAIR)], table.at[j, k], sems.at[j, k]
        ).wait()

    def fold(values, how):
        return how(values.reshape(TS // 8, 8, values.shape[-1]), axis=0)

    keep_first, keep_second = halves()
    pairs = pairs_ref[...]
    queries = pairs * keep_first
    cots = pairs * keep_second
    highest = None
    for k in range(tiles):
        s = mm(table[j, k], queries, NT) + bias[k]
        scores[k] = s
        top = fold(s, jnp.max)
        highest = top if highest is None else jnp.maximum(highest, top)
    highest = jnp.max(highest, axis=0, keepdims=True)
    norm = None
    for k in range(tiles):
        e = jnp.exp(scores[k] - highest)
        scores[k] = e
        part = fold(e, jnp.sum)
        norm = part if norm is None else norm + part
    scale = 1.0 / jnp.sum(norm, axis=0, keepdims=True)
    delta = None
    for k in range(tiles):
        a = scores[k] * scale
        scores[k] = a
        both[k, :, TM:] = a.astype(jnp.bfloat16)
        d = mm(table[j, k], cots, NT)
        slopes[k] = d
        part = fold(a * d, jnp.sum)
        delta = part if delta is None else delta + part
    delta = jnp.sum(delta, axis=0, keepdims=True)
    for k in range(tiles):
        both[k, :, :TM] = (scores[k] * (slopes[k] - delta)).astype(jnp.bfloat16)
    stacked = jnp.concatenate([queries, cots], axis=0)
    for k in range(tiles):
        t = tiles_ref[j, k]
        total[t] = total[t] + mm(both[k], stacked)
    crossed = mm(table[j].reshape(tiles * TS, PAIR), both[...].reshape(tiles * TS, 2 * TM), TN)
    d_query = crossed[:HEAD, :TM]
    attended = crossed[HEAD:, TM:]
    mixed = jnp.concatenate([d_query, attended], axis=0)
    mixed_ref[...] = jnp.transpose(mixed).astype(jnp.bfloat16)
    cot = jnp.concatenate([cot_ref[f] for f in range(cot_ref.shape[0])], axis=1)
    wq_part = mm(d_query.astype(jnp.bfloat16), normed_ref[...])
    wo_part = mm(attended.astype(jnp.bfloat16), cot)
    columns = weight_grad_ref.shape[2]
    for f in range(weight_grad_ref.shape[0]):
        here = slice(f * columns, (f + 1) * columns)
        weight_grad_ref[f, :HEAD] += wq_part[:, here]
        weight_grad_ref[f, HEAD:] += wo_part[:, here]

    @pl.when(j == blocks - 1)
    def _():
        def own(t, carry):
            here = pl.ds(pl.multiple_of(t * TS, TS), TS)
            own_grad_ref[here, :] = total[t].astype(jnp.bfloat16)
            return carry

        lax.fori_loop(0, own_tiles, own, 0)

        def halo(q, carry):
            for half in range(2):
                halo_grad_ref[q, half * TS : (half + 1) * TS, :] = total[
                    own_tiles + 2 * q + half
                ].astype(jnp.bfloat16)
            return carry

        lax.fori_loop(0, halo_grad_ref.shape[0], halo, 0)


def attention(head, tile_src, own, halo, pairs, valid, normed, cot):
    rows, _ = pairs.shape
    blocks, tiles = tile_src.shape
    groups, _, columns = cot.shape
    width = normed.shape[1]
    own_grad = (own.shape[0], PAIR)
    table_tiles = own.shape[0] // TS + 2 * halo.shape[0]
    slots = tiles * TS
    return pl.pallas_call(
        lambda *refs: attention_kernel(head, *refs),
        grid=(blocks,),
        in_specs=[
            SMEM,
            ANY,
            ANY,
            pl.BlockSpec((TM, PAIR), lambda j: (j, 0)),
            pl.BlockSpec((TM, slots), lambda j: (j, 0)),
            pl.BlockSpec((TM, width), lambda j: (j, 0)),
            pl.BlockSpec((groups, TM, columns), lambda j: (0, j, 0)),
        ],
        out_specs=[
            pl.BlockSpec(own_grad, lambda j: (0, 0)),
            pl.BlockSpec(halo.shape, lambda j: (0, 0, 0)),
            pl.BlockSpec((groups, PAIR, columns), lambda j: (0, 0, 0)),
            pl.BlockSpec((TM, PAIR), lambda j: (j, 0)),
        ],
        out_shape=[
            jax.ShapeDtypeStruct(own_grad, jnp.bfloat16),
            jax.ShapeDtypeStruct(halo.shape, jnp.bfloat16),
            jax.ShapeDtypeStruct((groups, PAIR, columns), jnp.float32),
            jax.ShapeDtypeStruct((rows, PAIR), jnp.bfloat16),
        ],
        scratch_shapes=[
            pltpu.VMEM((blocks, tiles, TS, PAIR), jnp.bfloat16),
            pltpu.VMEM((tiles, TS, TM), jnp.float32),
            pltpu.VMEM((tiles, TS, TM), jnp.float32),
            pltpu.VMEM((tiles, TS, TM), jnp.float32),
            pltpu.VMEM((tiles, TS, 2 * TM), jnp.bfloat16),
            pltpu.VMEM((table_tiles, TS, PAIR), jnp.float32),
            pltpu.SemaphoreType.DMA((blocks, tiles)),
        ],
        compiler_params=room(60),
        cost_estimate=cost(18),
        name="attention",
    )(tile_src, own, halo, pairs, valid, normed, cot)


def scatter_kernel(earlier, where_ref, need_ref, own_ref, halo_ref, rows_ref, normed_hbm, *rest):
    *rest, total, normed, grad, list_ref, sem = rest
    done, grad_ref, out_refs = rest[:earlier], rest[earlier], rest[earlier + 1 :]
    table_rows = own_ref.shape[0]
    half = table_rows // 2
    groups = len(out_refs)
    group_rows = table_rows // groups
    chunk = 512
    fetch = pltpu.make_async_copy(normed_hbm, normed, sem)
    fetch.start()
    total[...] = own_ref[...].astype(jnp.float32)
    count = list_tiles(need_ref, list_ref)

    def quad(step, carry):
        spots, parts = [], []
        for k in range(QUAD):
            place = step * QUAD + k
            t = list_ref[jnp.minimum(place, count - 1)]
            spot = jnp.where(place < count, rows_ref[t], -1)
            upper = jnp.transpose(jnp.broadcast_to(spot, (TS, TS))) >= half
            part = halo_ref[t // 2, pl.ds((t % 2) * TS, TS), :]
            keep = jnp.where(upper, 1.0, 0.0).astype(jnp.bfloat16)
            drop = jnp.where(upper, 0.0, 1.0).astype(jnp.bfloat16)
            parts.append(jnp.concatenate([part * drop, part * keep], axis=1))
            spots.append(jnp.where(spot >= half, spot - half, spot))
        spots = jnp.concatenate(spots, axis=1)
        parts = jnp.concatenate(parts, axis=0)
        away = spots - lax.broadcasted_iota(jnp.int32, (chunk, QUAD * TS), 0)
        for c in range(half // chunk):
            hot = jnp.where(away == c * chunk, 1.0, 0.0).astype(jnp.bfloat16)
            added = mm(hot, parts)
            for n in range(2):
                here = slice(n * half + c * chunk, n * half + (c + 1) * chunk)
                total[here, :] = total[here, :] + added[:, n * PAIR : (n + 1) * PAIR]
        return carry

    lax.fori_loop(0, (count + QUAD - 1) // QUAD, quad, 0)
    for s, ref in enumerate(out_refs):
        f = lax.rem(where_ref[0] + s, groups)
        here = pl.ds(pl.multiple_of(f * group_rows, group_rows), group_rows)
        ref[...] = total[here, :].astype(jnp.bfloat16)
    fetch.wait()
    columns = grad.shape[2]
    for n in range(groups):
        here = slice(n * group_rows, (n + 1) * group_rows)
        added = mm(total[here, :].astype(jnp.bfloat16), normed[here, :], TN)
        for f in range(groups):
            part = added[:, f * columns : (f + 1) * columns]
            grad[f] = part if n == 0 else grad[f] + part
    if not earlier:
        grad_ref[...] = grad[...]
        return
    rows = grad_ref.shape[1] // (earlier + 1)
    per_block = grad.shape[1] // rows
    for p in range(grad_ref.shape[0]):
        here = slice(p % per_block * rows, (p % per_block + 1) * rows)
        for m, ref in enumerate(list(done) + [grad]):
            grad_ref[p, m * rows : (m + 1) * rows, :] = ref[p // per_block, here, :]


def scatter_rows(where, need, own, halo, rows, normed, groups, earlier=(), peers=None):
    table_rows = own.shape[0]
    columns = normed.shape[1] // groups
    grad = (groups, PAIR, columns)
    out = grad
    if earlier:
        out = (peers, groups * PAIR // peers * (len(earlier) + 1), columns)
    return pl.pallas_call(
        lambda *refs: scatter_kernel(len(earlier), *refs),
        in_specs=[SMEM, SMEM, VMEM, VMEM, VMEM, ANY] + [VMEM] * len(earlier),
        out_specs=[VMEM] * (1 + groups),
        out_shape=[jax.ShapeDtypeStruct(out, jnp.float32)]
        + [jax.ShapeDtypeStruct((table_rows // groups, PAIR), jnp.bfloat16)] * groups,
        scratch_shapes=[
            pltpu.VMEM((table_rows, PAIR), jnp.float32),
            pltpu.VMEM(normed.shape, jnp.bfloat16),
            pltpu.VMEM(grad, jnp.float32),
            pltpu.SMEM((need.shape[0],), jnp.int32),
            pltpu.SemaphoreType.DMA,
        ],
        compiler_params=room(60),
        cost_estimate=cost(11),
        name="scatter_rows",
    )(where, need, own, halo, rows, normed, *earlier)


def finish_kernel(shares_ref, wq_ref, wk_ref, wv_ref, wo_ref, grads):
    count, total_rows, _ = grads.shape
    heads = count // 2
    rows = shares_ref.shape[1] // count
    for p in range(shares_ref.shape[0]):
        for m in range(count):
            grads[m, p * rows : (p + 1) * rows, :] = shares_ref[p, m * rows : (m + 1) * rows, :]
    for f in range(total_rows // PAIR):
        block = slice(f * PAIR, (f + 1) * PAIR)
        turned = [jnp.transpose(grads[m, block, :]) for m in range(count)]
        for h in range(heads):
            here = slice(h * HEAD, (h + 1) * HEAD)
            wo_ref[here, block] = grads[h, f * PAIR + HEAD : (f + 1) * PAIR, :]
        wq_ref[block, :] = 0.125 * jnp.concatenate([t[:, :HEAD] for t in turned[:heads]], axis=1)
        wk_ref[block, :] = jnp.concatenate([t[:, :HEAD] for t in turned[heads:]], axis=1)
        wv_ref[block, :] = jnp.concatenate([t[:, HEAD:] for t in turned[heads:]], axis=1)


def finish(shares, width, columns):
    tall = jax.ShapeDtypeStruct((width, columns), jnp.float32)
    return pl.pallas_call(
        finish_kernel,
        in_specs=[VMEM],
        out_specs=[VMEM] * 4,
        out_shape=[tall] * 3 + [jax.ShapeDtypeStruct((columns, width), jnp.float32)],
        scratch_shapes=[pltpu.VMEM((2 * columns // HEAD, width, columns), jnp.float32)],
        compiler_params=room(24),
        cost_estimate=cost(2),
        name="finish",
    )(shares)


def grid_kernel(groups, heads, where_ref, weight_ref, feat_ref, gain_ref, *rest):
    parts = rest[: groups * heads]
    out_refs = rest[groups * heads : -1]
    placed = rest[-1]
    me = where_ref[0]
    d_src = None
    for s in range(groups):
        f = lax.rem(me - s + groups, groups)
        for h in range(heads):
            part = mm(parts[s * heads + h][...], weight_ref[f, 0, h])
            d_src = part if d_src is None else d_src + part
    hat, inverse = hat_of(feat_ref[...].astype(jnp.float32))
    result = norm_back(d_src * gain_ref[...], hat, inverse).astype(jnp.bfloat16)
    columns = placed.shape[2]
    for f in range(groups):
        placed[f] = result[:, f * columns : (f + 1) * columns]
    for s, ref in enumerate(out_refs):
        ref[...] = placed[lax.rem(me + s, groups)]


def grid_rows(where, weight, feat, gain, parts):
    groups, heads = len(parts), len(parts[0])
    rows = parts[0][0].shape[0]
    width = feat.shape[1]
    columns = width // groups
    step = 256
    steps = rows // step
    return pl.pallas_call(
        lambda *refs: grid_kernel(groups, heads, *refs),
        grid_spec=pltpu.PrefetchScalarGridSpec(
            num_scalar_prefetch=1,
            grid=(steps,),
            in_specs=[
                pl.BlockSpec((groups, 1, heads, PAIR, width), lambda i, w: (0, 0, 0, 0, 0)),
                pl.BlockSpec((step, width), lambda i, w: (w[0] * steps + i, 0)),
                pl.BlockSpec((1, width), lambda i, w: (0, 0)),
            ]
            + [pl.BlockSpec((step, PAIR), lambda i, w: (i, 0))] * (groups * heads),
            out_specs=[pl.BlockSpec((step, columns), lambda i, w: (i, 0))] * groups,
            scratch_shapes=[pltpu.VMEM((groups, step, columns), jnp.bfloat16)],
        ),
        out_shape=[jax.ShapeDtypeStruct((rows, columns), jnp.bfloat16)] * groups,
        compiler_params=room(60),
        cost_estimate=cost(6),
        name="grid_rows",
    )(where, weight, feat, gain, *[part for row in parts for part in row])


def mesh_kernel(heads, where_ref, weight_ref, feat_ref, cot_ref, gain_ref, *rest):
    parts, (mesh_out_ref, grad_ref, wide) = rest[:heads], rest[heads:]
    groups, columns = weight_ref.shape[0], cot_ref.shape[1]
    mine = pl.ds(pl.multiple_of(where_ref[0] * columns, columns), columns)
    keep_first, keep_second = halves()
    d_dst, added = None, None
    for f in range(groups):
        for h in range(heads):
            part = parts[h][f]
            one = mm(part * keep_first, weight_ref[f, 0, h])
            two = mm(part * keep_second, weight_ref[f, 0, h, :, mine])
            d_dst = one if d_dst is None else d_dst + one
            added = two if added is None else added + two
    feat = feat_ref[...].astype(jnp.float32)
    hat, inverse = hat_of(feat)
    wide[0] = feat
    wide[1] = norm_back(d_dst * 0.125 * gain_ref[...], hat, inverse)
    mesh_out_ref[...] = (wide[0, :, mine] + added).astype(jnp.bfloat16)
    grad_ref[...] = (cot_ref[...].astype(jnp.float32) + wide[1, :, mine]).astype(jnp.bfloat16)


def mesh_rows(where, weight, feat, cot, gain, parts):
    groups, heads = weight.shape[0], len(parts)
    rows, width = feat.shape
    columns = cot.shape[1]
    step = 256
    narrow = pl.BlockSpec((step, columns), lambda i, w: (i, 0))
    return pl.pallas_call(
        lambda *refs: mesh_kernel(heads, *refs),
        grid_spec=pltpu.PrefetchScalarGridSpec(
            num_scalar_prefetch=1,
            grid=(rows // step,),
            in_specs=[
                pl.BlockSpec((groups, 1, heads, PAIR, width), lambda i, w: (0, 1, 0, 0, 0)),
                pl.BlockSpec((step, width), lambda i, w: (i, 0)),
                narrow,
                pl.BlockSpec((1, width), lambda i, w: (0, 0)),
            ]
            + [pl.BlockSpec((groups, step, PAIR), lambda i, w: (0, i, 0))] * heads,
            out_specs=[narrow] * 2,
            scratch_shapes=[pltpu.VMEM((2, step, width), jnp.float32)],
        ),
        out_shape=[jax.ShapeDtypeStruct((rows, columns), jnp.bfloat16)] * 2,
        compiler_params=room(60),
        cost_estimate=cost(11),
        name="mesh_rows",
    )(where, weight, feat, cot, gain, *parts)


def place_kernel(groups, where_ref, *rest):
    parts, out_ref = rest[:groups], rest[groups]
    rows = parts[0].shape[0]
    for s in range(groups):
        f = lax.rem(where_ref[0] - s + groups, groups)
        here = pl.ds(pl.multiple_of(f * rows, rows), rows)
        out_ref[here, :] = parts[s][...]


def place_rows(where, parts):
    groups = len(parts)
    rows, columns = parts[0].shape
    return pl.pallas_call(
        lambda *refs: place_kernel(groups, *refs),
        in_specs=[SMEM] + [VMEM] * groups,
        out_specs=VMEM,
        out_shape=jax.ShapeDtypeStruct((groups * rows, columns), jnp.bfloat16),
        compiler_params=room(24),
        cost_estimate=cost(2),
        name="place_rows",
    )(where, *parts)


def over_graph(values):
    return lax.all_to_all(values, "graph", split_axis=0, concat_axis=0, tiled=True)


def over_feat(parts):
    groups = len(parts)
    return [parts[0]] + [
        lax.ppermute(parts[s], "feat", [(i, (i + s) % groups) for i in range(groups)])
        for s in range(1, groups)
    ]


def after(values, earlier):
    return lax.optimization_barrier((values, earlier))


def by_head(first, second):
    heads = first.shape[0] // HEAD
    parts = [x.reshape(heads, HEAD, -1) for x in (first, second)]
    return jnp.concatenate(parts, axis=1)


def body(
    grid_feat,
    mesh_feat,
    send_rows,
    tile_src,
    edge_mask,
    gain_src,
    gain_dst,
    w_query,
    w_key,
    w_value,
    w_out,
    d_out,
):
    grid_count, width = grid_feat.shape
    columns = w_query.shape[1]
    heads = columns // HEAD
    groups = width // columns
    peers = send_rows.shape[1]
    own_tiles = grid_count // TS
    where = lax.axis_index("feat").astype(jnp.int32).reshape(1)
    gain_src = gain_src.reshape(1, width)
    gain_dst = gain_dst.reshape(1, width)
    rows = send_rows.reshape(2 * peers, 1, TS)

    wanted = own_tiles + jnp.arange(2 * peers, dtype=jnp.int32)
    need = jnp.any(tile_src.reshape(-1, 1) == wanted[None, :], axis=0).astype(jnp.int32)
    need = over_graph(jnp.broadcast_to(need.reshape(peers, 2, 1), (peers, 2, TS)))
    need = need[:, :, 0].reshape(-1)

    cot = lax.all_gather(d_out, "feat", axis=0)
    back_weights = jnp.stack([by_head(w_key.T, w_value.T), by_head(w_query.T, w_out)])
    back_weights = lax.all_gather(back_weights, "feat", axis=0)

    pairs = source_terms(grid_feat, gain_src, w_key, w_value)
    outgoing = gather_rows(need, rows, pairs)
    normed_src = normed_rows(grid_feat, gain_src)
    normed_dst, *targets = target_terms(mesh_feat, gain_dst, w_query, w_out, cot)

    halo = []
    for h in range(heads):
        sent = outgoing[h]
        if h > 0:
            sent, (halo[h - 1], normed_src) = after(sent, (halo[h - 1], normed_src))
        halo.append(over_graph(sent))

    own_grads, returned, mixed, weight_grads = [], [], [], []
    for h in range(heads):
        own_grad, halo_grad, weight_grad, mixed_columns = attention(
            h, tile_src, pairs, halo[h], targets[h], edge_mask, normed_dst, cot
        )
        own_grads.append(own_grad)
        weight_grads.append(weight_grad)
        mixed.append(lax.all_gather(mixed_columns, "feat", axis=0))
        if h == 0:
            halo_grad, (halo[heads - 1], back_weights) = after(
                halo_grad, (halo[heads - 1], back_weights)
            )
        else:
            halo_grad, (returned[h - 1], mixed[h - 1]) = after(
                halo_grad, (returned[h - 1], mixed[h - 1])
            )
        returned.append(over_graph(halo_grad))

    sums = []
    for h in range(heads):
        last = h == heads - 1
        if last:
            returned[h], (sums, weight_grads, mixed) = after(
                returned[h], (sums, weight_grads, mixed)
            )
        weight_grad, *blocks = scatter_rows(
            where,
            need,
            own_grads[h],
            returned[h],
            rows,
            normed_src,
            groups,
            weight_grads if last else (),
            peers,
        )
        weight_grads.append(weight_grad)
        sums.append(over_feat(blocks))

    share = jnp.sum(over_graph(weight_grads[-1]), axis=0)
    sum_rows = [[sums[h][s] for h in range(heads)] for s in range(groups)]
    grid_parts = grid_rows(where, back_weights, grid_feat, gain_src, sum_rows)

    share, (grid_parts, mixed) = after(share, (grid_parts, mixed))
    grad_grid = place_rows(where, over_feat(grid_parts))
    shares = over_graph(jnp.broadcast_to(share[None], weight_grads[-1].shape))
    mesh_out, grad_mesh = mesh_rows(where, back_weights, mesh_feat, d_out, gain_dst, mixed)
    shares, (mesh_out, grad_mesh) = after(shares, (mesh_out, grad_mesh))
    grad_wq, grad_wk, grad_wv, grad_wo = finish(shares, width, columns)
    return (mesh_out, grad_grid, grad_mesh, grad_wq, grad_wk, grad_wv, grad_wo)


def solution(mesh):
    in_specs = (
        P("graph", None),
        P("graph", None),
        P("graph", None, None),
        P("graph", None),
        P("graph", None),
        P(),
        P(),
        P(None, "feat"),
        P(None, "feat"),
        P(None, "feat"),
        P("feat", None),
        P("graph", "feat"),
    )
    out_specs = (
        P("graph", "feat"),
        P("graph", "feat"),
        P("graph", "feat"),
        P(None, "feat"),
        P(None, "feat"),
        P(None, "feat"),
        P("feat", None),
    )
    return jax.shard_map(body, mesh=mesh, in_specs=in_specs, out_specs=out_specs, check_vma=False)
```

time: 677 us -> 264 us (0.39)
  waiting for transfers between devices: 285 us -> 68.6 us
  other arithmetic: 141 us -> 1.05 us
  Pallas kernels: 0 us -> 100 us
  matrix products: 97.5 us -> 0 us
  local copies, waits for them, and re-layouts: 96.8 us -> 9.91 us
  starting transfers between devices: 21.6 us -> 68.3 us
  blocking collectives: 12.2 us -> 0 us
    pallas_call x0 -> x12, Pallas kernels: none -> 100 us  [the longest x2 35.6 us: attention(): pl.pallas_call(lambda *refs: attention_kernel(head, *refs), grid=(blocks,...]
    psum x1 -> x0, waiting for transfers between devices: 85.8 us -> none  [body(): lax.psum((grad_wq, grad_wk, grad_wv, grad_wo), 'graph')]
    dot_general x34 -> x0, matrix products: 81.7 us -> none  [the longest x4 12.9 us: block_terms(): jnp.einsum('thd,ehd->hte', g_heads, v_heads, preferred_element_type=jnp.f...]
    scatter-add x9 -> x0, other arithmetic: 70.7 us -> none  [the longest x1 49.1 us: body(): own_part.at[flat_rows]]
    all_to_all x2 -> x7, waiting for transfers between devices: 106 us -> 38.1 us  [over_graph(): lax.all_to_all(values, 'graph', split_axis=0, concat_axis=0, tiled=True)]
    reduce_scatter x3 -> x0, waiting for transfers between devices: 62.7 us -> none  [the longest x1 62.7 us: body(): src_share = lax.psum_scatter(d_src, 'feat', scatter_dimension=1, tiled=True)]
    gather x17 -> x0, local copies, waits for them, and re-layouts: 57.9 us -> none  [the longest x1 36.5 us: body(): src_normed[flat_rows].reshape(peer_count, boundary, full_width)]
    all_to_all x2 -> x7, starting transfers between devices: 21.2 us -> 55.4 us  [over_graph(): lax.all_to_all(values, 'graph', split_axis=0, concat_axis=0, tiled=True)]
  transfers between devices with their start and end apart: 7 -> 20, of which waited for: 5 -> 8; matrix products, arithmetic and copies ran while one was open for 16% -> 2% of each run, Pallas kernels for 0% -> 35%
where the time goes in v2:
time: 264 us; the launch traced here: 262 us
  Pallas kernels  100 us (38%)
  waiting for transfers between devices  68.6 us (26%)
  starting transfers between devices  68.3 us (26%)
  between operations  14.2 us (5%)
  local copies, waits for them, and re-layouts  9.91 us (4%)
    all_to_all x7, starting transfers between devices, over_graph(): lax.all_to_all(values, 'graph', split_axis=0, concat_axis=0, tiled=True)  55.4 us
    all_to_all x7, waiting for transfers between devices, over_graph(): lax.all_to_all(values, 'graph', split_axis=0, concat_axis=0, tiled=True)  38.1 us
    pallas_call x2, Pallas kernels, attention(): pl.pallas_call(lambda *refs: attention_kernel(head, *refs), grid=(blocks,...  35.6 us
    ppermute x9, waiting for transfers between devices, over_feat(): lax.ppermute(parts[s], 'feat', [(i, (i + s) % groups) for i in range(grou...  29.7 us
    pallas_call x2, Pallas kernels, scatter_rows(): pl.pallas_call(lambda *refs: scatter_kernel(len(earlier), *refs), in_spec...  15.4 us
    ppermute x9, starting transfers between devices, over_feat(): lax.ppermute(parts[s], 'feat', [(i, (i + s) % groups) for i in range(grou...  12.5 us
    pallas_call x1, Pallas kernels, mesh_rows(): pl.pallas_call(lambda *refs: mesh_kernel(heads, *refs), grid_spec=pltpu.P...  10.8 us
    pallas_call x1, Pallas kernels, gather_rows(): pl.pallas_call(gather_kernel, in_specs=[SMEM, VMEM, VMEM], out_specs=[ANY...  8.74 us
  transfers between devices with their start and end apart: 20, of which 8 were waited for; matrix products, arithmetic and copies ran while one was open for 2% of the time, Pallas kernels for 35%

profile of v2, /device:TPU:1, one launch (start us, length us, event | category | flops | bytes accessed | tf_op | source)
XLA Modules:
  0.0 262.5 jit_solution(4986080656451262298)
XLA Ops:
  8.9 9.6 %all-to-all-start = ((s32[32,2,128]{2,1,0:T(2,128)}), s32[32,2,128]{2,1,0:T(2,128)S(1)}, u32[]{:S(2)}, u32[]{:S(2)}) async-start(s32[32,2,128]{2,1,0:T(2,128)} %broadcast_in_dim.4), calls=%async_computation | async-start | bytes 65536 | tf_op jit(solution)/shard_map/all_to_all | solution.py:677
  19.2 7.7 %source_terms.1.refs_1_ = bf16[4096,256]{1,0:T(8,128)(2,1)} custom-call(bf16[4096,512]{1,0:T(8,128)(2,1)} %refs_2_.2, f32[1,512]{1,0:T(1,128)} %bitcast.33, bf16[512,128]{1,0:T(8,128)(2,1)} %key_ref.1, bf16[512,128]{1,0:T(8,128)(2,1)} %value_ref.1), custom_call_target="tpu_custom_call" | custom-call | flops 9200000000 | bytes 1048576 | tf_op jit(solution)/shard_map/source_terms/pallas_call | solution.py:94
  28.8 8.7 %gather_rows.1 = (bf16[32,256,128]{2,1,0:T(8,128)(2,1)}, bf16[32,256,128]{2,1,0:T(8,128)(2,1)}) custom-call(s32[64]{0:T(128)} %reshape_squeeze.3.need_ref.refs_1_, s32[64,1,128]{2,1,0:T(1,128)} %reshape.58.rows_ref.refs_4_, bf16[2,2048,256]{2,1,0:T(8,128)(2,1)} %bitcast.38), custom_call_target="tpu_custom_call" | custom-call | flops 11500000256 | bytes 1048576 | tf_op jit(solution)/shard_map/gather_rows/pallas_call | solution.py:179
  37.6 9.9 %all-to-all-start.1 = ((bf16[32,256,128]{2,1,0:T(8,128)(2,1)}), bf16[32,256,128]{2,1,0:T(8,128)(2,1)S(1)}, u32[]{:S(2)}, u32[]{:S(2)}) async-start(bf16[32,256,128]{2,1,0:T(8,128)(2,1)} %get-tuple-element.70), calls=%async_computation.1 | async-start | bytes 4194304 | tf_op jit(solution)/shard_map/all_to_all | solution.py:677
  48.8 7.7 %normed_rows.1.refs_5_ = bf16[4096,512]{1,0:T(8,128)(2,1)} custom-call(bf16[4096,512]{1,0:T(8,128)(2,1)} %refs_2_.2, f32[1,512]{1,0:T(1,128)} %bitcast.34), custom_call_target="tpu_custom_call" | custom-call | flops 9200000000 | bytes 1048576 | tf_op jit(solution)/shard_map/normed_rows/pallas_call | solution.py:204
  56.5 18.8 %all-to-all-done.1.refs_2_ = bf16[32,256,128]{2,1,0:T(8,128)(2,1)S(1)} async-done(((bf16[32,256,128]{2,1,0:T(8,128)(2,1)}), bf16[32,256,128]{2,1,0:T(8,128)(2,1)S(1)}, u32[]{:S(2)}, u32[]{:S(2)}) %all-to-all-start.1) | async-done | bytes 2097184 | tf_op jit(solution)/shard_map/all_to_all | solution.py:677
  75.3 1.4 copy-done.2
  76.7 6.7 %all-to-all-start.2 = ((bf16[32,256,128]{2,1,0:T(8,128)(2,1)}), bf16[32,256,128]{2,1,0:T(8,128)(2,1)}, u32[]{:S(2)}, u32[]{:S(2)}) async-start(bf16[32,256,128]{2,1,0:T(8,128)(2,1)} %get-tuple-element.75), calls=%async_computation.2 | async-start | bytes 4194304 | tf_op jit(solution)/shard_map/all_to_all | solution.py:677
  83.5 5.9 %target_terms.1 = (bf16[2048,512]{1,0:T(8,128)(2,1)}, bf16[2048,128]{1,0:T(8,128)(2,1)}, bf16[2048,128]{1,0:T(8,128)(2,1)}) custom-call(bf16[2048,512]{1,0:T(8,128)(2,1)} %refs_2_.3, f32[1,512]{1,0:T(1,128)} %bitcast.36, bf16[512,128]{1,0:T(8,128)(2,1)} %wq_ref.1, bf16[128,512]{1,0:T(8,128)(2,1)} %wo_ref.1, bf16[4,2048,128]{2,1,0:T(8,128)(2,1)} %bitcast.30), custom_call_target="tpu_custom_call" | custom-call | flops 6899999744 | bytes 1048576 | tf_op jit(solution)/shard_map/target_terms/pallas_call | solution.py:236
  89.4 17.7 %attention.2 = (bf16[4096,128]{1,0:T(8,128)(2,1)}, bf16[32,256,128]{2,1,0:T(8,128)(2,1)}, f32[4,128,128]{2,1,0:T(8,128)}, bf16[2048,128]{1,0:T(8,128)(2,1)}) custom-call(s32[4,8]{1,0:T(4,128)} %refs_0_.3, bf16[4096,256]{1,0:T(8,128)(2,1)} %source_terms.1.refs_1_, bf16[32,256,128]{2,1,0:T(8,128)(2,1)} %copy-done.2, ...), custom_call_target="tpu_custom_call" | custom-call | flops 20700000256 | bytes 1048576 | tf_op jit(solution)/shard_map/attention/pallas_call | solution.py:399
  107.2 4.2 %all-to-all-done.2.refs_2_ = bf16[32,256,128]{2,1,0:T(8,128)(2,1)} async-done(((bf16[32,256,128]{2,1,0:T(8,128)(2,1)}), bf16[32,256,128]{2,1,0:T(8,128)(2,1)}, u32[]{:S(2)}, u32[]{:S(2)}) %all-to-all-start.2) | async-done | bytes 2097184 | tf_op jit(solution)/shard_map/all_to_all | solution.py:677
  111.4 6.1 %all-to-all-start.3 = ((bf16[32,256,128]{2,1,0:T(8,128)(2,1)}), bf16[32,256,128]{2,1,0:T(8,128)(2,1)S(1)}, u32[]{:S(2)}, u32[]{:S(2)}) async-start(bf16[32,256,128]{2,1,0:T(8,128)(2,1)} %get-tuple-element.80), calls=%async_computation.3 | async-start | bytes 4194304 | tf_op jit(solution)/shard_map/all_to_all | solution.py:677
  117.7 17.9 %attention.3 = (bf16[4096,128]{1,0:T(8,128)(2,1)}, bf16[32,256,128]{2,1,0:T(8,128)(2,1)}, f32[4,128,128]{2,1,0:T(8,128)}, bf16[2048,128]{1,0:T(8,128)(2,1)}) custom-call(s32[4,8]{1,0:T(4,128)} %refs_0_.3, bf16[4096,256]{1,0:T(8,128)(2,1)} %source_terms.1.refs_1_, bf16[32,256,128]{2,1,0:T(8,128)(2,1)} %all-to-all-done.2.refs_2_, ...), custom_call_target="tpu_custom_call" | custom-call | flops 20700000256 | bytes 1048576 | tf_op jit(solution)/shard_map/attention/pallas_call | solution.py:399
  135.6 9.8 %all-to-all-done.3.refs_3_ = bf16[32,256,128]{2,1,0:T(8,128)(2,1)S(1)} async-done(((bf16[32,256,128]{2,1,0:T(8,128)(2,1)}), bf16[32,256,128]{2,1,0:T(8,128)(2,1)S(1)}, u32[]{:S(2)}, u32[]{:S(2)}) %all-to-all-start.3) | async-done | bytes 2097184 | tf_op jit(solution)/shard_map/all_to_all | solution.py:677
  145.5 1.4 copy-done.3
  146.9 6.0 %all-to-all-start.4 = ((bf16[32,256,128]{2,1,0:T(8,128)(2,1)}), bf16[32,256,128]{2,1,0:T(8,128)(2,1)S(1)}, u32[]{:S(2)}, u32[]{:S(2)}) async-start(bf16[32,256,128]{2,1,0:T(8,128)(2,1)} %get-tuple-element.82), calls=%async_computation.4 | async-start | bytes 4194304 | tf_op jit(solution)/shard_map/all_to_all | solution.py:677
  152.9 7.5 %scatter_rows.2 = (f32[4,128,128]{2,1,0:T(8,128)}, bf16[1024,128]{1,0:T(8,128)(2,1)}, bf16[1024,128]{1,0:T(8,128)(2,1)}, bf16[1024,128]{1,0:T(8,128)(2,1)}, bf16[1024,128]{1,0:T(8,128)(2,1)}) custom-call(s32[1]{0:T(128)} %bitcast.refs_0_, s32[64]{0:T(128)} %reshape_squeeze.3.need_ref.refs_1_, bf16[4096,128]{1,0:T(8,128)(2,1)} %get-tuple-element.83.refs_2_, ...), custom_call_target="tpu_custom_call" | custom-call | flops 12650000384 | bytes 1048576 | tf_op jit(solution)/shard_map/scatter_rows/pallas_call | solution.py:505
  161.7 2.5 collective-permute-start.1
  165.3 10.4 %collective-permute-done.refs_6_ = bf16[1024,128]{1,0:T(8,128)(2,1)S(1)} collective-permute-done((bf16[1024,128]{1,0:T(8,128)(2,1)}, bf16[1024,128]{1,0:T(8,128)(2,1)S(1)}, u32[]{:S(2)}, u32[]{:S(2)}) %collective-permute-start) | collective-permute-done | bytes 262176 | tf_op jit(solution)/shard_map/ppermute | solution.py:683
  175.6 7.7 %collective-permute-done.1.refs_8_ = bf16[1024,128]{1,0:T(8,128)(2,1)S(1)} collective-permute-done((bf16[1024,128]{1,0:T(8,128)(2,1)}, bf16[1024,128]{1,0:T(8,128)(2,1)S(1)}, u32[]{:S(2)}, u32[]{:S(2)}) %collective-permute-start.1) | collective-permute-done | bytes 262176 | tf_op jit(solution)/shard_map/ppermute | solution.py:683
  183.3 1.4 copy-done.1
  184.8 8.0 %scatter_rows.3 = (f32[32,64,128]{2,1,0:T(8,128)}, bf16[1024,128]{1,0:T(8,128)(2,1)}, bf16[1024,128]{1,0:T(8,128)(2,1)}, bf16[1024,128]{1,0:T(8,128)(2,1)}, bf16[1024,128]{1,0:T(8,128)(2,1)}) custom-call(s32[1]{0:T(128)} %bitcast.refs_0_, s32[64]{0:T(128)} %reshape_squeeze.3.need_ref.refs_1_, bf16[4096,128]{1,0:T(8,128)(2,1)} %get-tuple-element.78.refs_2_, ...), custom_call_target="tpu_custom_call" | custom-call | flops 12650000384 | bytes 1048576 | tf_op jit(solution)/shard_map/scatter_rows/pallas_call | solution.py:505
  192.8 9.0 %all-to-all-start.5 = ((f32[32,64,128]{2,1,0:T(8,128)}), f32[32,64,128]{2,1,0:T(8,128)S(1)}, u32[]{:S(2)}, u32[]{:S(2)}) async-start(f32[32,64,128]{2,1,0:T(8,128)} %get-tuple-element.99), calls=%async_computation.5 | async-start | bytes 2097152 | tf_op jit(solution)/shard_map/all_to_all | solution.py:677
  203.2 1.8 collective-permute-start.5
  205.0 11.4 %collective-permute-done.3.refs_7_ = bf16[1024,128]{1,0:T(8,128)(2,1)S(1)} collective-permute-done((bf16[1024,128]{1,0:T(8,128)(2,1)S(1)}, bf16[1024,128]{1,0:T(8,128)(2,1)S(1)}, u32[]{:S(2)}, u32[]{:S(2)}) %collective-permute-start.3) | collective-permute-done | bytes 262176 | tf_op jit(solution)/shard_map/ppermute | solution.py:683
  217.4 6.2 %grid_rows.1 = (bf16[1024,128]{1,0:T(8,128)(2,1)}, bf16[1024,128]{1,0:T(8,128)(2,1)}, bf16[1024,128]{1,0:T(8,128)(2,1)}, bf16[1024,128]{1,0:T(8,128)(2,1)}) custom-call(s32[1]{0:T(128)} %bitcast.refs_0_, bf16[4,2,2,128,512]{4,3,2,1,0:T(8,128)(2,1)} %bitcast.26, bf16[4096,512]{1,0:T(8,128)(2,1)} %refs_2_.2, f32[1,512]{1,0:T(1,128)} %bitcast.35, ...), custom_call_target="tpu_custom_call" | custom-call | flops 6899999744 | bytes 1048576 | tf_op jit(solution)/shard_map/grid_rows/pallas_call | solution.py:583
  223.7 1.3 collective-permute-start.6
  225.0 3.2 %collective-permute-start.7 = (bf16[1024,128]{1,0:T(8,128)(2,1)}, bf16[1024,128]{1,0:T(8,128)(2,1)S(1)}, u32[]{:S(2)}, u32[]{:S(2)}) collective-permute-start(bf16[1024,128]{1,0:T(8,128)(2,1)} %get-tuple-element.123), channel_id=1, source_target_pairs={{0,2},{1,3},{2,0},{3,1},{4,6},{5,7},{6,4},{7,5},{8,10},{9,11},{10,... | collective-permute-start | bytes 786440 | tf_op jit(solution)/shard_map/ppermute | solution.py:683
  229.3 8.1 %all-to-all-start.6 = ((f32[32,64,128]{2,1,0:T(8,128)}), f32[32,64,128]{2,1,0:T(8,128)S(1)}, u32[]{:S(2)}, u32[]{:S(2)}) async-start(f32[32,64,128]{2,1,0:T(8,128)} %broadcast_in_dim.5), calls=%async_computation.6 | async-start | bytes 2097152 | tf_op jit(solution)/shard_map/all_to_all | solution.py:677
  237.4 10.8 %mesh_rows.1 = (bf16[2048,128]{1,0:T(8,128)(2,1)}, bf16[2048,128]{1,0:T(8,128)(2,1)}) custom-call(s32[1]{0:T(128)} %bitcast.refs_0_, bf16[4,2,2,128,512]{4,3,2,1,0:T(8,128)(2,1)} %bitcast.27, bf16[2048,512]{1,0:T(8,128)(2,1)} %refs_2_.3, bf16[2048,128]{1,0:T(8,128)(2,1)} %refs_3_.1, f32[1,512]{1,0:T(1,128)} %bitcast.37, bf16[4,2048,128]{2,1,0:T(8,128)(2,1)} %bitcast.28, ...), custom_call_target="tpu_custom_call" | custom-call | flops 12650000384 | bytes 1048576 | tf_op jit(solution)/shard_map/mesh_rows/pallas_call | solution.py:631
  249.3 5.3 %all-to-all-done.6.shares_ref = f32[32,64,128]{2,1,0:T(8,128)S(1)} async-done(((f32[32,64,128]{2,1,0:T(8,128)}), f32[32,64,128]{2,1,0:T(8,128)S(1)}, u32[]{:S(2)}, u32[]{:S(2)}) %all-to-all-start.6) | async-done | bytes 1048608 | tf_op jit(solution)/shard_map/all_to_all | solution.py:677
  254.5 1.4 finish.1
  (76 shorter events, 13.0 us)
Async XLA Ops:
  8.9 18.7 %all-to-all-start = ((s32[32,2,128]{2,1,0:T(2,128)}), s32[32,2,128]{2,1,0:T(2,128)S(1)}, u32[]{:S(2)}, u32[]{:S(2)}) async-start(s32[32,2,128]{2,1,0:T(2,128)} %broadcast_in_dim.4), calls=%async_computation | async-start | bytes 65536 | tf_op jit(solution)/shard_map/all_to_all | solution.py:677
  18.5 65.0 %all-gather.9.cloned.1.call-start = ((), (), s32[]{:S(2)}) async-start(), calls=%async_computation.7 | async-start | bytes 2621440 | tf_op jit(solution)/shard_map/all_gather | solution.py:728
  19.2 7.7 %copy-start.8 = (s32[1,32,256]{2,1,0:T(8,128)S(1)}, s32[1,32,256]{2,1,0:T(8,128)}, u32[]{:S(2)}) copy-start(s32[1,32,256]{2,1,0:T(8,128)} %param.14) | copy-start | bytes 98308
  37.5 10.0 %copy-start.4 = (bf16[512,128]{1,0:T(8,128)(2,1)S(1)}, bf16[512,128]{1,0:T(8,128)(2,1)}, u32[]{:S(2)}) copy-start(bf16[512,128]{1,0:T(8,128)(2,1)} %key_ref.1) | copy-start | bytes 393220
  37.6 10.1 %copy-start.5 = (bf16[512,128]{1,0:T(8,128)(2,1)S(1)}, bf16[512,128]{1,0:T(8,128)(2,1)}, u32[]{:S(2)}) copy-start(bf16[512,128]{1,0:T(8,128)(2,1)} %value_ref.1) | copy-start | bytes 393220
  37.6 10.2 %copy-start.6 = (bf16[512,128]{1,0:T(8,128)(2,1)S(1)}, bf16[512,128]{1,0:T(8,128)(2,1)}, u32[]{:S(2)}) copy-start(bf16[512,128]{1,0:T(8,128)(2,1)} %wq_ref.1) | copy-start | bytes 393220
  37.6 10.3 %copy-start.7 = (bf16[128,512]{1,0:T(8,128)(2,1)S(1)}, bf16[128,512]{1,0:T(8,128)(2,1)}, u32[]{:S(2)}) copy-start(bf16[128,512]{1,0:T(8,128)(2,1)} %wo_ref.1) | copy-start | bytes 393220
  37.6 37.7 %all-to-all-start.1 = ((bf16[32,256,128]{2,1,0:T(8,128)(2,1)}), bf16[32,256,128]{2,1,0:T(8,128)(2,1)S(1)}, u32[]{:S(2)}, u32[]{:S(2)}) async-start(bf16[32,256,128]{2,1,0:T(8,128)(2,1)} %get-tuple-element.70), calls=%async_computation.1 | async-start | bytes 4194304 | tf_op jit(solution)/shard_map/all_to_all | solution.py:677
  47.5 59.7 %all-gather.11.cloned.1.call-start = ((), (), s32[]{:S(2)}) async-start(), calls=%async_computation.8 | async-start | bytes 2621440 | tf_op jit(solution)/shard_map/all_gather | solution.py:730
  76.7 34.7 %all-to-all-start.2 = ((bf16[32,256,128]{2,1,0:T(8,128)(2,1)}), bf16[32,256,128]{2,1,0:T(8,128)(2,1)}, u32[]{:S(2)}, u32[]{:S(2)}) async-start(bf16[32,256,128]{2,1,0:T(8,128)(2,1)} %get-tuple-element.75), calls=%async_computation.2 | async-start | bytes 4194304 | tf_op jit(solution)/shard_map/all_to_all | solution.py:677
  83.4 62.0 %all-gather.13.cloned.1.call-start = ((), (), s32[]{:S(2)}) async-start(), calls=%async_computation.9 | async-start | bytes 2621440 | tf_op jit(solution)/shard_map/all_gather | solution.py:751
  111.4 34.0 %all-to-all-start.3 = ((bf16[32,256,128]{2,1,0:T(8,128)(2,1)}), bf16[32,256,128]{2,1,0:T(8,128)(2,1)S(1)}, u32[]{:S(2)}, u32[]{:S(2)}) async-start(bf16[32,256,128]{2,1,0:T(8,128)(2,1)} %get-tuple-element.80), calls=%async_computation.3 | async-start | bytes 4194304 | tf_op jit(solution)/shard_map/all_to_all | solution.py:677
  117.5 65.8 %all-gather.15.cloned.1.call-start = ((), (), s32[]{:S(2)}) async-start(), calls=%async_computation.10 | async-start | bytes 2621440 | tf_op jit(solution)/shard_map/all_gather | solution.py:751
  146.9 36.5 %all-to-all-start.4 = ((bf16[32,256,128]{2,1,0:T(8,128)(2,1)}), bf16[32,256,128]{2,1,0:T(8,128)(2,1)S(1)}, u32[]{:S(2)}, u32[]{:S(2)}) async-start(bf16[32,256,128]{2,1,0:T(8,128)(2,1)} %get-tuple-element.82), calls=%async_computation.4 | async-start | bytes 4194304 | tf_op jit(solution)/shard_map/all_to_all | solution.py:677
  160.4 15.2 %collective-permute-start = (bf16[1024,128]{1,0:T(8,128)(2,1)}, bf16[1024,128]{1,0:T(8,128)(2,1)S(1)}, u32[]{:S(2)}, u32[]{:S(2)}) collective-permute-start(bf16[1024,128]{1,0:T(8,128)(2,1)} %get-tuple-element.87), channel_id=1, source_target_pairs={{0,1},{1,2},{2,3},{3,0},{4,5},{5,6},{6,7},{7,4},{8,9},{9,10},{10,1... | collective-permute-start | bytes 786440 | tf_op jit(solution)/shard_map/ppermute | solution.py:683
  161.7 21.6 %collective-permute-start.1 = (bf16[1024,128]{1,0:T(8,128)(2,1)}, bf16[1024,128]{1,0:T(8,128)(2,1)S(1)}, u32[]{:S(2)}, u32[]{:S(2)}) collective-permute-start(bf16[1024,128]{1,0:T(8,128)(2,1)} %get-tuple-element.88), channel_id=1, source_target_pairs={{0,2},{1,3},{2,0},{3,1},{4,6},{5,7},{6,4},{7,5},{8,10},{9,11},{10,... | collective-permute-start | bytes 786440 | tf_op jit(solution)/shard_map/ppermute | solution.py:683
  164.1 19.2 %collective-permute-start.2 = (bf16[1024,128]{1,0:T(8,128)(2,1)}, bf16[1024,128]{1,0:T(8,128)(2,1)S(1)}, u32[]{:S(2)}, u32[]{:S(2)}) collective-permute-start(bf16[1024,128]{1,0:T(8,128)(2,1)} %get-tuple-element.89), channel_id=1, source_target_pairs={{0,3},{1,0},{2,1},{3,2},{4,7},{5,4},{6,5},{7,6},{8,11},{9,8},{10,9... | collective-permute-start | bytes 786440 | tf_op jit(solution)/shard_map/ppermute | solution.py:683
  175.6 17.1 %copy-start.9 = (bf16[1024,128]{1,0:T(8,128)(2,1)}, bf16[1024,128]{1,0:T(8,128)(2,1)S(1)}, u32[]{:S(2)}) copy-start(bf16[1024,128]{1,0:T(8,128)(2,1)S(1)} %collective-permute-done.refs_6_) | copy-start | bytes 786436
  183.3 9.5 %copy-start.10 = (bf16[1024,128]{1,0:T(8,128)(2,1)}, bf16[1024,128]{1,0:T(8,128)(2,1)S(1)}, u32[]{:S(2)}) copy-start(bf16[1024,128]{1,0:T(8,128)(2,1)S(1)} %collective-permute-done.1.refs_8_) | copy-start | bytes 786436
  183.3 9.5 %copy-start.11 = (bf16[1024,128]{1,0:T(8,128)(2,1)}, bf16[1024,128]{1,0:T(8,128)(2,1)S(1)}, u32[]{:S(2)}) copy-start(bf16[1024,128]{1,0:T(8,128)(2,1)S(1)} %collective-permute-done.2.refs_10_) | copy-start | bytes 786436
  192.8 9.0 %copy-start.15 = (bf16[1024,128]{1,0:T(8,128)(2,1)S(1)}, bf16[1024,128]{1,0:T(8,128)(2,1)}, u32[]{:S(2)}) copy-start(bf16[1024,128]{1,0:T(8,128)(2,1)} %get-tuple-element.104) | copy-start | bytes 786436
  192.8 9.1 %copy-start.13 = (bf16[1024,128]{1,0:T(8,128)(2,1)S(1)}, bf16[1024,128]{1,0:T(8,128)(2,1)}, u32[]{:S(2)}) copy-start(bf16[1024,128]{1,0:T(8,128)(2,1)} %get-tuple-element.106) | copy-start | bytes 786436
  192.8 10.4 %copy-start.12 = (bf16[1024,128]{1,0:T(8,128)(2,1)S(1)}, bf16[1024,128]{1,0:T(8,128)(2,1)}, u32[]{:S(2)}) copy-start(bf16[1024,128]{1,0:T(8,128)(2,1)} %get-tuple-element.108) | copy-start | bytes 786436
  192.8 30.8 %all-to-all-start.5 = ((f32[32,64,128]{2,1,0:T(8,128)}), f32[32,64,128]{2,1,0:T(8,128)S(1)}, u32[]{:S(2)}, u32[]{:S(2)}) async-start(f32[32,64,128]{2,1,0:T(8,128)} %get-tuple-element.99), calls=%async_computation.5 | async-start | bytes 2097152 | tf_op jit(solution)/shard_map/all_to_all | solution.py:677
  201.8 14.6 %collective-permute-start.3 = (bf16[1024,128]{1,0:T(8,128)(2,1)S(1)}, bf16[1024,128]{1,0:T(8,128)(2,1)S(1)}, u32[]{:S(2)}, u32[]{:S(2)}) collective-permute-start(bf16[1024,128]{1,0:T(8,128)(2,1)S(1)} %copy-done.15), channel_id=1, source_target_pairs={{0,1},{1,2},{2,3},{3,0},{4,5},{5,6},{6,7},{7,4},{8,9},{9,10},{10,1... | collective-permute-start | bytes 786440 | tf_op jit(solution)/shard_map/ppermute | solution.py:683
  201.9 14.5 %collective-permute-start.4 = (bf16[1024,128]{1,0:T(8,128)(2,1)S(1)}, bf16[1024,128]{1,0:T(8,128)(2,1)S(1)}, u32[]{:S(2)}, u32[]{:S(2)}) collective-permute-start(bf16[1024,128]{1,0:T(8,128)(2,1)S(1)} %copy-done.13), channel_id=1, source_target_pairs={{0,2},{1,3},{2,0},{3,1},{4,6},{5,7},{6,4},{7,5},{8,10},{9,11},{10,... | collective-permute-start | bytes 786440 | tf_op jit(solution)/shard_map/ppermute | solution.py:683
  203.2 13.5 %collective-permute-start.5 = (bf16[1024,128]{1,0:T(8,128)(2,1)S(1)}, bf16[1024,128]{1,0:T(8,128)(2,1)S(1)}, u32[]{:S(2)}, u32[]{:S(2)}) collective-permute-start(bf16[1024,128]{1,0:T(8,128)(2,1)S(1)} %copy-done.12), channel_id=1, source_target_pairs={{0,3},{1,0},{2,1},{3,2},{4,7},{5,4},{6,5},{7,6},{8,11},{9,8},{10,9... | collective-permute-start | bytes 786440 | tf_op jit(solution)/shard_map/ppermute | solution.py:683
  223.7 24.5 %collective-permute-start.6 = (bf16[1024,128]{1,0:T(8,128)(2,1)}, bf16[1024,128]{1,0:T(8,128)(2,1)S(1)}, u32[]{:S(2)}, u32[]{:S(2)}) collective-permute-start(bf16[1024,128]{1,0:T(8,128)(2,1)} %get-tuple-element.122), channel_id=1, source_target_pairs={{0,1},{1,2},{2,3},{3,0},{4,5},{5,6},{6,7},{7,4},{8,9},{9,10},{10,1... | collective-permute-start | bytes 786440 | tf_op jit(solution)/shard_map/ppermute | solution.py:683
  225.0 23.2 %collective-permute-start.7 = (bf16[1024,128]{1,0:T(8,128)(2,1)}, bf16[1024,128]{1,0:T(8,128)(2,1)S(1)}, u32[]{:S(2)}, u32[]{:S(2)}) collective-permute-start(bf16[1024,128]{1,0:T(8,128)(2,1)} %get-tuple-element.123), channel_id=1, source_target_pairs={{0,2},{1,3},{2,0},{3,1},{4,6},{5,7},{6,4},{7,5},{8,10},{9,11},{10,... | collective-permute-start | bytes 786440 | tf_op jit(solution)/shard_map/ppermute | solution.py:683
  228.2 20.0 %collective-permute-start.8 = (bf16[1024,128]{1,0:T(8,128)(2,1)}, bf16[1024,128]{1,0:T(8,128)(2,1)S(1)}, u32[]{:S(2)}, u32[]{:S(2)}) collective-permute-start(bf16[1024,128]{1,0:T(8,128)(2,1)} %get-tuple-element.124), channel_id=1, source_target_pairs={{0,3},{1,0},{2,1},{3,2},{4,7},{5,4},{6,5},{7,6},{8,11},{9,8},{10,9... | collective-permute-start | bytes 786440 | tf_op jit(solution)/shard_map/ppermute | solution.py:683
  229.3 25.3 %all-to-all-start.6 = ((f32[32,64,128]{2,1,0:T(8,128)}), f32[32,64,128]{2,1,0:T(8,128)S(1)}, u32[]{:S(2)}, u32[]{:S(2)}) async-start(f32[32,64,128]{2,1,0:T(8,128)} %broadcast_in_dim.5), calls=%async_computation.6 | async-start | bytes 2097152 | tf_op jit(solution)/shard_map/all_to_all | solution.py:677
  237.4 10.8 %copy-start = (bf16[1024,128]{1,0:T(8,128)(2,1)S(1)}, bf16[1024,128]{1,0:T(8,128)(2,1)}, u32[]{:S(2)}) copy-start(bf16[1024,128]{1,0:T(8,128)(2,1)} %get-tuple-element.121.refs_1_) | copy-start | bytes 786436
  (6 other events, 6.4 us)
Sparse Core Ops, SparseCore 0:
  21.0 31.7 all-gather.8
  55.0 30.8 all-gather.10
  107.3 31.8 all-gather.12
  141.3 36.7 all-gather.14

commit v3 on v2

--- a/solution.py
+++ b/solution.py
@@ -58,7 +58,7 @@
 
 def source_kernel(feat_hbm, gain_ref, key_ref, value_ref, pairs_ref, weight, feat, sems):
     i = pl.program_id(0)
-    ahead = 3
+    ahead = 2
 
     def fetch(n):
         step = feat.shape[1]
@@ -88,7 +88,7 @@
 def source_terms(feat, gain, w_key, w_value):
     rows, width = feat.shape
     wide = 2 * w_key.shape[1]
-    step = 512
+    step = 1024
     steps = rows // step
     whole = pl.BlockSpec(w_key.shape, lambda i: (0, 0))
     return pl.pallas_call(
@@ -110,7 +110,7 @@
 
 def list_tiles(need_ref, list_ref):
     def add(t, count):
-        used = need_ref[t] > 0
+        used = need_ref[t // 2, t % 2, 0] > 0
 
         @pl.when(used)
         def _():
@@ -118,13 +118,15 @@
 
         return count + used.astype(jnp.int32)
 
-    return lax.fori_loop(0, need_ref.shape[0], add, jnp.int32(0))
-
-
-def gather_kernel(need_ref, rows_ref, table_ref, *rest):
-    out_refs = rest[:-4]
-    hot, sent, list_ref, sems = rest[-4:]
+    return lax.fori_loop(0, list_ref.shape[0], add, jnp.int32(0))
+
+
+def gather_kernel(need_ref, rows_ref, table_hbm, *rest):
+    out_refs = rest[:-6]
+    table_ref, hot, sent, list_ref, sems, table_sem = rest[-6:]
     half = table_ref.shape[1]
+    fetch = pltpu.make_async_copy(table_hbm, table_ref, table_sem)
+    fetch.start()
     count = list_tiles(need_ref, list_ref)
 
     def copy(slot, k, h, t):
@@ -167,6 +169,7 @@
         return carry
 
     steps = (count + QUAD - 1) // QUAD
+    fetch.wait()
     lax.fori_loop(0, steps, quad, 0)
     each(steps - 2, lambda c: c.wait())
     each(steps - 1, lambda c: c.wait())
@@ -175,17 +178,19 @@
 def gather_rows(need, rows, pairs):
     count, wide = pairs.shape
     heads = wide // PAIR
-    peers = need.shape[0] // 2
+    peers = need.shape[0]
     return pl.pallas_call(
         gather_kernel,
-        in_specs=[SMEM, VMEM, VMEM],
+        in_specs=[SMEM, VMEM, ANY],
         out_specs=[ANY] * heads,
         out_shape=[jax.ShapeDtypeStruct((peers, 2 * TS, PAIR), jnp.bfloat16)] * heads,
         scratch_shapes=[
+            pltpu.VMEM((2, count // 2, wide), jnp.bfloat16),
             pltpu.VMEM((QUAD * TS, count // 2), jnp.bfloat16),
             pltpu.VMEM((2, heads, QUAD * TS, PAIR), jnp.bfloat16),
-            pltpu.SMEM((need.shape[0],), jnp.int32),
+            pltpu.SMEM((2 * need.shape[0],), jnp.int32),
             pltpu.SemaphoreType.DMA((2, QUAD, heads)),
+            pltpu.SemaphoreType.DMA,
         ],
         compiler_params=room(60),
         cost_estimate=cost(10),
@@ -512,7 +517,7 @@
             pltpu.VMEM((table_rows, PAIR), jnp.float32),
             pltpu.VMEM(normed.shape, jnp.bfloat16),
             pltpu.VMEM(grad, jnp.float32),
-            pltpu.SMEM((need.shape[0],), jnp.int32),
+            pltpu.SMEM((2 * need.shape[0],), jnp.int32),
             pltpu.SemaphoreType.DMA,
         ],
         compiler_params=room(60),
@@ -578,7 +583,7 @@
     rows = parts[0][0].shape[0]
     width = feat.shape[1]
     columns = width // groups
-    step = 256
+    step = 512
     steps = rows // step
     return pl.pallas_call(
         lambda *refs: grid_kernel(groups, heads, *refs),
@@ -723,7 +728,6 @@
     wanted = own_tiles + jnp.arange(2 * peers, dtype=jnp.int32)
     need = jnp.any(tile_src.reshape(-1, 1) == wanted[None, :], axis=0).astype(jnp.int32)
     need = over_graph(jnp.broadcast_to(need.reshape(peers, 2, 1), (peers, 2, TS)))
-    need = need[:, :, 0].reshape(-1)
 
     cot = lax.all_gather(d_out, "feat", axis=0)
     back_weights = jnp.stack([by_head(w_key.T, w_value.T), by_head(w_query.T, w_out)])
@@ -780,15 +784,15 @@
         weight_grads.append(weight_grad)
         sums.append(over_feat(blocks))
 
-    share = jnp.sum(over_graph(weight_grads[-1]), axis=0)
+    mixed, payload = after(mixed, weight_grads[-1])
+    mesh_out, grad_mesh = mesh_rows(where, back_weights, mesh_feat, d_out, gain_dst, mixed)
+    share = jnp.sum(over_graph(payload), axis=0)
+    share, (sums, mesh_out, grad_mesh) = after(share, (sums, mesh_out, grad_mesh))
+    shares = over_graph(jnp.broadcast_to(share[None], payload.shape))
     sum_rows = [[sums[h][s] for h in range(heads)] for s in range(groups)]
     grid_parts = grid_rows(where, back_weights, grid_feat, gain_src, sum_rows)
-
-    share, (grid_parts, mixed) = after(share, (grid_parts, mixed))
     grad_grid = place_rows(where, over_feat(grid_parts))
-    shares = over_graph(jnp.broadcast_to(share[None], weight_grads[-1].shape))
-    mesh_out, grad_mesh = mesh_rows(where, back_weights, mesh_feat, d_out, gain_dst, mixed)
-    shares, (mesh_out, grad_mesh) = after(shares, (mesh_out, grad_mesh))
+    shares, _ = after(shares, grid_parts)
     grad_wq, grad_wk, grad_wv, grad_wo = finish(shares, width, columns)
     return (mesh_out, grad_grid, grad_mesh, grad_wq, grad_wk, grad_wv, grad_wo)
 

time: 264 us -> 260 us (0.985)
  starting transfers between devices: 68.3 us -> 57.9 us
  Pallas kernels: 100 us -> 110 us
    all_to_all x7, starting transfers between devices: 55.4 us -> 45.5 us  [over_graph(): lax.all_to_all(values, 'graph', split_axis=0, concat_axis=0, tiled=True)]
    pallas_call x2, Pallas kernels: 15.4 us -> 21.3 us  [scatter_rows(): pl.pallas_call(lambda *refs: scatter_kernel(len(earlier), *refs), in_spec...]
    pallas_call x1, Pallas kernels: 8.74 us -> 13.6 us  [gather_rows(): pl.pallas_call(gather_kernel, in_specs=[SMEM, VMEM, ANY], out_specs=[ANY]...]
    ppermute x9, waiting for transfers between devices: 29.7 us -> 26.4 us  [over_feat(): lax.ppermute(parts[s], 'feat', [(i, (i + s) % groups) for i in range(grou...]
    unnamed x39 -> x35, local copies, waits for them, and re-layouts: 5.36 us -> 6.22 us
  transfers between devices with their start and end apart: 20 -> 20, of which waited for: 8 -> 9; matrix products, arithmetic and copies ran while one was open for 2% -> 1% of each run, Pallas kernels for 35% -> 38%
where the time goes in v3:
time: 260 us; the launch traced here: 259 us
  Pallas kernels  110 us (42%)
  waiting for transfers between devices  66.4 us (26%)
  starting transfers between devices  57.9 us (22%)
  between operations  14.2 us (5%)
  local copies, waits for them, and re-layouts  9.65 us (4%)
    all_to_all x7, starting transfers between devices, over_graph(): lax.all_to_all(values, 'graph', split_axis=0, concat_axis=0, tiled=True)  45.5 us
    all_to_all x7, waiting for transfers between devices, over_graph(): lax.all_to_all(values, 'graph', split_axis=0, concat_axis=0, tiled=True)  39.3 us
    pallas_call x2, Pallas kernels, attention(): pl.pallas_call(lambda *refs: attention_kernel(head, *refs), grid=(blocks,...  35.6 us
    ppermute x9, waiting for transfers between devices, over_feat(): lax.ppermute(parts[s], 'feat', [(i, (i + s) % groups) for i in range(grou...  26.4 us
    pallas_call x2, Pallas kernels, scatter_rows(): pl.pallas_call(lambda *refs: scatter_kernel(len(earlier), *refs), in_spec...  21.3 us
    pallas_call x1, Pallas kernels, gather_rows(): pl.pallas_call(gather_kernel, in_specs=[SMEM, VMEM, ANY], out_specs=[ANY]...  13.6 us
    ppermute x9, starting transfers between devices, over_feat(): lax.ppermute(parts[s], 'feat', [(i, (i + s) % groups) for i in range(grou...  12.1 us
    pallas_call x1, Pallas kernels, mesh_rows(): pl.pallas_call(lambda *refs: mesh_kernel(heads, *refs), grid_spec=pltpu.P...  10.8 us
  transfers between devices with their start and end apart: 20, of which 9 were waited for; matrix products, arithmetic and copies ran while one was open for 1% of the time, Pallas kernels for 38%

profile of v3, /device:TPU:1, one launch (start us, length us, event | category | flops | bytes accessed | tf_op | source)
XLA Modules:
  0.0 259.0 jit_solution(9300110436747570775)
XLA Ops:
  9.6 9.6 %all-to-all-start = ((s32[32,2,128]{2,1,0:T(2,128)}), s32[32,2,128]{2,1,0:T(2,128)S(1)}, u32[]{:S(2)}, u32[]{:S(2)}) async-start(s32[32,2,128]{2,1,0:T(2,128)} %broadcast_in_dim.4), calls=%async_computation | async-start | bytes 65536 | tf_op jit(solution)/shard_map/all_to_all | solution.py:682
  19.2 6.6 %source_terms.1.refs_1_ = bf16[4096,256]{1,0:T(8,128)(2,1)} custom-call(bf16[4096,512]{1,0:T(8,128)(2,1)} %refs_2_.3, f32[1,512]{1,0:T(1,128)} %bitcast.35, bf16[512,128]{1,0:T(8,128)(2,1)} %key_ref.1, bf16[512,128]{1,0:T(8,128)(2,1)} %value_ref.1), custom_call_target="tpu_custom_call" | custom-call | flops 9200000000 | bytes 1048576 | tf_op jit(solution)/shard_map/source_terms/pallas_call | solution.py:94
  27.1 13.6 %gather_rows.1 = (bf16[32,256,128]{2,1,0:T(8,128)(2,1)}, bf16[32,256,128]{2,1,0:T(8,128)(2,1)}) custom-call(s32[32,2,128]{2,1,0:T(2,128)} %copy-done.9, s32[64,1,128]{2,1,0:T(1,128)} %reshape.57.rows_ref.refs_4_, bf16[2,2048,256]{2,1,0:T(8,128)(2,1)} %bitcast.38), custom_call_target="tpu_custom_call" | custom-call | flops 11500000256 | bytes 1048576 | tf_op jit(solution)/shard_map/gather_rows/pallas_call | solution.py:182
  40.7 5.8 %all-to-all-start.1 = ((bf16[32,256,128]{2,1,0:T(8,128)(2,1)}), bf16[32,256,128]{2,1,0:T(8,128)(2,1)S(1)}, u32[]{:S(2)}, u32[]{:S(2)}) async-start(bf16[32,256,128]{2,1,0:T(8,128)(2,1)} %get-tuple-element.75), calls=%async_computation.1 | async-start | bytes 4194304 | tf_op jit(solution)/shard_map/all_to_all | solution.py:682
  47.9 7.7 %normed_rows.1.refs_5_ = bf16[4096,512]{1,0:T(8,128)(2,1)} custom-call(bf16[4096,512]{1,0:T(8,128)(2,1)} %refs_2_.3, f32[1,512]{1,0:T(1,128)} %bitcast.36), custom_call_target="tpu_custom_call" | custom-call | flops 9200000000 | bytes 1048576 | tf_op jit(solution)/shard_map/normed_rows/pallas_call | solution.py:209
  55.6 18.8 %all-to-all-done.1.refs_2_ = bf16[32,256,128]{2,1,0:T(8,128)(2,1)S(1)} async-done(((bf16[32,256,128]{2,1,0:T(8,128)(2,1)}), bf16[32,256,128]{2,1,0:T(8,128)(2,1)S(1)}, u32[]{:S(2)}, u32[]{:S(2)}) %all-to-all-start.1) | async-done | bytes 2097184 | tf_op jit(solution)/shard_map/all_to_all | solution.py:682
  75.8 6.7 %all-to-all-start.2 = ((bf16[32,256,128]{2,1,0:T(8,128)(2,1)}), bf16[32,256,128]{2,1,0:T(8,128)(2,1)}, u32[]{:S(2)}, u32[]{:S(2)}) async-start(bf16[32,256,128]{2,1,0:T(8,128)(2,1)} %get-tuple-element.80), calls=%async_computation.2 | async-start | bytes 4194304 | tf_op jit(solution)/shard_map/all_to_all | solution.py:682
  82.6 5.9 %target_terms.1 = (bf16[2048,512]{1,0:T(8,128)(2,1)}, bf16[2048,128]{1,0:T(8,128)(2,1)}, bf16[2048,128]{1,0:T(8,128)(2,1)}) custom-call(bf16[2048,512]{1,0:T(8,128)(2,1)} %refs_2_.2, f32[1,512]{1,0:T(1,128)} %bitcast.33, bf16[512,128]{1,0:T(8,128)(2,1)} %wq_ref.1, bf16[128,512]{1,0:T(8,128)(2,1)} %wo_ref.1, bf16[4,2048,128]{2,1,0:T(8,128)(2,1)} %bitcast.29), custom_call_target="tpu_custom_call" | custom-call | flops 6899999744 | bytes 1048576 | tf_op jit(solution)/shard_map/target_terms/pallas_call | solution.py:241
  88.5 17.7 %attention.2 = (bf16[4096,128]{1,0:T(8,128)(2,1)}, bf16[32,256,128]{2,1,0:T(8,128)(2,1)}, f32[4,128,128]{2,1,0:T(8,128)}, bf16[2048,128]{1,0:T(8,128)(2,1)}) custom-call(s32[4,8]{1,0:T(4,128)} %refs_0_.3, bf16[4096,256]{1,0:T(8,128)(2,1)} %source_terms.1.refs_1_, bf16[32,256,128]{2,1,0:T(8,128)(2,1)} %copy-done.2, ...), custom_call_target="tpu_custom_call" | custom-call | flops 20700000256 | bytes 1048576 | tf_op jit(solution)/shard_map/attention/pallas_call | solution.py:404
  106.2 4.2 %all-to-all-done.2.refs_2_ = bf16[32,256,128]{2,1,0:T(8,128)(2,1)} async-done(((bf16[32,256,128]{2,1,0:T(8,128)(2,1)}), bf16[32,256,128]{2,1,0:T(8,128)(2,1)}, u32[]{:S(2)}, u32[]{:S(2)}) %all-to-all-start.2) | async-done | bytes 2097184 | tf_op jit(solution)/shard_map/all_to_all | solution.py:682
  110.5 6.1 %all-to-all-start.3 = ((bf16[32,256,128]{2,1,0:T(8,128)(2,1)}), bf16[32,256,128]{2,1,0:T(8,128)(2,1)S(1)}, u32[]{:S(2)}, u32[]{:S(2)}) async-start(bf16[32,256,128]{2,1,0:T(8,128)(2,1)} %get-tuple-element.84), calls=%async_computation.3 | async-start | bytes 4194304 | tf_op jit(solution)/shard_map/all_to_all | solution.py:682
  116.8 17.9 %attention.3 = (bf16[4096,128]{1,0:T(8,128)(2,1)}, bf16[32,256,128]{2,1,0:T(8,128)(2,1)}, f32[4,128,128]{2,1,0:T(8,128)}, bf16[2048,128]{1,0:T(8,128)(2,1)}) custom-call(s32[4,8]{1,0:T(4,128)} %refs_0_.3, bf16[4096,256]{1,0:T(8,128)(2,1)} %source_terms.1.refs_1_, bf16[32,256,128]{2,1,0:T(8,128)(2,1)} %all-to-all-done.2.refs_2_, ...), custom_call_target="tpu_custom_call" | custom-call | flops 20700000256 | bytes 1048576 | tf_op jit(solution)/shard_map/attention/pallas_call | solution.py:404
  134.7 9.8 %all-to-all-done.3.refs_3_ = bf16[32,256,128]{2,1,0:T(8,128)(2,1)S(1)} async-done(((bf16[32,256,128]{2,1,0:T(8,128)(2,1)}), bf16[32,256,128]{2,1,0:T(8,128)(2,1)S(1)}, u32[]{:S(2)}, u32[]{:S(2)}) %all-to-all-start.3) | async-done | bytes 2097184 | tf_op jit(solution)/shard_map/all_to_all | solution.py:682
  144.5 1.4 copy-done.3
  145.9 6.0 %all-to-all-start.4 = ((bf16[32,256,128]{2,1,0:T(8,128)(2,1)}), bf16[32,256,128]{2,1,0:T(8,128)(2,1)S(1)}, u32[]{:S(2)}, u32[]{:S(2)}) async-start(bf16[32,256,128]{2,1,0:T(8,128)(2,1)} %get-tuple-element.86), calls=%async_computation.4 | async-start | bytes 4194304 | tf_op jit(solution)/shard_map/all_to_all | solution.py:682
  152.0 10.4 %scatter_rows.2 = (f32[4,128,128]{2,1,0:T(8,128)}, bf16[1024,128]{1,0:T(8,128)(2,1)}, bf16[1024,128]{1,0:T(8,128)(2,1)}, bf16[1024,128]{1,0:T(8,128)(2,1)}, bf16[1024,128]{1,0:T(8,128)(2,1)}) custom-call(s32[1]{0:T(128)} %bitcast.15.refs_0_, s32[32,2,128]{2,1,0:T(2,128)} %copy-done.9, bf16[4096,128]{1,0:T(8,128)(2,1)} %get-tuple-element.87.refs_2_, ...), custom_call_target="tpu_custom_call" | custom-call | flops 12650000384 | bytes 1048576 | tf_op jit(solution)/shard_map/scatter_rows/pallas_call | solution.py:510
  163.7 2.5 collective-permute-start.1
  167.3 9.4 %collective-permute-done.refs_6_ = bf16[1024,128]{1,0:T(8,128)(2,1)S(1)} collective-permute-done((bf16[1024,128]{1,0:T(8,128)(2,1)}, bf16[1024,128]{1,0:T(8,128)(2,1)S(1)}, u32[]{:S(2)}, u32[]{:S(2)}) %collective-permute-start) | collective-permute-done | bytes 262176 | tf_op jit(solution)/shard_map/ppermute | solution.py:688
  176.8 5.9 %collective-permute-done.1.refs_8_ = bf16[1024,128]{1,0:T(8,128)(2,1)S(1)} collective-permute-done((bf16[1024,128]{1,0:T(8,128)(2,1)}, bf16[1024,128]{1,0:T(8,128)(2,1)S(1)}, u32[]{:S(2)}, u32[]{:S(2)}) %collective-permute-start.1) | collective-permute-done | bytes 262176 | tf_op jit(solution)/shard_map/ppermute | solution.py:688
  182.7 1.5 copy-done.1
  184.2 10.9 %scatter_rows.3 = (f32[32,64,128]{2,1,0:T(8,128)}, bf16[1024,128]{1,0:T(8,128)(2,1)}, bf16[1024,128]{1,0:T(8,128)(2,1)}, bf16[1024,128]{1,0:T(8,128)(2,1)}, bf16[1024,128]{1,0:T(8,128)(2,1)}) custom-call(s32[1]{0:T(128)} %bitcast.15.refs_0_, s32[32,2,128]{2,1,0:T(2,128)} %copy-done.9, bf16[4096,128]{1,0:T(8,128)(2,1)} %get-tuple-element.101.refs_2_, ...), custom_call_target="tpu_custom_call" | custom-call | flops 12650000384 | bytes 1048576 | tf_op jit(solution)/shard_map/scatter_rows/pallas_call | solution.py:510
  196.3 2.0 collective-permute-start.5
  198.3 7.3 %all-to-all-start.5 = ((f32[32,64,128]{2,1,0:T(8,128)}), f32[32,64,128]{2,1,0:T(8,128)S(1)}, u32[]{:S(2)}, u32[]{:S(2)}) async-start(f32[32,64,128]{2,1,0:T(8,128)} %get-tuple-element.107), calls=%async_computation.5 | async-start | bytes 2097152 | tf_op jit(solution)/shard_map/all_to_all | solution.py:682
  205.6 10.8 %mesh_rows.1 = (bf16[2048,128]{1,0:T(8,128)(2,1)}, bf16[2048,128]{1,0:T(8,128)(2,1)}) custom-call(s32[1]{0:T(128)} %bitcast.15.refs_0_, bf16[4,2,2,128,512]{4,3,2,1,0:T(8,128)(2,1)} %bitcast.26, bf16[2048,512]{1,0:T(8,128)(2,1)} %refs_2_.2, bf16[2048,128]{1,0:T(8,128)(2,1)} %refs_3_.1, f32[1,512]{1,0:T(1,128)} %bitcast.34, bf16[4,2048,128]{2,1,0:T(8,128)(2,1)} %bitcast.28, ...), custom_call_target="tpu_custom_call" | custom-call | flops 12650000384 | bytes 1048576 | tf_op jit(solution)/shard_map/mesh_rows/pallas_call | solution.py:636
  216.4 6.4 %all-to-all-done.5 = f32[32,64,128]{2,1,0:T(8,128)S(1)} async-done(((f32[32,64,128]{2,1,0:T(8,128)}), f32[32,64,128]{2,1,0:T(8,128)S(1)}, u32[]{:S(2)}, u32[]{:S(2)}) %all-to-all-start.5) | async-done | bytes 1048608 | tf_op jit(solution)/shard_map/all_to_all | solution.py:682
  224.1 4.0 %all-to-all-start.6 = ((f32[32,64,128]{2,1,0:T(8,128)}), f32[32,64,128]{2,1,0:T(8,128)S(1)}, u32[]{:S(2)}, u32[]{:S(2)}) async-start(f32[32,64,128]{2,1,0:T(8,128)} %broadcast_in_dim.5), calls=%async_computation.6 | async-start | bytes 2097152 | tf_op jit(solution)/shard_map/all_to_all | solution.py:682
  228.1 5.9 %grid_rows.1 = (bf16[1024,128]{1,0:T(8,128)(2,1)}, bf16[1024,128]{1,0:T(8,128)(2,1)}, bf16[1024,128]{1,0:T(8,128)(2,1)}, bf16[1024,128]{1,0:T(8,128)(2,1)}) custom-call(s32[1]{0:T(128)} %bitcast.15.refs_0_, bf16[4,2,2,128,512]{4,3,2,1,0:T(8,128)(2,1)} %bitcast.27, bf16[4096,512]{1,0:T(8,128)(2,1)} %refs_2_.3, f32[1,512]{1,0:T(1,128)} %bitcast.37, ...), custom_call_target="tpu_custom_call" | custom-call | flops 6899999744 | bytes 1048576 | tf_op jit(solution)/shard_map/grid_rows/pallas_call | solution.py:588
  234.2 1.9 collective-permute-start.7
  236.0 2.0 collective-permute-start.8
  238.0 5.4 %collective-permute-done.6.refs_2_ = bf16[1024,128]{1,0:T(8,128)(2,1)S(1)} collective-permute-done((bf16[1024,128]{1,0:T(8,128)(2,1)}, bf16[1024,128]{1,0:T(8,128)(2,1)S(1)}, u32[]{:S(2)}, u32[]{:S(2)}) %collective-permute-start.6) | collective-permute-done | bytes 262176 | tf_op jit(solution)/shard_map/ppermute | solution.py:688
  243.4 4.6 %collective-permute-done.7.refs_3_ = bf16[1024,128]{1,0:T(8,128)(2,1)S(1)} collective-permute-done((bf16[1024,128]{1,0:T(8,128)(2,1)}, bf16[1024,128]{1,0:T(8,128)(2,1)S(1)}, u32[]{:S(2)}, u32[]{:S(2)}) %collective-permute-start.7) | collective-permute-done | bytes 262176 | tf_op jit(solution)/shard_map/ppermute | solution.py:688
  251.1 1.4 finish.1
  (70 shorter events, 14.8 us)
Async XLA Ops:
  7.2 75.4 %all-gather.9.cloned.1.call-start = ((), (), s32[]{:S(2)}) async-start(), calls=%async_computation.7 | async-start | bytes 2621440 | tf_op jit(solution)/shard_map/all_gather | solution.py:732
  9.6 16.9 %all-to-all-start = ((s32[32,2,128]{2,1,0:T(2,128)}), s32[32,2,128]{2,1,0:T(2,128)S(1)}, u32[]{:S(2)}, u32[]{:S(2)}) async-start(s32[32,2,128]{2,1,0:T(2,128)} %broadcast_in_dim.4), calls=%async_computation | async-start | bytes 65536 | tf_op jit(solution)/shard_map/all_to_all | solution.py:682
  19.2 6.6 %copy-start.8 = (s32[1,32,256]{2,1,0:T(8,128)S(1)}, s32[1,32,256]{2,1,0:T(8,128)}, u32[]{:S(2)}) copy-start(s32[1,32,256]{2,1,0:T(8,128)} %param.14) | copy-start | bytes 98308
  40.7 5.9 %copy-start.4 = (bf16[512,128]{1,0:T(8,128)(2,1)S(1)}, bf16[512,128]{1,0:T(8,128)(2,1)}, u32[]{:S(2)}) copy-start(bf16[512,128]{1,0:T(8,128)(2,1)} %key_ref.1) | copy-start | bytes 393220
  40.7 6.0 %copy-start.5 = (bf16[512,128]{1,0:T(8,128)(2,1)S(1)}, bf16[512,128]{1,0:T(8,128)(2,1)}, u32[]{:S(2)}) copy-start(bf16[512,128]{1,0:T(8,128)(2,1)} %value_ref.1) | copy-start | bytes 393220
  40.7 6.1 %copy-start.6 = (bf16[512,128]{1,0:T(8,128)(2,1)S(1)}, bf16[512,128]{1,0:T(8,128)(2,1)}, u32[]{:S(2)}) copy-start(bf16[512,128]{1,0:T(8,128)(2,1)} %wq_ref.1) | copy-start | bytes 393220
  40.7 6.3 %copy-start.7 = (bf16[128,512]{1,0:T(8,128)(2,1)S(1)}, bf16[128,512]{1,0:T(8,128)(2,1)}, u32[]{:S(2)}) copy-start(bf16[128,512]{1,0:T(8,128)(2,1)} %wo_ref.1) | copy-start | bytes 393220
  40.7 33.7 %all-to-all-start.1 = ((bf16[32,256,128]{2,1,0:T(8,128)(2,1)}), bf16[32,256,128]{2,1,0:T(8,128)(2,1)S(1)}, u32[]{:S(2)}, u32[]{:S(2)}) async-start(bf16[32,256,128]{2,1,0:T(8,128)(2,1)} %get-tuple-element.75), calls=%async_computation.1 | async-start | bytes 4194304 | tf_op jit(solution)/shard_map/all_to_all | solution.py:682
  46.5 59.7 %all-gather.11.cloned.1.call-start = ((), (), s32[]{:S(2)}) async-start(), calls=%async_computation.8 | async-start | bytes 2621440 | tf_op jit(solution)/shard_map/all_gather | solution.py:734
  75.8 34.7 %all-to-all-start.2 = ((bf16[32,256,128]{2,1,0:T(8,128)(2,1)}), bf16[32,256,128]{2,1,0:T(8,128)(2,1)}, u32[]{:S(2)}, u32[]{:S(2)}) async-start(bf16[32,256,128]{2,1,0:T(8,128)(2,1)} %get-tuple-element.80), calls=%async_computation.2 | async-start | bytes 4194304 | tf_op jit(solution)/shard_map/all_to_all | solution.py:682
  82.5 62.0 %all-gather.13.cloned.1.call-start = ((), (), s32[]{:S(2)}) async-start(), calls=%async_computation.9 | async-start | bytes 2621440 | tf_op jit(solution)/shard_map/all_gather | solution.py:755
  110.5 34.0 %all-to-all-start.3 = ((bf16[32,256,128]{2,1,0:T(8,128)(2,1)}), bf16[32,256,128]{2,1,0:T(8,128)(2,1)S(1)}, u32[]{:S(2)}, u32[]{:S(2)}) async-start(bf16[32,256,128]{2,1,0:T(8,128)(2,1)} %get-tuple-element.84), calls=%async_computation.3 | async-start | bytes 4194304 | tf_op jit(solution)/shard_map/all_to_all | solution.py:682
  116.5 66.1 %all-gather.15.cloned.1.call-start = ((), (), s32[]{:S(2)}) async-start(), calls=%async_computation.10 | async-start | bytes 2621440 | tf_op jit(solution)/shard_map/all_gather | solution.py:755
  145.9 36.8 %all-to-all-start.4 = ((bf16[32,256,128]{2,1,0:T(8,128)(2,1)}), bf16[32,256,128]{2,1,0:T(8,128)(2,1)S(1)}, u32[]{:S(2)}, u32[]{:S(2)}) async-start(bf16[32,256,128]{2,1,0:T(8,128)(2,1)} %get-tuple-element.86), calls=%async_computation.4 | async-start | bytes 4194304 | tf_op jit(solution)/shard_map/all_to_all | solution.py:682
  162.4 14.3 %collective-permute-start = (bf16[1024,128]{1,0:T(8,128)(2,1)}, bf16[1024,128]{1,0:T(8,128)(2,1)S(1)}, u32[]{:S(2)}, u32[]{:S(2)}) collective-permute-start(bf16[1024,128]{1,0:T(8,128)(2,1)} %get-tuple-element.91), channel_id=1, source_target_pairs={{0,1},{1,2},{2,3},{3,0},{4,5},{5,6},{6,7},{7,4},{8,9},{9,10},{10,1... | collective-permute-start | bytes 786440 | tf_op jit(solution)/shard_map/ppermute | solution.py:688
  163.7 18.9 %collective-permute-start.1 = (bf16[1024,128]{1,0:T(8,128)(2,1)}, bf16[1024,128]{1,0:T(8,128)(2,1)S(1)}, u32[]{:S(2)}, u32[]{:S(2)}) collective-permute-start(bf16[1024,128]{1,0:T(8,128)(2,1)} %get-tuple-element.92), channel_id=1, source_target_pairs={{0,2},{1,3},{2,0},{3,1},{4,6},{5,7},{6,4},{7,5},{8,10},{9,11},{10,... | collective-permute-start | bytes 786440 | tf_op jit(solution)/shard_map/ppermute | solution.py:688
  166.2 16.5 %collective-permute-start.2 = (bf16[1024,128]{1,0:T(8,128)(2,1)}, bf16[1024,128]{1,0:T(8,128)(2,1)S(1)}, u32[]{:S(2)}, u32[]{:S(2)}) collective-permute-start(bf16[1024,128]{1,0:T(8,128)(2,1)} %get-tuple-element.93), channel_id=1, source_target_pairs={{0,3},{1,0},{2,1},{3,2},{4,7},{5,4},{6,5},{7,6},{8,11},{9,8},{10,9... | collective-permute-start | bytes 786440 | tf_op jit(solution)/shard_map/ppermute | solution.py:688
  176.7 18.3 %copy-start.10 = (bf16[1024,128]{1,0:T(8,128)(2,1)}, bf16[1024,128]{1,0:T(8,128)(2,1)S(1)}, u32[]{:S(2)}) copy-start(bf16[1024,128]{1,0:T(8,128)(2,1)S(1)} %collective-permute-done.refs_6_) | copy-start | bytes 786436
  182.6 12.4 %copy-start.11 = (bf16[1024,128]{1,0:T(8,128)(2,1)}, bf16[1024,128]{1,0:T(8,128)(2,1)S(1)}, u32[]{:S(2)}) copy-start(bf16[1024,128]{1,0:T(8,128)(2,1)S(1)} %collective-permute-done.1.refs_8_) | copy-start | bytes 786436
  182.7 12.4 %copy-start.12 = (bf16[1024,128]{1,0:T(8,128)(2,1)}, bf16[1024,128]{1,0:T(8,128)(2,1)S(1)}, u32[]{:S(2)}) copy-start(bf16[1024,128]{1,0:T(8,128)(2,1)S(1)} %collective-permute-done.2.refs_10_) | copy-start | bytes 786436
  182.7 1.5 copy-start.1
  195.1 27.7 %collective-permute-start.3 = (bf16[1024,128]{1,0:T(8,128)(2,1)}, bf16[1024,128]{1,0:T(8,128)(2,1)S(1)}, u32[]{:S(2)}, u32[]{:S(2)}) collective-permute-start(bf16[1024,128]{1,0:T(8,128)(2,1)} %get-tuple-element.113), channel_id=1, source_target_pairs={{0,1},{1,2},{2,3},{3,0},{4,5},{5,6},{6,7},{7,4},{8,9},{9,10},{10,1... | collective-permute-start | bytes 786440 | tf_op jit(solution)/shard_map/ppermute | solution.py:688
  195.2 27.7 %collective-permute-start.4 = (bf16[1024,128]{1,0:T(8,128)(2,1)}, bf16[1024,128]{1,0:T(8,128)(2,1)S(1)}, u32[]{:S(2)}, u32[]{:S(2)}) collective-permute-start(bf16[1024,128]{1,0:T(8,128)(2,1)} %get-tuple-element.114), channel_id=1, source_target_pairs={{0,2},{1,3},{2,0},{3,1},{4,6},{5,7},{6,4},{7,5},{8,10},{9,11},{10,... | collective-permute-start | bytes 786440 | tf_op jit(solution)/shard_map/ppermute | solution.py:688
  196.3 26.5 %collective-permute-start.5 = (bf16[1024,128]{1,0:T(8,128)(2,1)}, bf16[1024,128]{1,0:T(8,128)(2,1)S(1)}, u32[]{:S(2)}, u32[]{:S(2)}) collective-permute-start(bf16[1024,128]{1,0:T(8,128)(2,1)} %get-tuple-element.115), channel_id=1, source_target_pairs={{0,3},{1,0},{2,1},{3,2},{4,7},{5,4},{6,5},{7,6},{8,11},{9,8},{10,9... | collective-permute-start | bytes 786440 | tf_op jit(solution)/shard_map/ppermute | solution.py:688
  198.3 24.4 %all-to-all-start.5 = ((f32[32,64,128]{2,1,0:T(8,128)}), f32[32,64,128]{2,1,0:T(8,128)S(1)}, u32[]{:S(2)}, u32[]{:S(2)}) async-start(f32[32,64,128]{2,1,0:T(8,128)} %get-tuple-element.107), calls=%async_computation.5 | async-start | bytes 2097152 | tf_op jit(solution)/shard_map/all_to_all | solution.py:682
  222.8 5.3 %copy-start.13 = (bf16[1024,128]{1,0:T(8,128)(2,1)}, bf16[1024,128]{1,0:T(8,128)(2,1)S(1)}, u32[]{:S(2)}) copy-start(bf16[1024,128]{1,0:T(8,128)(2,1)S(1)} %collective-permute-done.3.refs_7_) | copy-start | bytes 786436
  222.9 5.2 %copy-start.14 = (bf16[1024,128]{1,0:T(8,128)(2,1)}, bf16[1024,128]{1,0:T(8,128)(2,1)S(1)}, u32[]{:S(2)}) copy-start(bf16[1024,128]{1,0:T(8,128)(2,1)S(1)} %collective-permute-done.4.refs_9_) | copy-start | bytes 786436
  222.9 5.2 %copy-start.15 = (bf16[1024,128]{1,0:T(8,128)(2,1)}, bf16[1024,128]{1,0:T(8,128)(2,1)S(1)}, u32[]{:S(2)}) copy-start(bf16[1024,128]{1,0:T(8,128)(2,1)S(1)} %collective-permute-done.5.refs_11_) | copy-start | bytes 786436
  224.1 27.0 %all-to-all-start.6 = ((f32[32,64,128]{2,1,0:T(8,128)}), f32[32,64,128]{2,1,0:T(8,128)S(1)}, u32[]{:S(2)}, u32[]{:S(2)}) async-start(f32[32,64,128]{2,1,0:T(8,128)} %broadcast_in_dim.5), calls=%async_computation.6 | async-start | bytes 2097152 | tf_op jit(solution)/shard_map/all_to_all | solution.py:682
  234.1 9.3 %collective-permute-start.6 = (bf16[1024,128]{1,0:T(8,128)(2,1)}, bf16[1024,128]{1,0:T(8,128)(2,1)S(1)}, u32[]{:S(2)}, u32[]{:S(2)}) collective-permute-start(bf16[1024,128]{1,0:T(8,128)(2,1)} %get-tuple-element.131), channel_id=1, source_target_pairs={{0,1},{1,2},{2,3},{3,0},{4,5},{5,6},{6,7},{7,4},{8,9},{9,10},{10,1... | collective-permute-start | bytes 786440 | tf_op jit(solution)/shard_map/ppermute | solution.py:688
  234.2 13.8 %collective-permute-start.7 = (bf16[1024,128]{1,0:T(8,128)(2,1)}, bf16[1024,128]{1,0:T(8,128)(2,1)S(1)}, u32[]{:S(2)}, u32[]{:S(2)}) collective-permute-start(bf16[1024,128]{1,0:T(8,128)(2,1)} %get-tuple-element.132), channel_id=1, source_target_pairs={{0,2},{1,3},{2,0},{3,1},{4,6},{5,7},{6,4},{7,5},{8,10},{9,11},{10,... | collective-permute-start | bytes 786440 | tf_op jit(solution)/shard_map/ppermute | solution.py:688
  236.0 13.0 %collective-permute-start.8 = (bf16[1024,128]{1,0:T(8,128)(2,1)}, bf16[1024,128]{1,0:T(8,128)(2,1)S(1)}, u32[]{:S(2)}, u32[]{:S(2)}) collective-permute-start(bf16[1024,128]{1,0:T(8,128)(2,1)} %get-tuple-element.133), channel_id=1, source_target_pairs={{0,3},{1,0},{2,1},{3,2},{4,7},{5,4},{6,5},{7,6},{8,11},{9,8},{10,9... | collective-permute-start | bytes 786440 | tf_op jit(solution)/shard_map/ppermute | solution.py:688
  (4 other events, 4.4 us)
Sparse Core Ops, SparseCore 0:
  9.7 34.0 all-gather.8
  49.6 31.7 all-gather.10
  106.3 31.8 all-gather.12
  140.4 35.1 all-gather.14

commit v4 on v3

--- a/solution.py
+++ b/solution.py
@@ -110,7 +110,7 @@
 
 def list_tiles(need_ref, list_ref):
     def add(t, count):
-        used = need_ref[t // 2, t % 2, 0] > 0
+        used = need_ref[t] > 0
 
         @pl.when(used)
         def _():
@@ -178,7 +178,7 @@
 def gather_rows(need, rows, pairs):
     count, wide = pairs.shape
     heads = wide // PAIR
-    peers = need.shape[0]
+    peers = need.shape[0] // 2
     return pl.pallas_call(
         gather_kernel,
         in_specs=[SMEM, VMEM, ANY],
@@ -188,7 +188,7 @@
             pltpu.VMEM((2, count // 2, wide), jnp.bfloat16),
             pltpu.VMEM((QUAD * TS, count // 2), jnp.bfloat16),
             pltpu.VMEM((2, heads, QUAD * TS, PAIR), jnp.bfloat16),
-            pltpu.SMEM((2 * need.shape[0],), jnp.int32),
+            pltpu.SMEM((need.shape[0],), jnp.int32),
             pltpu.SemaphoreType.DMA((2, QUAD, heads)),
             pltpu.SemaphoreType.DMA,
         ],
@@ -517,7 +517,7 @@
             pltpu.VMEM((table_rows, PAIR), jnp.float32),
             pltpu.VMEM(normed.shape, jnp.bfloat16),
             pltpu.VMEM(grad, jnp.float32),
-            pltpu.SMEM((2 * need.shape[0],), jnp.int32),
+            pltpu.SMEM((need.shape[0],), jnp.int32),
             pltpu.SemaphoreType.DMA,
         ],
         compiler_params=room(60),
@@ -728,6 +728,7 @@
     wanted = own_tiles + jnp.arange(2 * peers, dtype=jnp.int32)
     need = jnp.any(tile_src.reshape(-1, 1) == wanted[None, :], axis=0).astype(jnp.int32)
     need = over_graph(jnp.broadcast_to(need.reshape(peers, 2, 1), (peers, 2, TS)))
+    need = need[:, :, 0].reshape(-1)
 
     cot = lax.all_gather(d_out, "feat", axis=0)
     back_weights = jnp.stack([by_head(w_key.T, w_value.T), by_head(w_query.T, w_out)])
@@ -786,13 +787,12 @@
 
     mixed, payload = after(mixed, weight_grads[-1])
     mesh_out, grad_mesh = mesh_rows(where, back_weights, mesh_feat, d_out, gain_dst, mixed)
-    share = jnp.sum(over_graph(payload), axis=0)
-    share, (sums, mesh_out, grad_mesh) = after(share, (sums, mesh_out, grad_mesh))
-    shares = over_graph(jnp.broadcast_to(share[None], payload.shape))
     sum_rows = [[sums[h][s] for h in range(heads)] for s in range(groups)]
     grid_parts = grid_rows(where, back_weights, grid_feat, gain_src, sum_rows)
+    share = jnp.sum(over_graph(payload), axis=0)
+    share, (grid_parts, mesh_out, grad_mesh) = after(share, (grid_parts, mesh_out, grad_mesh))
+    shares = over_graph(jnp.broadcast_to(share[None], payload.shape))
     grad_grid = place_rows(where, over_feat(grid_parts))
-    shares, _ = after(shares, grid_parts)
     grad_wq, grad_wk, grad_wv, grad_wo = finish(shares, width, columns)
     return (mesh_out, grad_grid, grad_mesh, grad_wq, grad_wk, grad_wv, grad_wo)
 

time: 260 us -> 258 us (level)
  Pallas kernels: 110 us -> 99.3 us
  starting transfers between devices: 57.9 us -> 66.9 us
  waiting for transfers between devices: 66.4 us -> 63.5 us
    all_to_all x7, starting transfers between devices: 45.5 us -> 54.5 us  [over_graph(): lax.all_to_all(values, 'graph', split_axis=0, concat_axis=0, tiled=True)]
    pallas_call x2, Pallas kernels: 21.3 us -> 15.4 us  [scatter_rows(): pl.pallas_call(lambda *refs: scatter_kernel(len(earlier), *refs), in_spec...]
    all_to_all x7, waiting for transfers between devices: 39.3 us -> 34.1 us  [over_graph(): lax.all_to_all(values, 'graph', split_axis=0, concat_axis=0, tiled=True)]
    pallas_call x1, Pallas kernels: 13.6 us -> 8.91 us  [gather_rows(): pl.pallas_call(gather_kernel, in_specs=[SMEM, VMEM, ANY], out_specs=[ANY]...]
    unnamed x35 -> x39, local copies, waits for them, and re-layouts: 6.22 us -> 5.48 us
  transfers between devices with their start and end apart: 20 -> 20, of which waited for: 9 -> 8; matrix products, arithmetic and copies ran while one was open for 1% -> 1% of each run, Pallas kernels for 38% -> 35%
where the time goes in v4:
time: 258 us; the launch traced here: 255 us
  Pallas kernels  99.3 us (38%)
  starting transfers between devices  66.9 us (26%)
  waiting for transfers between devices  63.5 us (25%)
  between operations  14.2 us (6%)
  local copies, waits for them, and re-layouts  10 us (4%)
    all_to_all x7, starting transfers between devices, over_graph(): lax.all_to_all(values, 'graph', split_axis=0, concat_axis=0, tiled=True)  54.5 us
    pallas_call x2, Pallas kernels, attention(): pl.pallas_call(lambda *refs: attention_kernel(head, *refs), grid=(blocks,...  35.6 us
    all_to_all x7, waiting for transfers between devices, over_graph(): lax.all_to_all(values, 'graph', split_axis=0, concat_axis=0, tiled=True)  34.1 us
    ppermute x9, waiting for transfers between devices, over_feat(): lax.ppermute(parts[s], 'feat', [(i, (i + s) % groups) for i in range(grou...  28.6 us
    pallas_call x2, Pallas kernels, scatter_rows(): pl.pallas_call(lambda *refs: scatter_kernel(len(earlier), *refs), in_spec...  15.4 us
    ppermute x9, starting transfers between devices, over_feat(): lax.ppermute(parts[s], 'feat', [(i, (i + s) % groups) for i in range(grou...  12.1 us
    pallas_call x1, Pallas kernels, mesh_rows(): pl.pallas_call(lambda *refs: mesh_kernel(heads, *refs), grid_spec=pltpu.P...  10.8 us
    pallas_call x1, Pallas kernels, gather_rows(): pl.pallas_call(gather_kernel, in_specs=[SMEM, VMEM, ANY], out_specs=[ANY]...  8.91 us
  transfers between devices with their start and end apart: 20, of which 8 were waited for; matrix products, arithmetic and copies ran while one was open for 1% of the time, Pallas kernels for 35%

profile of v4, /device:TPU:1, one launch (start us, length us, event | category | flops | bytes accessed | tf_op | source)
XLA Modules:
  0.0 255.0 jit_solution(14226896915335921403)
XLA Ops:
  8.9 9.6 %all-to-all-start = ((s32[32,2,128]{2,1,0:T(2,128)}), s32[32,2,128]{2,1,0:T(2,128)S(1)}, u32[]{:S(2)}, u32[]{:S(2)}) async-start(s32[32,2,128]{2,1,0:T(2,128)} %broadcast_in_dim.4), calls=%async_computation | async-start | bytes 65536 | tf_op jit(solution)/shard_map/all_to_all | solution.py:682
  19.2 6.6 %source_terms.1.refs_1_ = bf16[4096,256]{1,0:T(8,128)(2,1)} custom-call(bf16[4096,512]{1,0:T(8,128)(2,1)} %refs_2_.2, f32[1,512]{1,0:T(1,128)} %bitcast.35, bf16[512,128]{1,0:T(8,128)(2,1)} %key_ref.1, bf16[512,128]{1,0:T(8,128)(2,1)} %value_ref.1), custom_call_target="tpu_custom_call" | custom-call | flops 9200000000 | bytes 1048576 | tf_op jit(solution)/shard_map/source_terms/pallas_call | solution.py:94
  27.7 8.9 %gather_rows.1 = (bf16[32,256,128]{2,1,0:T(8,128)(2,1)}, bf16[32,256,128]{2,1,0:T(8,128)(2,1)}) custom-call(s32[64]{0:T(128)} %reshape_squeeze.3.need_ref.refs_1_, s32[64,1,128]{2,1,0:T(1,128)} %reshape.57.rows_ref.refs_4_, bf16[2,2048,256]{2,1,0:T(8,128)(2,1)} %bitcast.38), custom_call_target="tpu_custom_call" | custom-call | flops 11500000256 | bytes 1048576 | tf_op jit(solution)/shard_map/gather_rows/pallas_call | solution.py:182
  36.7 8.9 %all-to-all-start.1 = ((bf16[32,256,128]{2,1,0:T(8,128)(2,1)}), bf16[32,256,128]{2,1,0:T(8,128)(2,1)S(1)}, u32[]{:S(2)}, u32[]{:S(2)}) async-start(bf16[32,256,128]{2,1,0:T(8,128)(2,1)} %get-tuple-element.70), calls=%async_computation.1 | async-start | bytes 4194304 | tf_op jit(solution)/shard_map/all_to_all | solution.py:682
  47.0 7.7 %normed_rows.1.refs_5_ = bf16[4096,512]{1,0:T(8,128)(2,1)} custom-call(bf16[4096,512]{1,0:T(8,128)(2,1)} %refs_2_.2, f32[1,512]{1,0:T(1,128)} %bitcast.36), custom_call_target="tpu_custom_call" | custom-call | flops 9200000000 | bytes 1048576 | tf_op jit(solution)/shard_map/normed_rows/pallas_call | solution.py:209
  54.7 18.8 %all-to-all-done.1.refs_2_ = bf16[32,256,128]{2,1,0:T(8,128)(2,1)S(1)} async-done(((bf16[32,256,128]{2,1,0:T(8,128)(2,1)}), bf16[32,256,128]{2,1,0:T(8,128)(2,1)S(1)}, u32[]{:S(2)}, u32[]{:S(2)}) %all-to-all-start.1) | async-done | bytes 2097184 | tf_op jit(solution)/shard_map/all_to_all | solution.py:682
  73.5 1.4 copy-done.2
  74.9 6.7 %all-to-all-start.2 = ((bf16[32,256,128]{2,1,0:T(8,128)(2,1)}), bf16[32,256,128]{2,1,0:T(8,128)(2,1)}, u32[]{:S(2)}, u32[]{:S(2)}) async-start(bf16[32,256,128]{2,1,0:T(8,128)(2,1)} %get-tuple-element.75), calls=%async_computation.2 | async-start | bytes 4194304 | tf_op jit(solution)/shard_map/all_to_all | solution.py:682
  81.7 5.9 %target_terms.1 = (bf16[2048,512]{1,0:T(8,128)(2,1)}, bf16[2048,128]{1,0:T(8,128)(2,1)}, bf16[2048,128]{1,0:T(8,128)(2,1)}) custom-call(bf16[2048,512]{1,0:T(8,128)(2,1)} %refs_2_.3, f32[1,512]{1,0:T(1,128)} %bitcast.33, bf16[512,128]{1,0:T(8,128)(2,1)} %wq_ref.1, bf16[128,512]{1,0:T(8,128)(2,1)} %wo_ref.1, bf16[4,2048,128]{2,1,0:T(8,128)(2,1)} %bitcast.29), custom_call_target="tpu_custom_call" | custom-call | flops 6899999744 | bytes 1048576 | tf_op jit(solution)/shard_map/target_terms/pallas_call | solution.py:241
  87.6 17.7 %attention.2 = (bf16[4096,128]{1,0:T(8,128)(2,1)}, bf16[32,256,128]{2,1,0:T(8,128)(2,1)}, f32[4,128,128]{2,1,0:T(8,128)}, bf16[2048,128]{1,0:T(8,128)(2,1)}) custom-call(s32[4,8]{1,0:T(4,128)} %refs_0_.3, bf16[4096,256]{1,0:T(8,128)(2,1)} %source_terms.1.refs_1_, bf16[32,256,128]{2,1,0:T(8,128)(2,1)} %copy-done.2, ...), custom_call_target="tpu_custom_call" | custom-call | flops 20700000256 | bytes 1048576 | tf_op jit(solution)/shard_map/attention/pallas_call | solution.py:404
  105.4 4.2 %all-to-all-done.2.refs_2_ = bf16[32,256,128]{2,1,0:T(8,128)(2,1)} async-done(((bf16[32,256,128]{2,1,0:T(8,128)(2,1)}), bf16[32,256,128]{2,1,0:T(8,128)(2,1)}, u32[]{:S(2)}, u32[]{:S(2)}) %all-to-all-start.2) | async-done | bytes 2097184 | tf_op jit(solution)/shard_map/all_to_all | solution.py:682
  109.6 6.1 %all-to-all-start.3 = ((bf16[32,256,128]{2,1,0:T(8,128)(2,1)}), bf16[32,256,128]{2,1,0:T(8,128)(2,1)S(1)}, u32[]{:S(2)}, u32[]{:S(2)}) async-start(bf16[32,256,128]{2,1,0:T(8,128)(2,1)} %get-tuple-element.79), calls=%async_computation.3 | async-start | bytes 4194304 | tf_op jit(solution)/shard_map/all_to_all | solution.py:682
  115.9 17.9 %attention.3 = (bf16[4096,128]{1,0:T(8,128)(2,1)}, bf16[32,256,128]{2,1,0:T(8,128)(2,1)}, f32[4,128,128]{2,1,0:T(8,128)}, bf16[2048,128]{1,0:T(8,128)(2,1)}) custom-call(s32[4,8]{1,0:T(4,128)} %refs_0_.3, bf16[4096,256]{1,0:T(8,128)(2,1)} %source_terms.1.refs_1_, bf16[32,256,128]{2,1,0:T(8,128)(2,1)} %all-to-all-done.2.refs_2_, ...), custom_call_target="tpu_custom_call" | custom-call | flops 20700000256 | bytes 1048576 | tf_op jit(solution)/shard_map/attention/pallas_call | solution.py:404
  133.8 9.8 %all-to-all-done.3.refs_3_ = bf16[32,256,128]{2,1,0:T(8,128)(2,1)S(1)} async-done(((bf16[32,256,128]{2,1,0:T(8,128)(2,1)}), bf16[32,256,128]{2,1,0:T(8,128)(2,1)S(1)}, u32[]{:S(2)}, u32[]{:S(2)}) %all-to-all-start.3) | async-done | bytes 2097184 | tf_op jit(solution)/shard_map/all_to_all | solution.py:682
  143.6 1.4 copy-done.3
  145.0 6.0 %all-to-all-start.4 = ((bf16[32,256,128]{2,1,0:T(8,128)(2,1)}), bf16[32,256,128]{2,1,0:T(8,128)(2,1)S(1)}, u32[]{:S(2)}, u32[]{:S(2)}) async-start(bf16[32,256,128]{2,1,0:T(8,128)(2,1)} %get-tuple-element.81), calls=%async_computation.4 | async-start | bytes 4194304 | tf_op jit(solution)/shard_map/all_to_all | solution.py:682
  151.1 7.5 %scatter_rows.2 = (f32[4,128,128]{2,1,0:T(8,128)}, bf16[1024,128]{1,0:T(8,128)(2,1)}, bf16[1024,128]{1,0:T(8,128)(2,1)}, bf16[1024,128]{1,0:T(8,128)(2,1)}, bf16[1024,128]{1,0:T(8,128)(2,1)}) custom-call(s32[1]{0:T(128)} %bitcast.15.refs_0_, s32[64]{0:T(128)} %reshape_squeeze.3.need_ref.refs_1_, bf16[4096,128]{1,0:T(8,128)(2,1)} %get-tuple-element.82.refs_2_, ...), custom_call_target="tpu_custom_call" | custom-call | flops 12650000384 | bytes 1048576 | tf_op jit(solution)/shard_map/scatter_rows/pallas_call | solution.py:510
  159.9 2.5 collective-permute-start.1
  163.5 10.0 %collective-permute-done.refs_6_ = bf16[1024,128]{1,0:T(8,128)(2,1)S(1)} collective-permute-done((bf16[1024,128]{1,0:T(8,128)(2,1)}, bf16[1024,128]{1,0:T(8,128)(2,1)S(1)}, u32[]{:S(2)}, u32[]{:S(2)}) %collective-permute-start) | collective-permute-done | bytes 262176 | tf_op jit(solution)/shard_map/ppermute | solution.py:688
  173.5 7.7 %collective-permute-done.1.refs_8_ = bf16[1024,128]{1,0:T(8,128)(2,1)S(1)} collective-permute-done((bf16[1024,128]{1,0:T(8,128)(2,1)}, bf16[1024,128]{1,0:T(8,128)(2,1)S(1)}, u32[]{:S(2)}, u32[]{:S(2)}) %collective-permute-start.1) | collective-permute-done | bytes 262176 | tf_op jit(solution)/shard_map/ppermute | solution.py:688
  181.3 1.4 copy-done.1
  182.8 8.0 %scatter_rows.3 = (f32[32,64,128]{2,1,0:T(8,128)}, bf16[1024,128]{1,0:T(8,128)(2,1)}, bf16[1024,128]{1,0:T(8,128)(2,1)}, bf16[1024,128]{1,0:T(8,128)(2,1)}, bf16[1024,128]{1,0:T(8,128)(2,1)}) custom-call(s32[1]{0:T(128)} %bitcast.15.refs_0_, s32[64]{0:T(128)} %reshape_squeeze.3.need_ref.refs_1_, bf16[4096,128]{1,0:T(8,128)(2,1)} %get-tuple-element.96.refs_2_, ...), custom_call_target="tpu_custom_call" | custom-call | flops 12650000384 | bytes 1048576 | tf_op jit(solution)/shard_map/scatter_rows/pallas_call | solution.py:510
  190.8 1.4 collective-permute-start.4
  192.2 1.7 collective-permute-start.5
  193.9 9.7 %all-to-all-start.5 = ((f32[32,64,128]{2,1,0:T(8,128)}), f32[32,64,128]{2,1,0:T(8,128)S(1)}, u32[]{:S(2)}, u32[]{:S(2)}) async-start(f32[32,64,128]{2,1,0:T(8,128)} %get-tuple-element.102), calls=%async_computation.5 | async-start | bytes 2097152 | tf_op jit(solution)/shard_map/all_to_all | solution.py:682
  203.7 10.8 %mesh_rows.1 = (bf16[2048,128]{1,0:T(8,128)(2,1)}, bf16[2048,128]{1,0:T(8,128)(2,1)}) custom-call(s32[1]{0:T(128)} %bitcast.15.refs_0_, bf16[4,2,2,128,512]{4,3,2,1,0:T(8,128)(2,1)} %bitcast.26, bf16[2048,512]{1,0:T(8,128)(2,1)} %refs_2_.3, bf16[2048,128]{1,0:T(8,128)(2,1)} %refs_3_.1, f32[1,512]{1,0:T(1,128)} %bitcast.34, bf16[4,2048,128]{2,1,0:T(8,128)(2,1)} %bitcast.28, ...), custom_call_target="tpu_custom_call" | custom-call | flops 12650000384 | bytes 1048576 | tf_op jit(solution)/shard_map/mesh_rows/pallas_call | solution.py:636
  215.3 5.9 %grid_rows.1 = (bf16[1024,128]{1,0:T(8,128)(2,1)}, bf16[1024,128]{1,0:T(8,128)(2,1)}, bf16[1024,128]{1,0:T(8,128)(2,1)}, bf16[1024,128]{1,0:T(8,128)(2,1)}) custom-call(s32[1]{0:T(128)} %bitcast.15.refs_0_, bf16[4,2,2,128,512]{4,3,2,1,0:T(8,128)(2,1)} %bitcast.27, bf16[4096,512]{1,0:T(8,128)(2,1)} %refs_2_.2, f32[1,512]{1,0:T(1,128)} %bitcast.37, ...), custom_call_target="tpu_custom_call" | custom-call | flops 6899999744 | bytes 1048576 | tf_op jit(solution)/shard_map/grid_rows/pallas_call | solution.py:588
  222.5 7.4 %all-to-all-start.6 = ((f32[32,64,128]{2,1,0:T(8,128)}), f32[32,64,128]{2,1,0:T(8,128)S(1)}, u32[]{:S(2)}, u32[]{:S(2)}) async-start(f32[32,64,128]{2,1,0:T(8,128)} %broadcast_in_dim.5), calls=%async_computation.6 | async-start | bytes 2097152 | tf_op jit(solution)/shard_map/all_to_all | solution.py:682
  230.0 1.9 collective-permute-start.7
  232.0 2.0 collective-permute-start.8
  233.9 10.6 %collective-permute-done.6.refs_2_ = bf16[1024,128]{1,0:T(8,128)(2,1)S(1)} collective-permute-done((bf16[1024,128]{1,0:T(8,128)(2,1)S(1)}, bf16[1024,128]{1,0:T(8,128)(2,1)S(1)}, u32[]{:S(2)}, u32[]{:S(2)}) %collective-permute-start.6) | collective-permute-done | bytes 262176 | tf_op jit(solution)/shard_map/ppermute | solution.py:688
  247.1 1.4 finish.1
  (76 shorter events, 13.2 us)
Async XLA Ops:
  8.9 17.7 %all-to-all-start = ((s32[32,2,128]{2,1,0:T(2,128)}), s32[32,2,128]{2,1,0:T(2,128)S(1)}, u32[]{:S(2)}, u32[]{:S(2)}) async-start(s32[32,2,128]{2,1,0:T(2,128)} %broadcast_in_dim.4), calls=%async_computation | async-start | bytes 65536 | tf_op jit(solution)/shard_map/all_to_all | solution.py:682
  18.5 63.2 %all-gather.9.cloned.1.call-start = ((), (), s32[]{:S(2)}) async-start(), calls=%async_computation.7 | async-start | bytes 2621440 | tf_op jit(solution)/shard_map/all_gather | solution.py:733
  19.2 6.6 %copy-start.8 = (s32[1,32,256]{2,1,0:T(8,128)S(1)}, s32[1,32,256]{2,1,0:T(8,128)}, u32[]{:S(2)}) copy-start(s32[1,32,256]{2,1,0:T(8,128)} %param.14) | copy-start | bytes 98308
  36.7 9.0 %copy-start.4 = (bf16[512,128]{1,0:T(8,128)(2,1)S(1)}, bf16[512,128]{1,0:T(8,128)(2,1)}, u32[]{:S(2)}) copy-start(bf16[512,128]{1,0:T(8,128)(2,1)} %key_ref.1) | copy-start | bytes 393220
  36.7 9.2 %copy-start.5 = (bf16[512,128]{1,0:T(8,128)(2,1)S(1)}, bf16[512,128]{1,0:T(8,128)(2,1)}, u32[]{:S(2)}) copy-start(bf16[512,128]{1,0:T(8,128)(2,1)} %value_ref.1) | copy-start | bytes 393220
  36.7 9.3 %copy-start.6 = (bf16[512,128]{1,0:T(8,128)(2,1)S(1)}, bf16[512,128]{1,0:T(8,128)(2,1)}, u32[]{:S(2)}) copy-start(bf16[512,128]{1,0:T(8,128)(2,1)} %wq_ref.1) | copy-start | bytes 393220
  36.7 9.4 %copy-start.7 = (bf16[128,512]{1,0:T(8,128)(2,1)S(1)}, bf16[128,512]{1,0:T(8,128)(2,1)}, u32[]{:S(2)}) copy-start(bf16[128,512]{1,0:T(8,128)(2,1)} %wo_ref.1) | copy-start | bytes 393220
  36.7 36.8 %all-to-all-start.1 = ((bf16[32,256,128]{2,1,0:T(8,128)(2,1)}), bf16[32,256,128]{2,1,0:T(8,128)(2,1)S(1)}, u32[]{:S(2)}, u32[]{:S(2)}) async-start(bf16[32,256,128]{2,1,0:T(8,128)(2,1)} %get-tuple-element.70), calls=%async_computation.1 | async-start | bytes 4194304 | tf_op jit(solution)/shard_map/all_to_all | solution.py:682
  45.6 59.7 %all-gather.11.cloned.1.call-start = ((), (), s32[]{:S(2)}) async-start(), calls=%async_computation.8 | async-start | bytes 2621440 | tf_op jit(solution)/shard_map/all_gather | solution.py:735
  74.9 34.7 %all-to-all-start.2 = ((bf16[32,256,128]{2,1,0:T(8,128)(2,1)}), bf16[32,256,128]{2,1,0:T(8,128)(2,1)}, u32[]{:S(2)}, u32[]{:S(2)}) async-start(bf16[32,256,128]{2,1,0:T(8,128)(2,1)} %get-tuple-element.75), calls=%async_computation.2 | async-start | bytes 4194304 | tf_op jit(solution)/shard_map/all_to_all | solution.py:682
  81.6 62.0 %all-gather.13.cloned.1.call-start = ((), (), s32[]{:S(2)}) async-start(), calls=%async_computation.9 | async-start | bytes 2621440 | tf_op jit(solution)/shard_map/all_gather | solution.py:756
  109.6 34.0 %all-to-all-start.3 = ((bf16[32,256,128]{2,1,0:T(8,128)(2,1)}), bf16[32,256,128]{2,1,0:T(8,128)(2,1)S(1)}, u32[]{:S(2)}, u32[]{:S(2)}) async-start(bf16[32,256,128]{2,1,0:T(8,128)(2,1)} %get-tuple-element.79), calls=%async_computation.3 | async-start | bytes 4194304 | tf_op jit(solution)/shard_map/all_to_all | solution.py:682
  115.7 65.6 %all-gather.15.cloned.1.call-start = ((), (), s32[]{:S(2)}) async-start(), calls=%async_computation.10 | async-start | bytes 2621440 | tf_op jit(solution)/shard_map/all_gather | solution.py:756
  145.0 36.3 %all-to-all-start.4 = ((bf16[32,256,128]{2,1,0:T(8,128)(2,1)}), bf16[32,256,128]{2,1,0:T(8,128)(2,1)S(1)}, u32[]{:S(2)}, u32[]{:S(2)}) async-start(bf16[32,256,128]{2,1,0:T(8,128)(2,1)} %get-tuple-element.81), calls=%async_computation.4 | async-start | bytes 4194304 | tf_op jit(solution)/shard_map/all_to_all | solution.py:682
  158.6 15.0 %collective-permute-start = (bf16[1024,128]{1,0:T(8,128)(2,1)}, bf16[1024,128]{1,0:T(8,128)(2,1)S(1)}, u32[]{:S(2)}, u32[]{:S(2)}) collective-permute-start(bf16[1024,128]{1,0:T(8,128)(2,1)} %get-tuple-element.86), channel_id=1, source_target_pairs={{0,1},{1,2},{2,3},{3,0},{4,5},{5,6},{6,7},{7,4},{8,9},{9,10},{10,1... | collective-permute-start | bytes 786440 | tf_op jit(solution)/shard_map/ppermute | solution.py:688
  159.9 21.4 %collective-permute-start.1 = (bf16[1024,128]{1,0:T(8,128)(2,1)}, bf16[1024,128]{1,0:T(8,128)(2,1)S(1)}, u32[]{:S(2)}, u32[]{:S(2)}) collective-permute-start(bf16[1024,128]{1,0:T(8,128)(2,1)} %get-tuple-element.87), channel_id=1, source_target_pairs={{0,2},{1,3},{2,0},{3,1},{4,6},{5,7},{6,4},{7,5},{8,10},{9,11},{10,... | collective-permute-start | bytes 786440 | tf_op jit(solution)/shard_map/ppermute | solution.py:688
  162.3 18.9 %collective-permute-start.2 = (bf16[1024,128]{1,0:T(8,128)(2,1)}, bf16[1024,128]{1,0:T(8,128)(2,1)S(1)}, u32[]{:S(2)}, u32[]{:S(2)}) collective-permute-start(bf16[1024,128]{1,0:T(8,128)(2,1)} %get-tuple-element.88), channel_id=1, source_target_pairs={{0,3},{1,0},{2,1},{3,2},{4,7},{5,4},{6,5},{7,6},{8,11},{9,8},{10,9... | collective-permute-start | bytes 786440 | tf_op jit(solution)/shard_map/ppermute | solution.py:688
  173.5 17.2 %copy-start.9 = (bf16[1024,128]{1,0:T(8,128)(2,1)}, bf16[1024,128]{1,0:T(8,128)(2,1)S(1)}, u32[]{:S(2)}) copy-start(bf16[1024,128]{1,0:T(8,128)(2,1)S(1)} %collective-permute-done.refs_6_) | copy-start | bytes 786436
  181.3 9.5 %copy-start.10 = (bf16[1024,128]{1,0:T(8,128)(2,1)}, bf16[1024,128]{1,0:T(8,128)(2,1)S(1)}, u32[]{:S(2)}) copy-start(bf16[1024,128]{1,0:T(8,128)(2,1)S(1)} %collective-permute-done.1.refs_8_) | copy-start | bytes 786436
  181.3 9.5 %copy-start.11 = (bf16[1024,128]{1,0:T(8,128)(2,1)}, bf16[1024,128]{1,0:T(8,128)(2,1)S(1)}, u32[]{:S(2)}) copy-start(bf16[1024,128]{1,0:T(8,128)(2,1)S(1)} %collective-permute-done.2.refs_10_) | copy-start | bytes 786436
  190.7 23.7 %collective-permute-start.3 = (bf16[1024,128]{1,0:T(8,128)(2,1)}, bf16[1024,128]{1,0:T(8,128)(2,1)S(1)}, u32[]{:S(2)}, u32[]{:S(2)}) collective-permute-start(bf16[1024,128]{1,0:T(8,128)(2,1)} %get-tuple-element.107), channel_id=1, source_target_pairs={{0,1},{1,2},{2,3},{3,0},{4,5},{5,6},{6,7},{7,4},{8,9},{9,10},{10,1... | collective-permute-start | bytes 786440 | tf_op jit(solution)/shard_map/ppermute | solution.py:688
  190.8 23.6 %collective-permute-start.4 = (bf16[1024,128]{1,0:T(8,128)(2,1)}, bf16[1024,128]{1,0:T(8,128)(2,1)S(1)}, u32[]{:S(2)}, u32[]{:S(2)}) collective-permute-start(bf16[1024,128]{1,0:T(8,128)(2,1)} %get-tuple-element.109), channel_id=1, source_target_pairs={{0,2},{1,3},{2,0},{3,1},{4,6},{5,7},{6,4},{7,5},{8,10},{9,11},{10,... | collective-permute-start | bytes 786440 | tf_op jit(solution)/shard_map/ppermute | solution.py:688
  192.2 22.3 %collective-permute-start.5 = (bf16[1024,128]{1,0:T(8,128)(2,1)}, bf16[1024,128]{1,0:T(8,128)(2,1)S(1)}, u32[]{:S(2)}, u32[]{:S(2)}) collective-permute-start(bf16[1024,128]{1,0:T(8,128)(2,1)} %get-tuple-element.111), channel_id=1, source_target_pairs={{0,3},{1,0},{2,1},{3,2},{4,7},{5,4},{6,5},{7,6},{8,11},{9,8},{10,9... | collective-permute-start | bytes 786440 | tf_op jit(solution)/shard_map/ppermute | solution.py:688
  193.9 27.4 %all-to-all-start.5 = ((f32[32,64,128]{2,1,0:T(8,128)}), f32[32,64,128]{2,1,0:T(8,128)S(1)}, u32[]{:S(2)}, u32[]{:S(2)}) async-start(f32[32,64,128]{2,1,0:T(8,128)} %get-tuple-element.102), calls=%async_computation.5 | async-start | bytes 2097152 | tf_op jit(solution)/shard_map/all_to_all | solution.py:682
  221.3 8.6 %copy-start.15 = (bf16[1024,128]{1,0:T(8,128)(2,1)S(1)}, bf16[1024,128]{1,0:T(8,128)(2,1)}, u32[]{:S(2)}) copy-start(bf16[1024,128]{1,0:T(8,128)(2,1)} %get-tuple-element.122) | copy-start | bytes 786436
  221.3 8.7 %copy-start.13 = (bf16[1024,128]{1,0:T(8,128)(2,1)S(1)}, bf16[1024,128]{1,0:T(8,128)(2,1)}, u32[]{:S(2)}) copy-start(bf16[1024,128]{1,0:T(8,128)(2,1)} %get-tuple-element.123) | copy-start | bytes 786436
  221.3 10.7 %copy-start.12 = (bf16[1024,128]{1,0:T(8,128)(2,1)S(1)}, bf16[1024,128]{1,0:T(8,128)(2,1)}, u32[]{:S(2)}) copy-start(bf16[1024,128]{1,0:T(8,128)(2,1)} %get-tuple-element.124) | copy-start | bytes 786436
  221.3 23.5 %copy-start = (bf16[1024,128]{1,0:T(8,128)(2,1)S(1)}, bf16[1024,128]{1,0:T(8,128)(2,1)}, u32[]{:S(2)}) copy-start(bf16[1024,128]{1,0:T(8,128)(2,1)} %get-tuple-element.121.refs_1_) | copy-start | bytes 786436
  222.5 24.6 %all-to-all-start.6 = ((f32[32,64,128]{2,1,0:T(8,128)}), f32[32,64,128]{2,1,0:T(8,128)S(1)}, u32[]{:S(2)}, u32[]{:S(2)}) async-start(f32[32,64,128]{2,1,0:T(8,128)} %broadcast_in_dim.5), calls=%async_computation.6 | async-start | bytes 2097152 | tf_op jit(solution)/shard_map/all_to_all | solution.py:682
  229.9 14.6 %collective-permute-start.6 = (bf16[1024,128]{1,0:T(8,128)(2,1)S(1)}, bf16[1024,128]{1,0:T(8,128)(2,1)S(1)}, u32[]{:S(2)}, u32[]{:S(2)}) collective-permute-start(bf16[1024,128]{1,0:T(8,128)(2,1)S(1)} %copy-done.15), channel_id=1, source_target_pairs={{0,1},{1,2},{2,3},{3,0},{4,5},{5,6},{6,7},{7,4},{8,9},{9,10},{10,1... | collective-permute-start | bytes 786440 | tf_op jit(solution)/shard_map/ppermute | solution.py:688
  230.0 14.5 %collective-permute-start.7 = (bf16[1024,128]{1,0:T(8,128)(2,1)S(1)}, bf16[1024,128]{1,0:T(8,128)(2,1)S(1)}, u32[]{:S(2)}, u32[]{:S(2)}) collective-permute-start(bf16[1024,128]{1,0:T(8,128)(2,1)S(1)} %copy-done.13), channel_id=1, source_target_pairs={{0,2},{1,3},{2,0},{3,1},{4,6},{5,7},{6,4},{7,5},{8,10},{9,11},{10,... | collective-permute-start | bytes 786440 | tf_op jit(solution)/shard_map/ppermute | solution.py:688
  232.0 12.8 %collective-permute-start.8 = (bf16[1024,128]{1,0:T(8,128)(2,1)S(1)}, bf16[1024,128]{1,0:T(8,128)(2,1)S(1)}, u32[]{:S(2)}, u32[]{:S(2)}) collective-permute-start(bf16[1024,128]{1,0:T(8,128)(2,1)S(1)} %copy-done.12), channel_id=1, source_target_pairs={{0,3},{1,0},{2,1},{3,2},{4,7},{5,4},{6,5},{7,6},{8,11},{9,8},{10,9... | collective-permute-start | bytes 786440 | tf_op jit(solution)/shard_map/ppermute | solution.py:688
  (6 other events, 6.6 us)
Sparse Core Ops, SparseCore 0:
  21.0 31.7 all-gather.8
  55.0 30.8 all-gather.10
  105.4 31.9 all-gather.12
  139.5 36.8 all-gather.14

commit v5 on v4

--- a/solution.py
+++ b/solution.py
@@ -121,6 +121,11 @@
     return lax.fori_loop(0, list_ref.shape[0], add, jnp.int32(0))
 
 
+def tile_rows(rows_ref, t):
+    both = rows_ref[pl.ds(t // 2, 1), :]
+    return jnp.where(t % 2 == 1, both[:, TS:], both[:, :TS])
+
+
 def gather_kernel(need_ref, rows_ref, table_hbm, *rest):
     out_refs = rest[:-6]
     table_ref, hot, sent, list_ref, sems, table_sem = rest[-6:]
@@ -149,7 +154,7 @@
     def quad(step, carry):
         tiles = [list_ref[jnp.minimum(step * QUAD + k, count - 1)] for k in range(QUAD)]
         wanted = jnp.concatenate(
-            [jnp.transpose(jnp.broadcast_to(rows_ref[t], (TS, TS))) for t in tiles], axis=0
+            [jnp.transpose(jnp.broadcast_to(tile_rows(rows_ref, t), (TS, TS))) for t in tiles], axis=0
         )
         upper = wanted >= half
         away = jnp.where(upper, wanted - half, wanted)
@@ -458,7 +463,7 @@
         for k in range(QUAD):
             place = step * QUAD + k
             t = list_ref[jnp.minimum(place, count - 1)]
-            spot = jnp.where(place < count, rows_ref[t], -1)
+            spot = jnp.where(place < count, tile_rows(rows_ref, t), -1)
             upper = jnp.transpose(jnp.broadcast_to(spot, (TS, TS))) >= half
             part = halo_ref[t // 2, pl.ds((t % 2) * TS, TS), :]
             keep = jnp.where(upper, 1.0, 0.0).astype(jnp.bfloat16)
@@ -692,6 +697,10 @@
 
 def after(values, earlier):
     return lax.optimization_barrier((values, earlier))
+
+
+def corner(values):
+    return values[:1, :16, :]
 
 
 def by_head(first, second):
@@ -723,7 +732,7 @@
     where = lax.axis_index("feat").astype(jnp.int32).reshape(1)
     gain_src = gain_src.reshape(1, width)
     gain_dst = gain_dst.reshape(1, width)
-    rows = send_rows.reshape(2 * peers, 1, TS)
+    rows = send_rows.reshape(peers, 2 * TS)
 
     wanted = own_tiles + jnp.arange(2 * peers, dtype=jnp.int32)
     need = jnp.any(tile_src.reshape(-1, 1) == wanted[None, :], axis=0).astype(jnp.int32)
@@ -743,7 +752,7 @@
     for h in range(heads):
         sent = outgoing[h]
         if h > 0:
-            sent, (halo[h - 1], normed_src) = after(sent, (halo[h - 1], normed_src))
+            sent, (_, normed_src) = after(sent, (corner(halo[h - 1]), normed_src))
         halo.append(over_graph(sent))
 
     own_grads, returned, mixed, weight_grads = [], [], [], []
@@ -759,8 +768,8 @@
                 halo_grad, (halo[heads - 1], back_weights)
             )
         else:
-            halo_grad, (returned[h - 1], mixed[h - 1]) = after(
-                halo_grad, (returned[h - 1], mixed[h - 1])
+            halo_grad, (_, mixed[h - 1]) = after(
+                halo_grad, (corner(returned[h - 1]), mixed[h - 1])
             )
         returned.append(over_graph(halo_grad))
 

time: 258 us -> 255 us (0.988)
  Pallas kernels: 99.3 us -> 102 us
    ppermute x9, waiting for transfers between devices: 28.6 us -> 24.5 us  [over_feat(): lax.ppermute(parts[s], 'feat', [(i, (i + s) % groups) for i in range(grou...]
    all_to_all x7, waiting for transfers between devices: 34.1 us -> 36.9 us  [over_graph(): lax.all_to_all(values, 'graph', split_axis=0, concat_axis=0, tiled=True)]
    unnamed x39 -> x37, local copies, waits for them, and re-layouts: 5.48 us -> 5.34 us
  transfers between devices with their start and end apart: 20 -> 20, of which waited for: 8 -> 10; matrix products, arithmetic and copies ran while one was open for 1% -> 2% of each run, Pallas kernels for 35% -> 36%
where the time goes in v5:
time: 255 us; the launch traced here: 254 us
  Pallas kernels  102 us (40%)
  starting transfers between devices  65.1 us (26%)
  waiting for transfers between devices  62.2 us (24%)
  between operations  14.1 us (6%)
  local copies, waits for them, and re-layouts  9.35 us (4%)
    all_to_all x7, starting transfers between devices, over_graph(): lax.all_to_all(values, 'graph', split_axis=0, concat_axis=0, tiled=True)  52 us
    all_to_all x7, waiting for transfers between devices, over_graph(): lax.all_to_all(values, 'graph', split_axis=0, concat_axis=0, tiled=True)  36.9 us
    pallas_call x2, Pallas kernels, attention(): pl.pallas_call(lambda *refs: attention_kernel(head, *refs), grid=(blocks,...  35.4 us
    ppermute x9, waiting for transfers between devices, over_feat(): lax.ppermute(parts[s], 'feat', [(i, (i + s) % groups) for i in range(grou...  24.5 us
    pallas_call x2, Pallas kernels, scatter_rows(): pl.pallas_call(lambda *refs: scatter_kernel(len(earlier), *refs), in_spec...  17.3 us
    ppermute x9, starting transfers between devices, over_feat(): lax.ppermute(parts[s], 'feat', [(i, (i + s) % groups) for i in range(grou...  12.7 us
    pallas_call x1, Pallas kernels, mesh_rows(): pl.pallas_call(lambda *refs: mesh_kernel(heads, *refs), grid_spec=pltpu.P...  10.8 us
    pallas_call x1, Pallas kernels, gather_rows(): pl.pallas_call(gather_kernel, in_specs=[SMEM, VMEM, ANY], out_specs=[ANY]...  10.4 us
  transfers between devices with their start and end apart: 20, of which 10 were waited for; matrix products, arithmetic and copies ran while one was open for 2% of the time, Pallas kernels for 36%

profile of v5, /device:TPU:1, one launch (start us, length us, event | category | flops | bytes accessed | tf_op | source)
XLA Modules:
  0.0 254.2 jit_solution(14298952549826613596)
XLA Ops:
  9.6 9.6 %all-to-all-start = ((s32[32,2,128]{2,1,0:T(2,128)}), s32[32,2,128]{2,1,0:T(2,128)S(1)}, u32[]{:S(2)}, u32[]{:S(2)}) async-start(s32[32,2,128]{2,1,0:T(2,128)} %broadcast_in_dim.4), calls=%async_computation | async-start | bytes 65536 | tf_op jit(solution)/shard_map/all_to_all | solution.py:687
  19.2 6.6 %source_terms.1.refs_1_ = bf16[4096,256]{1,0:T(8,128)(2,1)} custom-call(bf16[4096,512]{1,0:T(8,128)(2,1)} %refs_2_.2, f32[1,512]{1,0:T(1,128)} %bitcast.39, bf16[512,128]{1,0:T(8,128)(2,1)} %key_ref.1, bf16[512,128]{1,0:T(8,128)(2,1)} %value_ref.1), custom_call_target="tpu_custom_call" | custom-call | flops 9200000000 | bytes 1048576 | tf_op jit(solution)/shard_map/source_terms/pallas_call | solution.py:94
  27.8 10.4 %gather_rows.1 = (bf16[32,256,128]{2,1,0:T(8,128)(2,1)}, bf16[32,256,128]{2,1,0:T(8,128)(2,1)}) custom-call(s32[64]{0:T(128)} %reshape_squeeze.3.need_ref.refs_1_, s32[32,256]{1,0:T(8,128)} %bitcast.34, bf16[2,2048,256]{2,1,0:T(8,128)(2,1)} %bitcast.42), custom_call_target="tpu_custom_call" | custom-call | flops 11500000256 | bytes 1048576 | tf_op jit(solution)/shard_map/gather_rows/pallas_call | solution.py:187
  38.2 9.3 %all-to-all-start.1 = ((bf16[32,256,128]{2,1,0:T(8,128)(2,1)}), bf16[32,256,128]{2,1,0:T(8,128)(2,1)S(1)}, u32[]{:S(2)}, u32[]{:S(2)}) async-start(bf16[32,256,128]{2,1,0:T(8,128)(2,1)} %get-tuple-element.67), calls=%async_computation.1 | async-start | bytes 4194304 | tf_op jit(solution)/shard_map/all_to_all | solution.py:687
  48.9 7.7 %normed_rows.1.refs_5_ = bf16[4096,512]{1,0:T(8,128)(2,1)} custom-call(bf16[4096,512]{1,0:T(8,128)(2,1)} %refs_2_.2, f32[1,512]{1,0:T(1,128)} %bitcast.40), custom_call_target="tpu_custom_call" | custom-call | flops 9200000000 | bytes 1048576 | tf_op jit(solution)/shard_map/normed_rows/pallas_call | solution.py:214
  56.5 6.0 %target_terms.1 = (bf16[2048,512]{1,0:T(8,128)(2,1)}, bf16[2048,128]{1,0:T(8,128)(2,1)}, bf16[2048,128]{1,0:T(8,128)(2,1)}) custom-call(bf16[2048,512]{1,0:T(8,128)(2,1)} %refs_2_.3, f32[1,512]{1,0:T(1,128)} %bitcast.37, bf16[512,128]{1,0:T(8,128)(2,1)} %wq_ref.1, bf16[128,512]{1,0:T(8,128)(2,1)} %wo_ref.1, bf16[4,2048,128]{2,1,0:T(8,128)(2,1)} %bitcast.30), custom_call_target="tpu_custom_call" | custom-call | flops 6899999744 | bytes 1048576 | tf_op jit(solution)/shard_map/target_terms/pallas_call | solution.py:246
  62.5 12.9 %all-to-all-done.1.refs_2_ = bf16[32,256,128]{2,1,0:T(8,128)(2,1)S(1)} async-done(((bf16[32,256,128]{2,1,0:T(8,128)(2,1)}), bf16[32,256,128]{2,1,0:T(8,128)(2,1)S(1)}, u32[]{:S(2)}, u32[]{:S(2)}) %all-to-all-start.1) | async-done | bytes 2097184 | tf_op jit(solution)/shard_map/all_to_all | solution.py:687
  75.4 1.4 copy-done.2
  76.8 6.7 %all-to-all-start.2 = ((bf16[32,256,128]{2,1,0:T(8,128)(2,1)}), bf16[32,256,128]{2,1,0:T(8,128)(2,1)}, u32[]{:S(2)}, u32[]{:S(2)}) async-start(bf16[32,256,128]{2,1,0:T(8,128)(2,1)} %get-tuple-element.72), calls=%async_computation.2 | async-start | bytes 4194304 | tf_op jit(solution)/shard_map/all_to_all | solution.py:687
  83.5 17.7 %attention.2 = (bf16[4096,128]{1,0:T(8,128)(2,1)}, bf16[32,256,128]{2,1,0:T(8,128)(2,1)}, f32[4,128,128]{2,1,0:T(8,128)}, bf16[2048,128]{1,0:T(8,128)(2,1)}) custom-call(s32[4,8]{1,0:T(4,128)} %refs_0_.3, bf16[4096,256]{1,0:T(8,128)(2,1)} %source_terms.1.refs_1_, bf16[32,256,128]{2,1,0:T(8,128)(2,1)} %copy-done.2, ...), custom_call_target="tpu_custom_call" | custom-call | flops 20700000256 | bytes 1048576 | tf_op jit(solution)/shard_map/attention/pallas_call | solution.py:409
  101.2 10.2 %all-to-all-done.2.refs_2_ = bf16[32,256,128]{2,1,0:T(8,128)(2,1)} async-done(((bf16[32,256,128]{2,1,0:T(8,128)(2,1)}), bf16[32,256,128]{2,1,0:T(8,128)(2,1)}, u32[]{:S(2)}, u32[]{:S(2)}) %all-to-all-start.2) | async-done | bytes 2097184 | tf_op jit(solution)/shard_map/all_to_all | solution.py:687
  111.5 6.1 %all-to-all-start.4 = ((bf16[32,256,128]{2,1,0:T(8,128)(2,1)}), bf16[32,256,128]{2,1,0:T(8,128)(2,1)S(1)}, u32[]{:S(2)}, u32[]{:S(2)}) async-start(bf16[32,256,128]{2,1,0:T(8,128)(2,1)} %get-tuple-element.79), calls=%async_computation.4 | async-start | bytes 4194304 | tf_op jit(solution)/shard_map/all_to_all | solution.py:687
  117.8 17.8 %attention.3 = (bf16[4096,128]{1,0:T(8,128)(2,1)}, bf16[32,256,128]{2,1,0:T(8,128)(2,1)}, f32[4,128,128]{2,1,0:T(8,128)}, bf16[2048,128]{1,0:T(8,128)(2,1)}) custom-call(s32[4,8]{1,0:T(4,128)} %refs_0_.3, bf16[4096,256]{1,0:T(8,128)(2,1)} %source_terms.1.refs_1_, bf16[32,256,128]{2,1,0:T(8,128)(2,1)} %all-to-all-done.2.refs_2_, ...), custom_call_target="tpu_custom_call" | custom-call | flops 20700000256 | bytes 1048576 | tf_op jit(solution)/shard_map/attention/pallas_call | solution.py:409
  135.6 9.9 %all-to-all-done.4.refs_3_ = bf16[32,256,128]{2,1,0:T(8,128)(2,1)S(1)} async-done(((bf16[32,256,128]{2,1,0:T(8,128)(2,1)}), bf16[32,256,128]{2,1,0:T(8,128)(2,1)S(1)}, u32[]{:S(2)}, u32[]{:S(2)}) %all-to-all-start.4) | async-done | bytes 2097184 | tf_op jit(solution)/shard_map/all_to_all | solution.py:687
  145.5 1.3 copy-done.3
  146.8 6.0 %all-to-all-start.3 = ((bf16[32,256,128]{2,1,0:T(8,128)(2,1)}), bf16[32,256,128]{2,1,0:T(8,128)(2,1)S(1)}, u32[]{:S(2)}, u32[]{:S(2)}) async-start(bf16[32,256,128]{2,1,0:T(8,128)(2,1)} %get-tuple-element.77), calls=%async_computation.3 | async-start | bytes 4194304 | tf_op jit(solution)/shard_map/all_to_all | solution.py:687
  152.8 8.4 %scatter_rows.2 = (f32[4,128,128]{2,1,0:T(8,128)}, bf16[1024,128]{1,0:T(8,128)(2,1)}, bf16[1024,128]{1,0:T(8,128)(2,1)}, bf16[1024,128]{1,0:T(8,128)(2,1)}, bf16[1024,128]{1,0:T(8,128)(2,1)}) custom-call(s32[1]{0:T(128)} %bitcast.16.refs_0_, s32[64]{0:T(128)} %reshape_squeeze.3.need_ref.refs_1_, bf16[4096,128]{1,0:T(8,128)(2,1)} %get-tuple-element.78.refs_2_, ...), custom_call_target="tpu_custom_call" | custom-call | flops 12650000384 | bytes 1048576 | tf_op jit(solution)/shard_map/scatter_rows/pallas_call | solution.py:515
  161.2 1.3 collective-permute-start
  162.5 2.5 collective-permute-start.1
  166.1 6.7 %collective-permute-done.refs_6_ = bf16[1024,128]{1,0:T(8,128)(2,1)S(1)} collective-permute-done((bf16[1024,128]{1,0:T(8,128)(2,1)}, bf16[1024,128]{1,0:T(8,128)(2,1)S(1)}, u32[]{:S(2)}, u32[]{:S(2)}) %collective-permute-start) | collective-permute-done | bytes 262176 | tf_op jit(solution)/shard_map/ppermute | solution.py:693
  172.8 5.9 %collective-permute-done.1.refs_8_ = bf16[1024,128]{1,0:T(8,128)(2,1)S(1)} collective-permute-done((bf16[1024,128]{1,0:T(8,128)(2,1)}, bf16[1024,128]{1,0:T(8,128)(2,1)S(1)}, u32[]{:S(2)}, u32[]{:S(2)}) %collective-permute-start.1) | collective-permute-done | bytes 262176 | tf_op jit(solution)/shard_map/ppermute | solution.py:693
  178.8 2.0 all-to-all-done.3.refs_3_
  180.8 1.4 copy-done.1
  182.2 8.9 %scatter_rows.3 = (f32[32,64,128]{2,1,0:T(8,128)}, bf16[1024,128]{1,0:T(8,128)(2,1)}, bf16[1024,128]{1,0:T(8,128)(2,1)}, bf16[1024,128]{1,0:T(8,128)(2,1)}, bf16[1024,128]{1,0:T(8,128)(2,1)}) custom-call(s32[1]{0:T(128)} %bitcast.16.refs_0_, s32[64]{0:T(128)} %reshape_squeeze.3.need_ref.refs_1_, bf16[4096,128]{1,0:T(8,128)(2,1)} %get-tuple-element.92.refs_2_, ...), custom_call_target="tpu_custom_call" | custom-call | flops 12650000384 | bytes 1048576 | tf_op jit(solution)/shard_map/scatter_rows/pallas_call | solution.py:515
  192.4 2.5 collective-permute-start.4
  196.0 6.8 %all-to-all-start.5 = ((f32[32,64,128]{2,1,0:T(8,128)}), f32[32,64,128]{2,1,0:T(8,128)S(1)}, u32[]{:S(2)}, u32[]{:S(2)}) async-start(f32[32,64,128]{2,1,0:T(8,128)} %get-tuple-element.98), calls=%async_computation.5 | async-start | bytes 2097152 | tf_op jit(solution)/shard_map/all_to_all | solution.py:687
  202.8 10.8 %mesh_rows.1 = (bf16[2048,128]{1,0:T(8,128)(2,1)}, bf16[2048,128]{1,0:T(8,128)(2,1)}) custom-call(s32[1]{0:T(128)} %bitcast.16.refs_0_, bf16[4,2,2,128,512]{4,3,2,1,0:T(8,128)(2,1)} %bitcast.27, bf16[2048,512]{1,0:T(8,128)(2,1)} %refs_2_.3, bf16[2048,128]{1,0:T(8,128)(2,1)} %refs_3_.1, f32[1,512]{1,0:T(1,128)} %bitcast.38, bf16[4,2048,128]{2,1,0:T(8,128)(2,1)} %bitcast.29, ...), custom_call_target="tpu_custom_call" | custom-call | flops 12650000384 | bytes 1048576 | tf_op jit(solution)/shard_map/mesh_rows/pallas_call | solution.py:641
  214.4 6.0 %grid_rows.1 = (bf16[1024,128]{1,0:T(8,128)(2,1)}, bf16[1024,128]{1,0:T(8,128)(2,1)}, bf16[1024,128]{1,0:T(8,128)(2,1)}, bf16[1024,128]{1,0:T(8,128)(2,1)}) custom-call(s32[1]{0:T(128)} %bitcast.16.refs_0_, bf16[4,2,2,128,512]{4,3,2,1,0:T(8,128)(2,1)} %bitcast.28, bf16[4096,512]{1,0:T(8,128)(2,1)} %refs_2_.2, f32[1,512]{1,0:T(1,128)} %bitcast.41, ...), custom_call_target="tpu_custom_call" | custom-call | flops 6899999744 | bytes 1048576 | tf_op jit(solution)/shard_map/grid_rows/pallas_call | solution.py:593
  221.6 7.5 %all-to-all-start.6 = ((f32[32,64,128]{2,1,0:T(8,128)}), f32[32,64,128]{2,1,0:T(8,128)S(1)}, u32[]{:S(2)}, u32[]{:S(2)}) async-start(f32[32,64,128]{2,1,0:T(8,128)} %broadcast_in_dim.5), calls=%async_computation.6 | async-start | bytes 2097152 | tf_op jit(solution)/shard_map/all_to_all | solution.py:687
  230.2 1.9 collective-permute-start.8
  232.1 11.6 %collective-permute-done.6.refs_2_ = bf16[1024,128]{1,0:T(8,128)(2,1)S(1)} collective-permute-done((bf16[1024,128]{1,0:T(8,128)(2,1)S(1)}, bf16[1024,128]{1,0:T(8,128)(2,1)S(1)}, u32[]{:S(2)}, u32[]{:S(2)}) %collective-permute-start.6) | collective-permute-done | bytes 262176 | tf_op jit(solution)/shard_map/ppermute | solution.py:693
  246.3 1.4 finish.1
  (73 shorter events, 15.2 us)
Async XLA Ops:
  7.2 49.4 %all-gather.9.cloned.1.call-start = ((), (), s32[]{:S(2)}) async-start(), calls=%async_computation.7 | async-start | bytes 2621440 | tf_op jit(solution)/shard_map/all_gather | solution.py:742
  9.6 16.9 %all-to-all-start = ((s32[32,2,128]{2,1,0:T(2,128)}), s32[32,2,128]{2,1,0:T(2,128)S(1)}, u32[]{:S(2)}, u32[]{:S(2)}) async-start(s32[32,2,128]{2,1,0:T(2,128)} %broadcast_in_dim.4), calls=%async_computation | async-start | bytes 65536 | tf_op jit(solution)/shard_map/all_to_all | solution.py:687
  38.1 9.4 %copy-start.4 = (bf16[512,128]{1,0:T(8,128)(2,1)S(1)}, bf16[512,128]{1,0:T(8,128)(2,1)}, u32[]{:S(2)}) copy-start(bf16[512,128]{1,0:T(8,128)(2,1)} %key_ref.1) | copy-start | bytes 393220
  38.1 9.6 %copy-start.5 = (bf16[512,128]{1,0:T(8,128)(2,1)S(1)}, bf16[512,128]{1,0:T(8,128)(2,1)}, u32[]{:S(2)}) copy-start(bf16[512,128]{1,0:T(8,128)(2,1)} %value_ref.1) | copy-start | bytes 393220
  38.2 9.7 %copy-start.6 = (bf16[512,128]{1,0:T(8,128)(2,1)S(1)}, bf16[512,128]{1,0:T(8,128)(2,1)}, u32[]{:S(2)}) copy-start(bf16[512,128]{1,0:T(8,128)(2,1)} %wq_ref.1) | copy-start | bytes 393220
  38.2 9.8 %copy-start.7 = (bf16[128,512]{1,0:T(8,128)(2,1)S(1)}, bf16[128,512]{1,0:T(8,128)(2,1)}, u32[]{:S(2)}) copy-start(bf16[128,512]{1,0:T(8,128)(2,1)} %wo_ref.1) | copy-start | bytes 393220
  38.2 37.2 %all-to-all-start.1 = ((bf16[32,256,128]{2,1,0:T(8,128)(2,1)}), bf16[32,256,128]{2,1,0:T(8,128)(2,1)S(1)}, u32[]{:S(2)}, u32[]{:S(2)}) async-start(bf16[32,256,128]{2,1,0:T(8,128)(2,1)} %get-tuple-element.67), calls=%async_computation.1 | async-start | bytes 4194304 | tf_op jit(solution)/shard_map/all_to_all | solution.py:687
  47.5 63.9 %all-gather.11.cloned.1.call-start = ((), (), s32[]{:S(2)}) async-start(), calls=%async_computation.8 | async-start | bytes 2621440 | tf_op jit(solution)/shard_map/all_gather | solution.py:744
  76.8 34.7 %all-to-all-start.2 = ((bf16[32,256,128]{2,1,0:T(8,128)(2,1)}), bf16[32,256,128]{2,1,0:T(8,128)(2,1)}, u32[]{:S(2)}, u32[]{:S(2)}) async-start(bf16[32,256,128]{2,1,0:T(8,128)(2,1)} %get-tuple-element.72), calls=%async_computation.2 | async-start | bytes 4194304 | tf_op jit(solution)/shard_map/all_to_all | solution.py:687
  83.5 52.1 %all-gather.13.cloned.1.call-start = ((), (), s32[]{:S(2)}) async-start(), calls=%async_computation.9 | async-start | bytes 2621440 | tf_op jit(solution)/shard_map/all_gather | solution.py:765
  111.5 34.0 %all-to-all-start.4 = ((bf16[32,256,128]{2,1,0:T(8,128)(2,1)}), bf16[32,256,128]{2,1,0:T(8,128)(2,1)S(1)}, u32[]{:S(2)}, u32[]{:S(2)}) async-start(bf16[32,256,128]{2,1,0:T(8,128)(2,1)} %get-tuple-element.79), calls=%async_computation.4 | async-start | bytes 4194304 | tf_op jit(solution)/shard_map/all_to_all | solution.py:687
  117.5 61.2 %all-gather.15.cloned.1.call-start = ((), (), s32[]{:S(2)}) async-start(), calls=%async_computation.10 | async-start | bytes 2621440 | tf_op jit(solution)/shard_map/all_gather | solution.py:765
  146.8 34.0 %all-to-all-start.3 = ((bf16[32,256,128]{2,1,0:T(8,128)(2,1)}), bf16[32,256,128]{2,1,0:T(8,128)(2,1)S(1)}, u32[]{:S(2)}, u32[]{:S(2)}) async-start(bf16[32,256,128]{2,1,0:T(8,128)(2,1)} %get-tuple-element.77), calls=%async_computation.3 | async-start | bytes 4194304 | tf_op jit(solution)/shard_map/all_to_all | solution.py:687
  161.2 11.6 %collective-permute-start = (bf16[1024,128]{1,0:T(8,128)(2,1)}, bf16[1024,128]{1,0:T(8,128)(2,1)S(1)}, u32[]{:S(2)}, u32[]{:S(2)}) collective-permute-start(bf16[1024,128]{1,0:T(8,128)(2,1)} %get-tuple-element.82), channel_id=1, source_target_pairs={{0,1},{1,2},{2,3},{3,0},{4,5},{5,6},{6,7},{7,4},{8,9},{9,10},{10,1... | collective-permute-start | bytes 786440 | tf_op jit(solution)/shard_map/ppermute | solution.py:693
  162.5 16.2 %collective-permute-start.1 = (bf16[1024,128]{1,0:T(8,128)(2,1)}, bf16[1024,128]{1,0:T(8,128)(2,1)S(1)}, u32[]{:S(2)}, u32[]{:S(2)}) collective-permute-start(bf16[1024,128]{1,0:T(8,128)(2,1)} %get-tuple-element.83), channel_id=1, source_target_pairs={{0,2},{1,3},{2,0},{3,1},{4,6},{5,7},{6,4},{7,5},{8,10},{9,11},{10,... | collective-permute-start | bytes 786440 | tf_op jit(solution)/shard_map/ppermute | solution.py:693
  165.0 13.7 %collective-permute-start.2 = (bf16[1024,128]{1,0:T(8,128)(2,1)}, bf16[1024,128]{1,0:T(8,128)(2,1)S(1)}, u32[]{:S(2)}, u32[]{:S(2)}) collective-permute-start(bf16[1024,128]{1,0:T(8,128)(2,1)} %get-tuple-element.84), channel_id=1, source_target_pairs={{0,3},{1,0},{2,1},{3,2},{4,7},{5,4},{6,5},{7,6},{8,11},{9,8},{10,9... | collective-permute-start | bytes 786440 | tf_op jit(solution)/shard_map/ppermute | solution.py:693
  172.8 18.3 %copy-start.8 = (bf16[1024,128]{1,0:T(8,128)(2,1)}, bf16[1024,128]{1,0:T(8,128)(2,1)S(1)}, u32[]{:S(2)}) copy-start(bf16[1024,128]{1,0:T(8,128)(2,1)S(1)} %collective-permute-done.refs_6_) | copy-start | bytes 786436
  178.7 12.4 %copy-start.9 = (bf16[1024,128]{1,0:T(8,128)(2,1)}, bf16[1024,128]{1,0:T(8,128)(2,1)S(1)}, u32[]{:S(2)}) copy-start(bf16[1024,128]{1,0:T(8,128)(2,1)S(1)} %collective-permute-done.1.refs_8_) | copy-start | bytes 786436
  178.7 12.4 %copy-start.10 = (bf16[1024,128]{1,0:T(8,128)(2,1)}, bf16[1024,128]{1,0:T(8,128)(2,1)S(1)}, u32[]{:S(2)}) copy-start(bf16[1024,128]{1,0:T(8,128)(2,1)S(1)} %collective-permute-done.2.refs_10_) | copy-start | bytes 786436
  180.8 1.4 copy-start.1
  191.1 22.5 %collective-permute-start.3 = (bf16[1024,128]{1,0:T(8,128)(2,1)}, bf16[1024,128]{1,0:T(8,128)(2,1)S(1)}, u32[]{:S(2)}, u32[]{:S(2)}) collective-permute-start(bf16[1024,128]{1,0:T(8,128)(2,1)} %get-tuple-element.103), channel_id=1, source_target_pairs={{0,1},{1,2},{2,3},{3,0},{4,5},{5,6},{6,7},{7,4},{8,9},{9,10},{10,1... | collective-permute-start | bytes 786440 | tf_op jit(solution)/shard_map/ppermute | solution.py:693
  192.4 21.2 %collective-permute-start.4 = (bf16[1024,128]{1,0:T(8,128)(2,1)}, bf16[1024,128]{1,0:T(8,128)(2,1)S(1)}, u32[]{:S(2)}, u32[]{:S(2)}) collective-permute-start(bf16[1024,128]{1,0:T(8,128)(2,1)} %get-tuple-element.105), channel_id=1, source_target_pairs={{0,2},{1,3},{2,0},{3,1},{4,6},{5,7},{6,4},{7,5},{8,10},{9,11},{10,... | collective-permute-start | bytes 786440 | tf_op jit(solution)/shard_map/ppermute | solution.py:693
  194.9 18.7 %collective-permute-start.5 = (bf16[1024,128]{1,0:T(8,128)(2,1)}, bf16[1024,128]{1,0:T(8,128)(2,1)S(1)}, u32[]{:S(2)}, u32[]{:S(2)}) collective-permute-start(bf16[1024,128]{1,0:T(8,128)(2,1)} %get-tuple-element.107), channel_id=1, source_target_pairs={{0,3},{1,0},{2,1},{3,2},{4,7},{5,4},{6,5},{7,6},{8,11},{9,8},{10,9... | collective-permute-start | bytes 786440 | tf_op jit(solution)/shard_map/ppermute | solution.py:693
  196.0 24.5 %all-to-all-start.5 = ((f32[32,64,128]{2,1,0:T(8,128)}), f32[32,64,128]{2,1,0:T(8,128)S(1)}, u32[]{:S(2)}, u32[]{:S(2)}) async-start(f32[32,64,128]{2,1,0:T(8,128)} %get-tuple-element.98), calls=%async_computation.5 | async-start | bytes 2097152 | tf_op jit(solution)/shard_map/all_to_all | solution.py:687
  220.4 8.7 %copy-start.14 = (bf16[1024,128]{1,0:T(8,128)(2,1)S(1)}, bf16[1024,128]{1,0:T(8,128)(2,1)}, u32[]{:S(2)}) copy-start(bf16[1024,128]{1,0:T(8,128)(2,1)} %get-tuple-element.118) | copy-start | bytes 786436
  220.4 9.2 %copy-start.12 = (bf16[1024,128]{1,0:T(8,128)(2,1)S(1)}, bf16[1024,128]{1,0:T(8,128)(2,1)}, u32[]{:S(2)}) copy-start(bf16[1024,128]{1,0:T(8,128)(2,1)} %get-tuple-element.119) | copy-start | bytes 786436
  220.4 9.8 %copy-start.11 = (bf16[1024,128]{1,0:T(8,128)(2,1)S(1)}, bf16[1024,128]{1,0:T(8,128)(2,1)}, u32[]{:S(2)}) copy-start(bf16[1024,128]{1,0:T(8,128)(2,1)} %get-tuple-element.120) | copy-start | bytes 786436
  220.4 23.6 %copy-start = (bf16[1024,128]{1,0:T(8,128)(2,1)S(1)}, bf16[1024,128]{1,0:T(8,128)(2,1)}, u32[]{:S(2)}) copy-start(bf16[1024,128]{1,0:T(8,128)(2,1)} %get-tuple-element.117.refs_1_) | copy-start | bytes 786436
  221.6 24.7 %all-to-all-start.6 = ((f32[32,64,128]{2,1,0:T(8,128)}), f32[32,64,128]{2,1,0:T(8,128)S(1)}, u32[]{:S(2)}, u32[]{:S(2)}) async-start(f32[32,64,128]{2,1,0:T(8,128)} %broadcast_in_dim.5), calls=%async_computation.6 | async-start | bytes 2097152 | tf_op jit(solution)/shard_map/all_to_all | solution.py:687
  229.1 14.6 %collective-permute-start.6 = (bf16[1024,128]{1,0:T(8,128)(2,1)S(1)}, bf16[1024,128]{1,0:T(8,128)(2,1)S(1)}, u32[]{:S(2)}, u32[]{:S(2)}) collective-permute-start(bf16[1024,128]{1,0:T(8,128)(2,1)S(1)} %copy-done.14), channel_id=1, source_target_pairs={{0,1},{1,2},{2,3},{3,0},{4,5},{5,6},{6,7},{7,4},{8,9},{9,10},{10,1... | collective-permute-start | bytes 786440 | tf_op jit(solution)/shard_map/ppermute | solution.py:693
  229.6 14.1 %collective-permute-start.7 = (bf16[1024,128]{1,0:T(8,128)(2,1)S(1)}, bf16[1024,128]{1,0:T(8,128)(2,1)S(1)}, u32[]{:S(2)}, u32[]{:S(2)}) collective-permute-start(bf16[1024,128]{1,0:T(8,128)(2,1)S(1)} %copy-done.12), channel_id=1, source_target_pairs={{0,2},{1,3},{2,0},{3,1},{4,6},{5,7},{6,4},{7,5},{8,10},{9,11},{10,... | collective-permute-start | bytes 786440 | tf_op jit(solution)/shard_map/ppermute | solution.py:693
  230.2 13.9 %collective-permute-start.8 = (bf16[1024,128]{1,0:T(8,128)(2,1)S(1)}, bf16[1024,128]{1,0:T(8,128)(2,1)S(1)}, u32[]{:S(2)}, u32[]{:S(2)}) collective-permute-start(bf16[1024,128]{1,0:T(8,128)(2,1)S(1)} %copy-done.11), channel_id=1, source_target_pairs={{0,3},{1,0},{2,1},{3,2},{4,7},{5,4},{6,5},{7,6},{8,11},{9,8},{10,9... | collective-permute-start | bytes 786440 | tf_op jit(solution)/shard_map/ppermute | solution.py:693
  (5 other events, 5.0 us)
Sparse Core Ops, SparseCore 0:
  9.7 34.0 all-gather.8
  50.6 31.7 all-gather.10
  101.4 31.8 all-gather.12
  135.7 33.4 all-gather.14

commit v6 on v5

--- a/solution.py
+++ b/solution.py
@@ -636,7 +636,7 @@
     groups, heads = weight.shape[0], len(parts)
     rows, width = feat.shape
     columns = cot.shape[1]
-    step = 256
+    step = 512
     narrow = pl.BlockSpec((step, columns), lambda i, w: (i, 0))
     return pl.pallas_call(
         lambda *refs: mesh_kernel(heads, *refs),

time: 255 us -> 253 us (level)
  Pallas kernels: 102 us -> 98.4 us
  transfers between devices with their start and end apart: 20 -> 20, of which waited for: 10 -> 11; matrix products, arithmetic and copies ran while one was open for 2% -> 2% of each run, Pallas kernels for 36% -> 35%
where the time goes in v6:
time: 253 us; the launch traced here: 252 us
  Pallas kernels  98.4 us (39%)
  starting transfers between devices  65.9 us (26%)
  waiting for transfers between devices  63.5 us (25%)
  between operations  14.1 us (6%)
  local copies, waits for them, and re-layouts  9.35 us (4%)
    all_to_all x7, starting transfers between devices, over_graph(): lax.all_to_all(values, 'graph', split_axis=0, concat_axis=0, tiled=True)  52.9 us
    all_to_all x7, waiting for transfers between devices, over_graph(): lax.all_to_all(values, 'graph', split_axis=0, concat_axis=0, tiled=True)  37.6 us
    pallas_call x2, Pallas kernels, attention(): pl.pallas_call(lambda *refs: attention_kernel(head, *refs), grid=(blocks,...  35.4 us
    ppermute x9, waiting for transfers between devices, over_feat(): lax.ppermute(parts[s], 'feat', [(i, (i + s) % groups) for i in range(grou...  25.1 us
    pallas_call x2, Pallas kernels, scatter_rows(): pl.pallas_call(lambda *refs: scatter_kernel(len(earlier), *refs), in_spec...  15.6 us
    ppermute x9, starting transfers between devices, over_feat(): lax.ppermute(parts[s], 'feat', [(i, (i + s) % groups) for i in range(grou...  12.7 us
    pallas_call x1, Pallas kernels, mesh_rows(): pl.pallas_call(lambda *refs: mesh_kernel(heads, *refs), grid_spec=pltpu.P...  9.83 us
    pallas_call x1, Pallas kernels, gather_rows(): pl.pallas_call(gather_kernel, in_specs=[SMEM, VMEM, ANY], out_specs=[ANY]...  8.92 us
  transfers between devices with their start and end apart: 20, of which 11 were waited for; matrix products, arithmetic and copies ran while one was open for 2% of the time, Pallas kernels for 35%

profile of v6, /device:TPU:1, one launch (start us, length us, event | category | flops | bytes accessed | tf_op | source)
XLA Modules:
  0.0 252.3 jit_solution(17108706844875566398)
XLA Ops:
  9.6 9.6 %all-to-all-start = ((s32[32,2,128]{2,1,0:T(2,128)}), s32[32,2,128]{2,1,0:T(2,128)S(1)}, u32[]{:S(2)}, u32[]{:S(2)}) async-start(s32[32,2,128]{2,1,0:T(2,128)} %broadcast_in_dim.4), calls=%async_computation | async-start | bytes 65536 | tf_op jit(solution)/shard_map/all_to_all | solution.py:687
  19.2 6.6 %source_terms.1.refs_1_ = bf16[4096,256]{1,0:T(8,128)(2,1)} custom-call(bf16[4096,512]{1,0:T(8,128)(2,1)} %refs_2_.2, f32[1,512]{1,0:T(1,128)} %bitcast.39, bf16[512,128]{1,0:T(8,128)(2,1)} %key_ref.1, bf16[512,128]{1,0:T(8,128)(2,1)} %value_ref.1), custom_call_target="tpu_custom_call" | custom-call | flops 9200000000 | bytes 1048576 | tf_op jit(solution)/shard_map/source_terms/pallas_call | solution.py:94
  27.8 8.9 %gather_rows.1 = (bf16[32,256,128]{2,1,0:T(8,128)(2,1)}, bf16[32,256,128]{2,1,0:T(8,128)(2,1)}) custom-call(s32[64]{0:T(128)} %reshape_squeeze.3.need_ref.refs_1_, s32[32,256]{1,0:T(8,128)} %bitcast.34, bf16[2,2048,256]{2,1,0:T(8,128)(2,1)} %bitcast.42), custom_call_target="tpu_custom_call" | custom-call | flops 11500000256 | bytes 1048576 | tf_op jit(solution)/shard_map/gather_rows/pallas_call | solution.py:187
  36.8 9.5 %all-to-all-start.1 = ((bf16[32,256,128]{2,1,0:T(8,128)(2,1)}), bf16[32,256,128]{2,1,0:T(8,128)(2,1)S(1)}, u32[]{:S(2)}, u32[]{:S(2)}) async-start(bf16[32,256,128]{2,1,0:T(8,128)(2,1)} %get-tuple-element.67), calls=%async_computation.1 | async-start | bytes 4194304 | tf_op jit(solution)/shard_map/all_to_all | solution.py:687
  47.6 7.7 %normed_rows.1.refs_5_ = bf16[4096,512]{1,0:T(8,128)(2,1)} custom-call(bf16[4096,512]{1,0:T(8,128)(2,1)} %refs_2_.2, f32[1,512]{1,0:T(1,128)} %bitcast.40), custom_call_target="tpu_custom_call" | custom-call | flops 9200000000 | bytes 1048576 | tf_op jit(solution)/shard_map/normed_rows/pallas_call | solution.py:214
  55.3 6.0 %target_terms.1 = (bf16[2048,512]{1,0:T(8,128)(2,1)}, bf16[2048,128]{1,0:T(8,128)(2,1)}, bf16[2048,128]{1,0:T(8,128)(2,1)}) custom-call(bf16[2048,512]{1,0:T(8,128)(2,1)} %refs_2_.3, f32[1,512]{1,0:T(1,128)} %bitcast.37, bf16[512,128]{1,0:T(8,128)(2,1)} %wq_ref.1, bf16[128,512]{1,0:T(8,128)(2,1)} %wo_ref.1, bf16[4,2048,128]{2,1,0:T(8,128)(2,1)} %bitcast.30), custom_call_target="tpu_custom_call" | custom-call | flops 6899999744 | bytes 1048576 | tf_op jit(solution)/shard_map/target_terms/pallas_call | solution.py:246
  61.2 12.9 %all-to-all-done.1.refs_2_ = bf16[32,256,128]{2,1,0:T(8,128)(2,1)S(1)} async-done(((bf16[32,256,128]{2,1,0:T(8,128)(2,1)}), bf16[32,256,128]{2,1,0:T(8,128)(2,1)S(1)}, u32[]{:S(2)}, u32[]{:S(2)}) %all-to-all-start.1) | async-done | bytes 2097184 | tf_op jit(solution)/shard_map/all_to_all | solution.py:687
  74.1 1.4 copy-done.2
  75.5 6.7 %all-to-all-start.2 = ((bf16[32,256,128]{2,1,0:T(8,128)(2,1)}), bf16[32,256,128]{2,1,0:T(8,128)(2,1)}, u32[]{:S(2)}, u32[]{:S(2)}) async-start(bf16[32,256,128]{2,1,0:T(8,128)(2,1)} %get-tuple-element.72), calls=%async_computation.2 | async-start | bytes 4194304 | tf_op jit(solution)/shard_map/all_to_all | solution.py:687
  82.3 17.7 %attention.2 = (bf16[4096,128]{1,0:T(8,128)(2,1)}, bf16[32,256,128]{2,1,0:T(8,128)(2,1)}, f32[4,128,128]{2,1,0:T(8,128)}, bf16[2048,128]{1,0:T(8,128)(2,1)}) custom-call(s32[4,8]{1,0:T(4,128)} %refs_0_.3, bf16[4096,256]{1,0:T(8,128)(2,1)} %source_terms.1.refs_1_, bf16[32,256,128]{2,1,0:T(8,128)(2,1)} %copy-done.2, ...), custom_call_target="tpu_custom_call" | custom-call | flops 20700000256 | bytes 1048576 | tf_op jit(solution)/shard_map/attention/pallas_call | solution.py:409
  100.0 10.2 %all-to-all-done.2.refs_2_ = bf16[32,256,128]{2,1,0:T(8,128)(2,1)} async-done(((bf16[32,256,128]{2,1,0:T(8,128)(2,1)}), bf16[32,256,128]{2,1,0:T(8,128)(2,1)}, u32[]{:S(2)}, u32[]{:S(2)}) %all-to-all-start.2) | async-done | bytes 2097184 | tf_op jit(solution)/shard_map/all_to_all | solution.py:687
  110.2 6.1 %all-to-all-start.4 = ((bf16[32,256,128]{2,1,0:T(8,128)(2,1)}), bf16[32,256,128]{2,1,0:T(8,128)(2,1)S(1)}, u32[]{:S(2)}, u32[]{:S(2)}) async-start(bf16[32,256,128]{2,1,0:T(8,128)(2,1)} %get-tuple-element.79), calls=%async_computation.4 | async-start | bytes 4194304 | tf_op jit(solution)/shard_map/all_to_all | solution.py:687
  116.5 17.8 %attention.3 = (bf16[4096,128]{1,0:T(8,128)(2,1)}, bf16[32,256,128]{2,1,0:T(8,128)(2,1)}, f32[4,128,128]{2,1,0:T(8,128)}, bf16[2048,128]{1,0:T(8,128)(2,1)}) custom-call(s32[4,8]{1,0:T(4,128)} %refs_0_.3, bf16[4096,256]{1,0:T(8,128)(2,1)} %source_terms.1.refs_1_, bf16[32,256,128]{2,1,0:T(8,128)(2,1)} %all-to-all-done.2.refs_2_, ...), custom_call_target="tpu_custom_call" | custom-call | flops 20700000256 | bytes 1048576 | tf_op jit(solution)/shard_map/attention/pallas_call | solution.py:409
  134.3 9.9 %all-to-all-done.4.refs_3_ = bf16[32,256,128]{2,1,0:T(8,128)(2,1)S(1)} async-done(((bf16[32,256,128]{2,1,0:T(8,128)(2,1)}), bf16[32,256,128]{2,1,0:T(8,128)(2,1)S(1)}, u32[]{:S(2)}, u32[]{:S(2)}) %all-to-all-start.4) | async-done | bytes 2097184 | tf_op jit(solution)/shard_map/all_to_all | solution.py:687
  144.2 1.3 copy-done.3
  145.5 6.0 %all-to-all-start.3 = ((bf16[32,256,128]{2,1,0:T(8,128)(2,1)}), bf16[32,256,128]{2,1,0:T(8,128)(2,1)S(1)}, u32[]{:S(2)}, u32[]{:S(2)}) async-start(bf16[32,256,128]{2,1,0:T(8,128)(2,1)} %get-tuple-element.77), calls=%async_computation.3 | async-start | bytes 4194304 | tf_op jit(solution)/shard_map/all_to_all | solution.py:687
  151.6 7.6 %scatter_rows.2 = (f32[4,128,128]{2,1,0:T(8,128)}, bf16[1024,128]{1,0:T(8,128)(2,1)}, bf16[1024,128]{1,0:T(8,128)(2,1)}, bf16[1024,128]{1,0:T(8,128)(2,1)}, bf16[1024,128]{1,0:T(8,128)(2,1)}) custom-call(s32[1]{0:T(128)} %bitcast.16.refs_0_, s32[64]{0:T(128)} %reshape_squeeze.3.need_ref.refs_1_, bf16[4096,128]{1,0:T(8,128)(2,1)} %get-tuple-element.78.refs_2_, ...), custom_call_target="tpu_custom_call" | custom-call | flops 12650000384 | bytes 1048576 | tf_op jit(solution)/shard_map/scatter_rows/pallas_call | solution.py:515
  159.2 1.3 collective-permute-start
  160.5 2.5 collective-permute-start.1
  164.1 7.2 %collective-permute-done.refs_6_ = bf16[1024,128]{1,0:T(8,128)(2,1)S(1)} collective-permute-done((bf16[1024,128]{1,0:T(8,128)(2,1)}, bf16[1024,128]{1,0:T(8,128)(2,1)S(1)}, u32[]{:S(2)}, u32[]{:S(2)}) %collective-permute-start) | collective-permute-done | bytes 262176 | tf_op jit(solution)/shard_map/ppermute | solution.py:693
  171.3 5.9 %collective-permute-done.1.refs_8_ = bf16[1024,128]{1,0:T(8,128)(2,1)S(1)} collective-permute-done((bf16[1024,128]{1,0:T(8,128)(2,1)}, bf16[1024,128]{1,0:T(8,128)(2,1)S(1)}, u32[]{:S(2)}, u32[]{:S(2)}) %collective-permute-start.1) | collective-permute-done | bytes 262176 | tf_op jit(solution)/shard_map/ppermute | solution.py:693
  177.2 2.3 all-to-all-done.3.refs_3_
  179.5 1.4 copy-done.1
  181.0 8.0 %scatter_rows.3 = (f32[32,64,128]{2,1,0:T(8,128)}, bf16[1024,128]{1,0:T(8,128)(2,1)}, bf16[1024,128]{1,0:T(8,128)(2,1)}, bf16[1024,128]{1,0:T(8,128)(2,1)}, bf16[1024,128]{1,0:T(8,128)(2,1)}) custom-call(s32[1]{0:T(128)} %bitcast.16.refs_0_, s32[64]{0:T(128)} %reshape_squeeze.3.need_ref.refs_1_, bf16[4096,128]{1,0:T(8,128)(2,1)} %get-tuple-element.92.refs_2_, ...), custom_call_target="tpu_custom_call" | custom-call | flops 12650000384 | bytes 1048576 | tf_op jit(solution)/shard_map/scatter_rows/pallas_call | solution.py:515
  190.3 2.4 collective-permute-start.4
  193.9 8.0 %all-to-all-start.5 = ((f32[32,64,128]{2,1,0:T(8,128)}), f32[32,64,128]{2,1,0:T(8,128)S(1)}, u32[]{:S(2)}, u32[]{:S(2)}) async-start(f32[32,64,128]{2,1,0:T(8,128)} %get-tuple-element.98), calls=%async_computation.5 | async-start | bytes 2097152 | tf_op jit(solution)/shard_map/all_to_all | solution.py:687
  201.9 9.8 %mesh_rows.1 = (bf16[2048,128]{1,0:T(8,128)(2,1)}, bf16[2048,128]{1,0:T(8,128)(2,1)}) custom-call(s32[1]{0:T(128)} %bitcast.16.refs_0_, bf16[4,2,2,128,512]{4,3,2,1,0:T(8,128)(2,1)} %bitcast.27, bf16[2048,512]{1,0:T(8,128)(2,1)} %refs_2_.3, bf16[2048,128]{1,0:T(8,128)(2,1)} %refs_3_.1, f32[1,512]{1,0:T(1,128)} %bitcast.38, bf16[4,2048,128]{2,1,0:T(8,128)(2,1)} %bitcast.29, ...), custom_call_target="tpu_custom_call" | custom-call | flops 12650000384 | bytes 1048576 | tf_op jit(solution)/shard_map/mesh_rows/pallas_call | solution.py:641
  212.6 5.9 %grid_rows.1 = (bf16[1024,128]{1,0:T(8,128)(2,1)}, bf16[1024,128]{1,0:T(8,128)(2,1)}, bf16[1024,128]{1,0:T(8,128)(2,1)}, bf16[1024,128]{1,0:T(8,128)(2,1)}) custom-call(s32[1]{0:T(128)} %bitcast.16.refs_0_, bf16[4,2,2,128,512]{4,3,2,1,0:T(8,128)(2,1)} %bitcast.28, bf16[4096,512]{1,0:T(8,128)(2,1)} %refs_2_.2, f32[1,512]{1,0:T(1,128)} %bitcast.41, ...), custom_call_target="tpu_custom_call" | custom-call | flops 6899999744 | bytes 1048576 | tf_op jit(solution)/shard_map/grid_rows/pallas_call | solution.py:593
  220.3 6.9 %all-to-all-start.6 = ((f32[32,64,128]{2,1,0:T(8,128)}), f32[32,64,128]{2,1,0:T(8,128)S(1)}, u32[]{:S(2)}, u32[]{:S(2)}) async-start(f32[32,64,128]{2,1,0:T(8,128)} %broadcast_in_dim.5), calls=%async_computation.6 | async-start | bytes 2097152 | tf_op jit(solution)/shard_map/all_to_all | solution.py:687
  228.3 1.9 collective-permute-start.8
  230.1 11.7 %collective-permute-done.6.refs_2_ = bf16[1024,128]{1,0:T(8,128)(2,1)S(1)} collective-permute-done((bf16[1024,128]{1,0:T(8,128)(2,1)S(1)}, bf16[1024,128]{1,0:T(8,128)(2,1)S(1)}, u32[]{:S(2)}, u32[]{:S(2)}) %collective-permute-start.6) | collective-permute-done | bytes 262176 | tf_op jit(solution)/shard_map/ppermute | solution.py:693
  244.4 1.4 finish.1
  (73 shorter events, 15.7 us)
Async XLA Ops:
  7.2 48.1 %all-gather.9.cloned.1.call-start = ((), (), s32[]{:S(2)}) async-start(), calls=%async_computation.7 | async-start | bytes 2621440 | tf_op jit(solution)/shard_map/all_gather | solution.py:742
  9.6 16.9 %all-to-all-start = ((s32[32,2,128]{2,1,0:T(2,128)}), s32[32,2,128]{2,1,0:T(2,128)S(1)}, u32[]{:S(2)}, u32[]{:S(2)}) async-start(s32[32,2,128]{2,1,0:T(2,128)} %broadcast_in_dim.4), calls=%async_computation | async-start | bytes 65536 | tf_op jit(solution)/shard_map/all_to_all | solution.py:687
  36.7 9.6 %copy-start.4 = (bf16[512,128]{1,0:T(8,128)(2,1)S(1)}, bf16[512,128]{1,0:T(8,128)(2,1)}, u32[]{:S(2)}) copy-start(bf16[512,128]{1,0:T(8,128)(2,1)} %key_ref.1) | copy-start | bytes 393220
  36.7 9.7 %copy-start.5 = (bf16[512,128]{1,0:T(8,128)(2,1)S(1)}, bf16[512,128]{1,0:T(8,128)(2,1)}, u32[]{:S(2)}) copy-start(bf16[512,128]{1,0:T(8,128)(2,1)} %value_ref.1) | copy-start | bytes 393220
  36.7 9.9 %copy-start.6 = (bf16[512,128]{1,0:T(8,128)(2,1)S(1)}, bf16[512,128]{1,0:T(8,128)(2,1)}, u32[]{:S(2)}) copy-start(bf16[512,128]{1,0:T(8,128)(2,1)} %wq_ref.1) | copy-start | bytes 393220
  36.7 10.0 %copy-start.7 = (bf16[128,512]{1,0:T(8,128)(2,1)S(1)}, bf16[128,512]{1,0:T(8,128)(2,1)}, u32[]{:S(2)}) copy-start(bf16[128,512]{1,0:T(8,128)(2,1)} %wo_ref.1) | copy-start | bytes 393220
  36.8 37.4 %all-to-all-start.1 = ((bf16[32,256,128]{2,1,0:T(8,128)(2,1)}), bf16[32,256,128]{2,1,0:T(8,128)(2,1)S(1)}, u32[]{:S(2)}, u32[]{:S(2)}) async-start(bf16[32,256,128]{2,1,0:T(8,128)(2,1)} %get-tuple-element.67), calls=%async_computation.1 | async-start | bytes 4194304 | tf_op jit(solution)/shard_map/all_to_all | solution.py:687
  46.3 63.9 %all-gather.11.cloned.1.call-start = ((), (), s32[]{:S(2)}) async-start(), calls=%async_computation.8 | async-start | bytes 2621440 | tf_op jit(solution)/shard_map/all_gather | solution.py:744
  75.5 34.7 %all-to-all-start.2 = ((bf16[32,256,128]{2,1,0:T(8,128)(2,1)}), bf16[32,256,128]{2,1,0:T(8,128)(2,1)}, u32[]{:S(2)}, u32[]{:S(2)}) async-start(bf16[32,256,128]{2,1,0:T(8,128)(2,1)} %get-tuple-element.72), calls=%async_computation.2 | async-start | bytes 4194304 | tf_op jit(solution)/shard_map/all_to_all | solution.py:687
  82.2 52.1 %all-gather.13.cloned.1.call-start = ((), (), s32[]{:S(2)}) async-start(), calls=%async_computation.9 | async-start | bytes 2621440 | tf_op jit(solution)/shard_map/all_gather | solution.py:765
  110.2 34.0 %all-to-all-start.4 = ((bf16[32,256,128]{2,1,0:T(8,128)(2,1)}), bf16[32,256,128]{2,1,0:T(8,128)(2,1)S(1)}, u32[]{:S(2)}, u32[]{:S(2)}) async-start(bf16[32,256,128]{2,1,0:T(8,128)(2,1)} %get-tuple-element.79), calls=%async_computation.4 | async-start | bytes 4194304 | tf_op jit(solution)/shard_map/all_to_all | solution.py:687
  116.3 61.0 %all-gather.15.cloned.1.call-start = ((), (), s32[]{:S(2)}) async-start(), calls=%async_computation.10 | async-start | bytes 2621440 | tf_op jit(solution)/shard_map/all_gather | solution.py:765
  145.5 34.0 %all-to-all-start.3 = ((bf16[32,256,128]{2,1,0:T(8,128)(2,1)}), bf16[32,256,128]{2,1,0:T(8,128)(2,1)S(1)}, u32[]{:S(2)}, u32[]{:S(2)}) async-start(bf16[32,256,128]{2,1,0:T(8,128)(2,1)} %get-tuple-element.77), calls=%async_computation.3 | async-start | bytes 4194304 | tf_op jit(solution)/shard_map/all_to_all | solution.py:687
  159.2 12.1 %collective-permute-start = (bf16[1024,128]{1,0:T(8,128)(2,1)}, bf16[1024,128]{1,0:T(8,128)(2,1)S(1)}, u32[]{:S(2)}, u32[]{:S(2)}) collective-permute-start(bf16[1024,128]{1,0:T(8,128)(2,1)} %get-tuple-element.82), channel_id=1, source_target_pairs={{0,1},{1,2},{2,3},{3,0},{4,5},{5,6},{6,7},{7,4},{8,9},{9,10},{10,1... | collective-permute-start | bytes 786440 | tf_op jit(solution)/shard_map/ppermute | solution.py:693
  160.5 16.7 %collective-permute-start.1 = (bf16[1024,128]{1,0:T(8,128)(2,1)}, bf16[1024,128]{1,0:T(8,128)(2,1)S(1)}, u32[]{:S(2)}, u32[]{:S(2)}) collective-permute-start(bf16[1024,128]{1,0:T(8,128)(2,1)} %get-tuple-element.83), channel_id=1, source_target_pairs={{0,2},{1,3},{2,0},{3,1},{4,6},{5,7},{6,4},{7,5},{8,10},{9,11},{10,... | collective-permute-start | bytes 786440 | tf_op jit(solution)/shard_map/ppermute | solution.py:693
  162.9 14.3 %collective-permute-start.2 = (bf16[1024,128]{1,0:T(8,128)(2,1)}, bf16[1024,128]{1,0:T(8,128)(2,1)S(1)}, u32[]{:S(2)}, u32[]{:S(2)}) collective-permute-start(bf16[1024,128]{1,0:T(8,128)(2,1)} %get-tuple-element.84), channel_id=1, source_target_pairs={{0,3},{1,0},{2,1},{3,2},{4,7},{5,4},{6,5},{7,6},{8,11},{9,8},{10,9... | collective-permute-start | bytes 786440 | tf_op jit(solution)/shard_map/ppermute | solution.py:693
  171.3 17.7 %copy-start.8 = (bf16[1024,128]{1,0:T(8,128)(2,1)}, bf16[1024,128]{1,0:T(8,128)(2,1)S(1)}, u32[]{:S(2)}) copy-start(bf16[1024,128]{1,0:T(8,128)(2,1)S(1)} %collective-permute-done.refs_6_) | copy-start | bytes 786436
  177.2 11.8 %copy-start.9 = (bf16[1024,128]{1,0:T(8,128)(2,1)}, bf16[1024,128]{1,0:T(8,128)(2,1)S(1)}, u32[]{:S(2)}) copy-start(bf16[1024,128]{1,0:T(8,128)(2,1)S(1)} %collective-permute-done.1.refs_8_) | copy-start | bytes 786436
  177.2 11.8 %copy-start.10 = (bf16[1024,128]{1,0:T(8,128)(2,1)}, bf16[1024,128]{1,0:T(8,128)(2,1)S(1)}, u32[]{:S(2)}) copy-start(bf16[1024,128]{1,0:T(8,128)(2,1)S(1)} %collective-permute-done.2.refs_10_) | copy-start | bytes 786436
  179.5 1.4 copy-start.1
  189.0 22.7 %collective-permute-start.3 = (bf16[1024,128]{1,0:T(8,128)(2,1)}, bf16[1024,128]{1,0:T(8,128)(2,1)S(1)}, u32[]{:S(2)}, u32[]{:S(2)}) collective-permute-start(bf16[1024,128]{1,0:T(8,128)(2,1)} %get-tuple-element.103), channel_id=1, source_target_pairs={{0,1},{1,2},{2,3},{3,0},{4,5},{5,6},{6,7},{7,4},{8,9},{9,10},{10,1... | collective-permute-start | bytes 786440 | tf_op jit(solution)/shard_map/ppermute | solution.py:693
  190.3 21.4 %collective-permute-start.4 = (bf16[1024,128]{1,0:T(8,128)(2,1)}, bf16[1024,128]{1,0:T(8,128)(2,1)S(1)}, u32[]{:S(2)}, u32[]{:S(2)}) collective-permute-start(bf16[1024,128]{1,0:T(8,128)(2,1)} %get-tuple-element.105), channel_id=1, source_target_pairs={{0,2},{1,3},{2,0},{3,1},{4,6},{5,7},{6,4},{7,5},{8,10},{9,11},{10,... | collective-permute-start | bytes 786440 | tf_op jit(solution)/shard_map/ppermute | solution.py:693
  192.8 19.0 %collective-permute-start.5 = (bf16[1024,128]{1,0:T(8,128)(2,1)}, bf16[1024,128]{1,0:T(8,128)(2,1)S(1)}, u32[]{:S(2)}, u32[]{:S(2)}) collective-permute-start(bf16[1024,128]{1,0:T(8,128)(2,1)} %get-tuple-element.107), channel_id=1, source_target_pairs={{0,3},{1,0},{2,1},{3,2},{4,7},{5,4},{6,5},{7,6},{8,11},{9,8},{10,9... | collective-permute-start | bytes 786440 | tf_op jit(solution)/shard_map/ppermute | solution.py:693
  193.9 25.2 %all-to-all-start.5 = ((f32[32,64,128]{2,1,0:T(8,128)}), f32[32,64,128]{2,1,0:T(8,128)S(1)}, u32[]{:S(2)}, u32[]{:S(2)}) async-start(f32[32,64,128]{2,1,0:T(8,128)} %get-tuple-element.98), calls=%async_computation.5 | async-start | bytes 2097152 | tf_op jit(solution)/shard_map/all_to_all | solution.py:687
  218.6 8.6 %copy-start.14 = (bf16[1024,128]{1,0:T(8,128)(2,1)S(1)}, bf16[1024,128]{1,0:T(8,128)(2,1)}, u32[]{:S(2)}) copy-start(bf16[1024,128]{1,0:T(8,128)(2,1)} %get-tuple-element.118) | copy-start | bytes 786436
  218.6 9.0 %copy-start.12 = (bf16[1024,128]{1,0:T(8,128)(2,1)S(1)}, bf16[1024,128]{1,0:T(8,128)(2,1)}, u32[]{:S(2)}) copy-start(bf16[1024,128]{1,0:T(8,128)(2,1)} %get-tuple-element.119) | copy-start | bytes 786436
  218.6 9.7 %copy-start.11 = (bf16[1024,128]{1,0:T(8,128)(2,1)S(1)}, bf16[1024,128]{1,0:T(8,128)(2,1)}, u32[]{:S(2)}) copy-start(bf16[1024,128]{1,0:T(8,128)(2,1)} %get-tuple-element.120) | copy-start | bytes 786436
  218.6 23.5 %copy-start = (bf16[1024,128]{1,0:T(8,128)(2,1)S(1)}, bf16[1024,128]{1,0:T(8,128)(2,1)}, u32[]{:S(2)}) copy-start(bf16[1024,128]{1,0:T(8,128)(2,1)} %get-tuple-element.117.refs_1_) | copy-start | bytes 786436
  220.3 24.1 %all-to-all-start.6 = ((f32[32,64,128]{2,1,0:T(8,128)}), f32[32,64,128]{2,1,0:T(8,128)S(1)}, u32[]{:S(2)}, u32[]{:S(2)}) async-start(f32[32,64,128]{2,1,0:T(8,128)} %broadcast_in_dim.5), calls=%async_computation.6 | async-start | bytes 2097152 | tf_op jit(solution)/shard_map/all_to_all | solution.py:687
  227.2 14.6 %collective-permute-start.6 = (bf16[1024,128]{1,0:T(8,128)(2,1)S(1)}, bf16[1024,128]{1,0:T(8,128)(2,1)S(1)}, u32[]{:S(2)}, u32[]{:S(2)}) collective-permute-start(bf16[1024,128]{1,0:T(8,128)(2,1)S(1)} %copy-done.14), channel_id=1, source_target_pairs={{0,1},{1,2},{2,3},{3,0},{4,5},{5,6},{6,7},{7,4},{8,9},{9,10},{10,1... | collective-permute-start | bytes 786440 | tf_op jit(solution)/shard_map/ppermute | solution.py:693
  227.6 14.2 %collective-permute-start.7 = (bf16[1024,128]{1,0:T(8,128)(2,1)S(1)}, bf16[1024,128]{1,0:T(8,128)(2,1)S(1)}, u32[]{:S(2)}, u32[]{:S(2)}) collective-permute-start(bf16[1024,128]{1,0:T(8,128)(2,1)S(1)} %copy-done.12), channel_id=1, source_target_pairs={{0,2},{1,3},{2,0},{3,1},{4,6},{5,7},{6,4},{7,5},{8,10},{9,11},{10,... | collective-permute-start | bytes 786440 | tf_op jit(solution)/shard_map/ppermute | solution.py:693
  228.3 13.9 %collective-permute-start.8 = (bf16[1024,128]{1,0:T(8,128)(2,1)S(1)}, bf16[1024,128]{1,0:T(8,128)(2,1)S(1)}, u32[]{:S(2)}, u32[]{:S(2)}) collective-permute-start(bf16[1024,128]{1,0:T(8,128)(2,1)S(1)} %copy-done.11), channel_id=1, source_target_pairs={{0,3},{1,0},{2,1},{3,2},{4,7},{5,4},{6,5},{7,6},{8,11},{9,8},{10,9... | collective-permute-start | bytes 786440 | tf_op jit(solution)/shard_map/ppermute | solution.py:693
  (5 other events, 5.0 us)
Sparse Core Ops, SparseCore 0:
  9.7 34.0 all-gather.8
  49.3 31.7 all-gather.10
  100.1 31.9 all-gather.12
  134.4 33.9 all-gather.14
